TPU v7x, 32 devices: a whole 2x2x4 slice. The times are simulated.
32 devices in a mesh: groups: 2 (over y), dev: 8 (over z, x), sub: 2 (over core).
Axes of the slice: x: 2, y: 2, z: 4, core: 2. Of those that a mesh axis runs over, the one named last changes fastest.
Arguments:
- hidden: bfloat16 [2, 512, 3584], P(None, ('groups', 'dev')), parts along dimension 1, may hold values from -6 to 6
- norm_gain: float32 [3584], replicated, may hold values from 0.1 to 1.9
- routes: int32 [2, 512, 2], P(None, ('groups', 'dev')), parts along dimension 1, may hold values from 0 to 3, all different within a row; in each aligned block of 32 rows (0 to 31, 32 to 63, ..., all dimensions but the last counted through in order) at most 32 rows name the same one
- route_weight: float32 [2, 512, 2], P(None, ('groups', 'dev')), parts along dimension 1, may hold values from 0.1 to 1
- w_in: bfloat16 [3584, 4096], P(None, ('dev', 'sub')), may hold values from -0.09375 to 0.09375
- w_out: bfloat16 [4096, 3584], P(('dev', 'sub')), may hold values from -0.1875 to 0.1875
Outputs:
- layer_out: bfloat16 [2, 512, 3584], P(None, ('groups', 'dev'), 'sub'), parts along dimension 1
There are 2 independent parts, one for each index of `groups`. A program takes and returns all parts, laid end to end along the dimension named above; an argument that names none is the same for every part. Nothing has to cross between parts.
Inputs may be any that keep to these rules, and one draw needn't show every extreme that they name: `routes`: each row names 2 different experts; in each micro-batch the 32 rows of one index of dev name one expert at most 32 times.
All inputs are finite; a program needn't handle non-finite values.
Results may differ from a plain program's by a relative error of at most 0.008.
Values may be sent and summed in bfloat16 or wider, within the bound.
No kernel may reach another device: no remote copies, remote signals or barrier semaphores. Data moves between devices by JAX's collectives and lax.ppermute only.
A program may use at most 64 MiB of HBM per device.

v0:
```python
import jax
import jax.numpy as jnp
from jax import lax
from jax.sharding import PartitionSpec as P

EPS = 1e-06


def route_tables(routes_now, weight_now, n_dev, cap, span):
    rows, top = routes_now.shape
    flat = routes_now.reshape(-1)
    order = jnp.arange(flat.shape[0], dtype=jnp.int32)
    earlier = (flat[None, :] == flat[:, None]) & (order[None, :] < order[:, None])
    rank = jnp.sum(earlier.astype(jnp.int32), axis=1)
    target = jnp.arange(n_dev * cap, dtype=jnp.int32)
    target_group = target // (cap * span)
    target_place = target % cap
    landing = (flat[None, :] == target_group[:, None]) & (rank[None, :] == target_place[:, None])
    landing = landing.reshape(n_dev * cap, rows, top)
    select = jnp.any(landing, axis=2).astype(jnp.bfloat16)
    weigh = jnp.sum(jnp.where(landing, weight_now[None, :, :], jnp.float32(0.0)), axis=2)
    return (select, weigh)


def local(hidden, norm_gain, routes, route_weight, w_in, w_out):
    batches, rows, width = hidden.shape
    n_dev = lax.axis_size("dev")
    n_sub = lax.axis_size("sub")
    experts = n_dev // 2
    top = routes.shape[2]
    cap = max(2, 2 * rows * top // experts)
    span = n_dev // experts
    hid = hidden.astype(jnp.float32)
    normed = (
        hid * lax.rsqrt(jnp.mean(hid * hid, axis=-1, keepdims=True) + EPS) * norm_gain
    ).astype(jnp.bfloat16)
    part_width = width // n_sub
    offset = lax.axis_index("sub") * part_width
    tables = [
        route_tables(routes[step], route_weight[step], n_dev, cap, span) for step in range(batches)
    ]
    buffers = [
        jnp.dot(tables[step][0], normed[step], preferred_element_type=jnp.float32)
        .astype(jnp.bfloat16)
        .reshape(n_dev, cap, -1)
        for step in range(batches)
    ]

    def run_expert(arrived):
        senders, count, features = arrived.shape
        inner = jnp.dot(
            arrived.reshape(senders * count, features), w_in, preferred_element_type=jnp.float32
        )
        act = jax.nn.silu(inner).astype(jnp.bfloat16)
        pieces = jnp.dot(act, w_out, preferred_element_type=jnp.float32).astype(jnp.bfloat16)
        return lax.all_to_all(
            pieces.reshape(senders, count, -1), "dev", split_axis=0, concat_axis=0, tiled=True
        )

    def dispatch(buffer):
        returned = run_expert(
            lax.all_to_all(buffer, "dev", split_axis=0, concat_axis=0, tiled=True)
        )
        return returned

    returned = [dispatch(buffer) for buffer in buffers]
    terms = []
    for step in range(batches):
        flat_back = returned[step].reshape(n_dev * cap, width).astype(jnp.float32)
        terms.append(
            jnp.dot(
                tables[step][1].T,
                flat_back,
                precision=lax.Precision.HIGHEST,
                preferred_element_type=jnp.float32,
            )
        )
    summed = lax.psum_scatter(
        jnp.stack(terms).astype(jnp.bfloat16), "sub", scatter_dimension=2, tiled=True
    ).astype(jnp.float32)
    own = lax.dynamic_slice_in_dim(hid, offset, part_width, 2)
    layer_out = (own + summed).astype(jnp.bfloat16)
    return layer_out


def solution(mesh):
    placed = (
        P(None, ("groups", "dev"), None),
        P(),
        P(None, ("groups", "dev"), None),
        P(None, ("groups", "dev"), None),
        P(None, ("dev", "sub")),
        P(("dev", "sub"), None),
    )
    return jax.shard_map(
        local,
        mesh=mesh,
        in_specs=placed,
        out_specs=P(None, ("groups", "dev"), "sub"),
        check_vma=False,
    )
```

profile of v0, /device:TPU:0, one launch (start us, length us, event | category | flops | bytes accessed | tf_op | source)
XLA Modules:
  0.0 221.7 jit_solution(17632762259572789889)
XLA Ops:
  6.5 0.8 slice_bitcast_fusion.6
  7.4 0.1 copy.19
  7.5 0.1 eq.101
  7.6 0.2 convert_reduce_fusion.1
  7.7 0.1 eq.105
  7.9 0.1 copy.20
  7.9 0.1 copy.21
  8.0 0.1 eq.112
  8.1 0.2 convert_reduce_fusion
  8.3 0.1 eq.116
  8.4 0.1 copy.22
  8.5 1.2 multiply_reduce_fusion
  9.7 1.2 multiply_convert_fusion
  11.0 0.1 fusion.4
  11.1 1.9 convolution_convert_fusion.3
  13.0 7.3 %all-to-all-start = ((bf16[8,32,3584]{2,1,0:T(8,128)(2,1)}), bf16[8,32,3584]{2,1,0:T(8,128)(2,1)}, u32[]{:S(2)}, u32[]{:S(2)}) async-start(bf16[8,32,3584]{2,1,0:T(8,128)(2,1)} %bitcast.41), calls=%async_computation | async-start | bytes 3670016 | tf_op jit(solution)/shard_map/all_to_all | solution.py:62
  20.3 2.0 convolution_convert_fusion.1
  22.2 40.8 %all-to-all-done = bf16[8,32,3584]{2,1,0:T(8,128)(2,1)} async-done(((bf16[8,32,3584]{2,1,0:T(8,128)(2,1)}), bf16[8,32,3584]{2,1,0:T(8,128)(2,1)}, u32[]{:S(2)}, u32[]{:S(2)}) %all-to-all-start) | async-done | bytes 1835040 | tf_op jit(solution)/shard_map/all_to_all | solution.py:62
  63.0 4.3 %all-to-all-start.2 = ((bf16[8,32,3584]{2,1,0:T(8,128)(2,1)}), bf16[8,32,3584]{2,1,0:T(8,128)(2,1)}, u32[]{:S(2)}, u32[]{:S(2)}) async-start(bf16[8,32,3584]{2,1,0:T(8,128)(2,1)} %bitcast.40), calls=%async_computation.2 | async-start | bytes 3670016 | tf_op jit(solution)/shard_map/all_to_all | solution.py:62
  67.3 5.4 %convolution_convert_fusion.2 = bf16[256,3584]{1,0:T(8,128)(2,1)} fusion(bf16[256,3584]{1,0:T(8,128)(2,1)S(1)} %copy-done, bf16[256,3584]{1,0:T(8,128)(2,1)} %bitcast.4, bf16[3584,256]{1,0:T(8,128)(2,1)} %param.10), kind=kOutput, calls=%fused_computation.2 | convolution fusion | flops 940769280 | bytes 7340032 | tf_op jit(solution)/shard_map/dot_general | solution.py:55
  72.7 36.8 %all-to-all-done.2 = bf16[8,32,3584]{2,1,0:T(8,128)(2,1)} async-done(((bf16[8,32,3584]{2,1,0:T(8,128)(2,1)}), bf16[8,32,3584]{2,1,0:T(8,128)(2,1)}, u32[]{:S(2)}, u32[]{:S(2)}) %all-to-all-start.2) | async-done | bytes 1835040 | tf_op jit(solution)/shard_map/all_to_all | solution.py:62
  109.5 4.3 %all-to-all-start.1 = ((bf16[8,32,3584]{2,1,0:T(8,128)(2,1)}), bf16[8,32,3584]{2,1,0:T(8,128)(2,1)}, u32[]{:S(2)}, u32[]{:S(2)}) async-start(bf16[8,32,3584]{2,1,0:T(8,128)(2,1)} %bitcast.39), calls=%async_computation.1 | async-start | bytes 3670016 | tf_op jit(solution)/shard_map/all_to_all | solution.py:56
  113.9 5.5 %convolution_convert_fusion = bf16[256,3584]{1,0:T(8,128)(2,1)} fusion(bf16[256,3584]{1,0:T(8,128)(2,1)S(1)} %copy-done, bf16[256,3584]{1,0:T(8,128)(2,1)} %bitcast.12, bf16[3584,256]{1,0:T(8,128)(2,1)} %param.10), kind=kOutput, calls=%fused_computation | convolution fusion | flops 940769280 | bytes 7340032 | tf_op jit(solution)/shard_map/dot_general | solution.py:55
  119.3 36.8 %all-to-all-done.1 = bf16[8,32,3584]{2,1,0:T(8,128)(2,1)} async-done(((bf16[8,32,3584]{2,1,0:T(8,128)(2,1)}), bf16[8,32,3584]{2,1,0:T(8,128)(2,1)}, u32[]{:S(2)}, u32[]{:S(2)}) %all-to-all-start.1) | async-done | bytes 1835040 | tf_op jit(solution)/shard_map/all_to_all | solution.py:56
  156.1 4.4 %all-to-all-start.3 = ((bf16[8,32,3584]{2,1,0:T(8,128)(2,1)}), bf16[8,32,3584]{2,1,0:T(8,128)(2,1)}, u32[]{:S(2)}, u32[]{:S(2)}) async-start(bf16[8,32,3584]{2,1,0:T(8,128)(2,1)} %bitcast.38), calls=%async_computation.3 | async-start | bytes 3670016 | tf_op jit(solution)/shard_map/all_to_all | solution.py:56
  160.6 0.1 select_reduce_fusion.1
  160.7 2.5 %fusion = bf16[1,32,3584]{2,1,0:T(8,128)(2,1)S(1)} fusion(f32[256,32]{0,1:T(8,128)S(1)} %get-tuple-element.7, bf16[256,3584]{1,0:T(8,128)(2,1)} %bitcast.6), kind=kOutput, calls=%fused_computation.6 | convolution fusion | flops 352436224 | bytes 2097152 | tf_op jit(solution)/shard_map/dot_general | solution.py:71
  163.2 39.5 %all-to-all-done.3 = bf16[8,32,3584]{2,1,0:T(8,128)(2,1)} async-done(((bf16[8,32,3584]{2,1,0:T(8,128)(2,1)}), bf16[8,32,3584]{2,1,0:T(8,128)(2,1)}, u32[]{:S(2)}, u32[]{:S(2)}) %all-to-all-start.3) | async-done | bytes 1835040 | tf_op jit(solution)/shard_map/all_to_all | solution.py:56
  202.8 2.5 %fusion.1 = bf16[1,32,3584]{2,1,0:T(8,128)(2,1)S(1)} fusion(f32[256,32]{0,1:T(8,128)S(1)} %get-tuple-element.8, bf16[256,3584]{1,0:T(8,128)(2,1)} %bitcast.14), kind=kOutput, calls=%fused_computation.7 | convolution fusion | flops 352436224 | bytes 2097152 | tf_op jit(solution)/shard_map/dot_general | solution.py:71
  205.3 0.8 pad_maximum_fusion
  206.2 7.0 %reduce-scatter.2.cloned.1.call-done = bf16[2,32,1792]{2,1,0:T(8,128)(2,1)} async-done(((bf16[2,32,3584]{2,1,0:T(8,128)(2,1)}), bf16[2,32,1792]{2,1,0:T(8,128)(2,1)}) %reduce-scatter.2.cloned.1.call-update) | async-done | bytes 229392 | tf_op jit(solution)/shard_map/reduce_scatter | solution.py:78
  213.2 1.7 add_convert_fusion
  (12 shorter events, 0.1 us)
Async XLA Ops:
  6.5 60.8 %copy-start = (bf16[256,3584]{1,0:T(8,128)(2,1)S(1)}, bf16[256,3584]{1,0:T(8,128)(2,1)}, u32[]{:S(2)}) copy-start(bf16[256,3584]{1,0:T(8,128)(2,1)} %param.11) | copy-start | bytes 5505028
  13.0 50.0 %all-to-all-start = ((bf16[8,32,3584]{2,1,0:T(8,128)(2,1)}), bf16[8,32,3584]{2,1,0:T(8,128)(2,1)}, u32[]{:S(2)}, u32[]{:S(2)}) async-start(bf16[8,32,3584]{2,1,0:T(8,128)(2,1)} %bitcast.41), calls=%async_computation | async-start | bytes 3670016 | tf_op jit(solution)/shard_map/all_to_all | solution.py:62
  63.0 46.6 %all-to-all-start.2 = ((bf16[8,32,3584]{2,1,0:T(8,128)(2,1)}), bf16[8,32,3584]{2,1,0:T(8,128)(2,1)}, u32[]{:S(2)}, u32[]{:S(2)}) async-start(bf16[8,32,3584]{2,1,0:T(8,128)(2,1)} %bitcast.40), calls=%async_computation.2 | async-start | bytes 3670016 | tf_op jit(solution)/shard_map/all_to_all | solution.py:62
  109.5 46.5 %all-to-all-start.1 = ((bf16[8,32,3584]{2,1,0:T(8,128)(2,1)}), bf16[8,32,3584]{2,1,0:T(8,128)(2,1)}, u32[]{:S(2)}, u32[]{:S(2)}) async-start(bf16[8,32,3584]{2,1,0:T(8,128)(2,1)} %bitcast.39), calls=%async_computation.1 | async-start | bytes 3670016 | tf_op jit(solution)/shard_map/all_to_all | solution.py:56
  156.1 4.5 %copy-start.2 = (f32[2,32,2]{1,2,0:T(2,128)S(1)}, f32[2,32,2]{1,2,0:T(2,128)}, u32[]{:S(2)}) copy-start(f32[2,32,2]{1,2,0:T(2,128)} %param.9) | copy-start | bytes 1540
  156.1 46.7 %all-to-all-start.3 = ((bf16[8,32,3584]{2,1,0:T(8,128)(2,1)}), bf16[8,32,3584]{2,1,0:T(8,128)(2,1)}, u32[]{:S(2)}, u32[]{:S(2)}) async-start(bf16[8,32,3584]{2,1,0:T(8,128)(2,1)} %bitcast.38), calls=%async_computation.3 | async-start | bytes 3670016 | tf_op jit(solution)/shard_map/all_to_all | solution.py:56
  160.5 52.6 %reduce-scatter.2.cloned.1.call-start = ((), (), s32[]{:S(2)}) async-start(), calls=%async_computation.5 | async-start | bytes 688128 | tf_op jit(solution)/shard_map/reduce_scatter | solution.py:78
  163.2 42.9 %copy-start.1 = (bf16[2,32,3584]{2,1,0:T(8,128)(2,1)S(1)}, bf16[2,32,3584]{2,1,0:T(8,128)(2,1)}, u32[]{:S(2)}) copy-start(bf16[2,32,3584]{2,1,0:T(8,128)(2,1)} %param.6) | copy-start | bytes 1376260
Sparse Core Ops, SparseCore 0:
  206.2 6.9 reduce-scatter.1
where the time goes:
time: 222 us
  waiting for transfers between devices  161 us (73%)
  starting transfers between devices  20.4 us (9%)
  matrix products  19.7 us (9%)
  between operations  13.5 us (6%)
  other arithmetic  5.56 us (3%)
    all_to_all x2, waiting for transfers between devices, dispatch(): lax.all_to_all(buffer, 'dev', split_axis=0, concat_axis=0, tiled=True)  77.6 us
    all_to_all x2, waiting for transfers between devices, run_expert(): lax.all_to_all(pieces.reshape(senders, count, -1), 'dev', split_axis=0, c...  76.3 us
    all_to_all x2, starting transfers between devices, dispatch(): lax.all_to_all(buffer, 'dev', split_axis=0, concat_axis=0, tiled=True)  11.6 us
    dot_general x2, matrix products, run_expert(): jnp.dot(act, w_out, preferred_element_type=jnp.float32).astype(jnp.bfloat16)  10.9 us
    all_to_all x2, starting transfers between devices, run_expert(): lax.all_to_all(pieces.reshape(senders, count, -1), 'dev', split_axis=0, c...  8.76 us
    reduce_scatter x1, waiting for transfers between devices, local(): lax.psum_scatter(jnp.stack(terms).astype(jnp.bfloat16), 'sub', scatter_di...  6.98 us
    dot_general x2, matrix products, local(): jnp.dot(tables[step][1].T, flat_back, precision=lax.Precision.HIGHEST, pr...  4.98 us
  transfers between devices with their start and end apart: 5, of which 5 were waited for; matrix products, arithmetic and copies ran while one was open for 7% of the time, Pallas kernels for 0%

commit v1 on v0

--- a/solution.py
+++ b/solution.py
@@ -4,6 +4,7 @@
 from jax.sharding import PartitionSpec as P
 
 EPS = 1e-06
+LANES = 128
 
 
 def route_tables(routes_now, weight_now, n_dev, cap, span):
@@ -22,7 +23,7 @@
     return (select, weigh)
 
 
-def local(hidden, norm_gain, routes, route_weight, w_in, w_out):
+def packed_blocks(hidden, norm_gain, routes, route_weight, w_in, w_out):
     batches, rows, width = hidden.shape
     n_dev = lax.axis_size("dev")
     n_sub = lax.axis_size("sub")
@@ -83,6 +84,91 @@
     return layer_out
 
 
+def swap_cores(value):
+    return lax.ppermute(value, "sub", [(0, 1), (1, 0)])
+
+
+def along(value, step, experts):
+    pairs = [(2 * z + x, 2 * ((z + step) % experts) + x) for z in range(experts) for x in range(2)]
+    return lax.ppermute(value, "dev", pairs)
+
+
+def across(value, n_dev):
+    return lax.ppermute(value, "dev", [(i, i ^ 1) for i in range(n_dev)])
+
+
+def whole_blocks(hidden, norm_gain, routes, route_weight, w_in, w_out):
+    batches, rows, width = hidden.shape
+    n_dev = lax.axis_size("dev")
+    experts = n_dev // 2
+    core = lax.axis_index("sub")
+    mine = lax.axis_index("dev") // 2
+    w_in_other = swap_cores(w_in)
+    w_out_other = swap_cores(w_out)
+
+    hid = lax.dynamic_index_in_dim(hidden, core, 0, keepdims=False).astype(jnp.float32)
+    route = lax.dynamic_index_in_dim(routes, core, 0, keepdims=False)
+    weight = lax.dynamic_index_in_dim(route_weight, core, 0, keepdims=False)
+    normed = (
+        hid * lax.rsqrt(jnp.mean(hid * hid, axis=-1, keepdims=True) + EPS) * norm_gain
+    ).astype(jnp.bfloat16)
+    lane = jnp.arange(LANES, dtype=jnp.int32)[None, :]
+    gate = sum(
+        jnp.where(route[:, k : k + 1] == lane % experts, weight[:, k : k + 1], jnp.float32(0.0))
+        for k in range(route.shape[1])
+    )
+    high = gate.astype(jnp.bfloat16).astype(jnp.float32)
+    tail = jnp.where(lane < experts, high, jnp.where(lane < 2 * experts, gate - high, 0.0))
+    block = jnp.concatenate([normed, tail.astype(jnp.bfloat16)], axis=1)
+
+    order = [1, 3, 2]
+    column = {0: block}
+    for k in order:
+        column[k] = along(block, k, experts)
+    beside = {k: across(column[k], n_dev) for k in [0] + order}
+
+    def expert(ks):
+        x = jnp.concatenate([part[k] for k in ks for part in (column, beside)], axis=0)
+        gates = x[:, width:].astype(jnp.float32)
+        keep = (lane == mine) | (lane == mine + experts)
+        scale = jnp.sum(jnp.where(keep, gates, 0.0), axis=1, keepdims=True)
+        x = x[:, :width]
+        out = 0.0
+        for up, down in ((w_in, w_out), (w_in_other, w_out_other)):
+            inner = jnp.dot(x, up, preferred_element_type=jnp.float32)
+            act = jax.nn.silu(inner).astype(jnp.bfloat16)
+            out = out + jnp.dot(act, down, preferred_element_type=jnp.float32)
+        out = (out * scale).astype(jnp.bfloat16).reshape(len(ks), 2, rows, width)
+        return {k: out[i, 0] for i, k in enumerate(ks)}, {k: out[i, 1] for i, k in enumerate(ks)}
+
+    own, give = {}, {}
+    for ks in ([0, 1], [3], [2]):
+        a, b = expert(ks)
+        own.update(a)
+        give.update(b)
+    total = {}
+    for k in [1, 3, 2, 0]:
+        total[k] = own[k].astype(jnp.float32) + across(give[k], n_dev).astype(jnp.float32)
+    result = hid + total[0]
+    for k in order:
+        result = result + along(total[k].astype(jnp.bfloat16), -k, experts).astype(jnp.float32)
+    result = result.astype(jnp.bfloat16)
+    half = width // 2
+    kept = lax.dynamic_slice_in_dim(result, core * half, half, 1)
+    passed = swap_cores(lax.dynamic_slice_in_dim(result, (1 - core) * half, half, 1))
+    first = core == 0
+    return jnp.stack([jnp.where(first, kept, passed), jnp.where(first, passed, kept)])
+
+
+def local(hidden, norm_gain, routes, route_weight, w_in, w_out):
+    batches, rows, _ = hidden.shape
+    n_dev = lax.axis_size("dev")
+    cap = max(2, 2 * rows * routes.shape[2] // (n_dev // 2))
+    if cap >= rows and batches == lax.axis_size("sub") == 2 and n_dev == 8:
+        return whole_blocks(hidden, norm_gain, routes, route_weight, w_in, w_out)
+    return packed_blocks(hidden, norm_gain, routes, route_weight, w_in, w_out)
+
+
 def solution(mesh):
     placed = (
         P(None, ("groups", "dev"), None),

time: 222 us -> 104 us (0.47)
  waiting for transfers between devices: 161 us -> 49.6 us
  between operations: 13.5 us -> 0.25 us
  local copies, waits for them, and re-layouts: 1.61 us -> 5.72 us
  other arithmetic: 5.56 us -> 8.51 us
  starting transfers between devices: 20.4 us -> 17.7 us
  matrix products: 19.7 us -> 22.1 us
    all_to_all x4 -> x0, waiting for transfers between devices: 154 us -> none  [the longest x2 77.6 us: dispatch(): lax.all_to_all(buffer, 'dev', split_axis=0, concat_axis=0, tiled=True)]
    ppermute x0 -> x17, waiting for transfers between devices: none -> 49.6 us  [the longest x6 29.7 us: along(): return lax.ppermute(value, 'dev', pairs)]
    all_to_all x4 -> x0, starting transfers between devices: 20.3 us -> none  [the longest x2 11.6 us: dispatch(): lax.all_to_all(buffer, 'dev', split_axis=0, concat_axis=0, tiled=True)]
    ppermute x0 -> x17, starting transfers between devices: none -> 17.7 us  [the longest x8 9.26 us: across(): return lax.ppermute(value, 'dev', [(i, i ^ 1) for i in range(n_dev)])]
    reduce_scatter x1 -> x0, waiting for transfers between devices: 6.98 us -> none  [local(): lax.psum_scatter(jnp.stack(terms).astype(jnp.bfloat16), 'sub', scatter_di...]
    unnamed x6 -> x32, local copies, waits for them, and re-layouts: 0.01 us -> 4.03 us
    dot_general x6, matrix products: 19.7 us -> 22.1 us  [expert(): out = out + jnp.dot(act, down, preferred_element_type=jnp.float32)]
    convert_element_type x3 -> x6, other arithmetic: 2.95 us -> 4.5 us  [the longest x3 2.08 us: whole_blocks(): total[k].astype(jnp.bfloat16)]
  transfers between devices with their start and end apart: 5 -> 17, of which waited for: 5 -> 10; matrix products, arithmetic and copies ran while one was open for 7% -> 23% of each run, Pallas kernels for 0% -> 0%
where the time goes in v1:
time: 104 us
  waiting for transfers between devices  49.6 us (48%)
  matrix products  22.1 us (21%)
  starting transfers between devices  17.7 us (17%)
  other arithmetic  8.51 us (8%)
  local copies, waits for them, and re-layouts  5.72 us (6%)
    ppermute x6, waiting for transfers between devices, along(): return lax.ppermute(value, 'dev', pairs)  29.7 us
    dot_general x6, matrix products, expert(): out = out + jnp.dot(act, down, preferred_element_type=jnp.float32)  22.1 us
    ppermute x8, waiting for transfers between devices, across(): return lax.ppermute(value, 'dev', [(i, i ^ 1) for i in range(n_dev)])  18.7 us
    ppermute x8, starting transfers between devices, across(): return lax.ppermute(value, 'dev', [(i, i ^ 1) for i in range(n_dev)])  9.26 us
    ppermute x6, starting transfers between devices, along(): return lax.ppermute(value, 'dev', pairs)  8.33 us
    unnamed x32, local copies, waits for them, and re-layouts  4.03 us
  transfers between devices with their start and end apart: 17, of which 10 were waited for; matrix products, arithmetic and copies ran while one was open for 23% of the time, Pallas kernels for 0%

profile of v1, /device:TPU:0, one launch (start us, length us, event | category | flops | bytes accessed | tf_op | source)
XLA Modules:
  0.0 103.9 jit_solution(16168015071919912700)
XLA Ops:
  1.4 1.1 %fusion.10 = f32[32]{0:T(128)S(1)} fusion(bf16[2,32,3584]{2,1,0:T(8,128)(2,1)} %param.6, s32[]{:T(128)S(6)} %select_n.73), kind=kLoop, calls=%fused_computation.17 | loop fusion | flops 344032 | bytes 229508 | tf_op jit(solution)/shard_map/reduce_sum | solution.py:113
  2.5 1.2 %fusion.12 = bf16[32,3584]{1,0:T(8,128)(2,1)S(1)} fusion(f32[3584]{0:T(1024)} %param.7, f32[32]{0:T(128)S(1)} %add_rsqrt_fusion, bf16[2,32,3584]{2,1,0:T(8,128)(2,1)} %param.6, s32[]{:T(128)S(6)} %select_n.73), kind=kLoop, calls=%fused_computation.19 | loop fusion | flops 458752 | bytes 473220 | tf_op jit(solution)/shard_map/convert_element_type | solution.py:114
  4.5 5.0 %collective-permute-start.8 = (bf16[32,3712]{1,0:T(8,128)(2,1)}, bf16[32,3712]{1,0:T(8,128)(2,1)}, u32[]{:S(2)}, u32[]{:S(2)}) collective-permute-start(bf16[32,3712]{1,0:T(8,128)(2,1)} %pad_maximum_fusion.1), channel_id=1, source_target_pairs={{0,12},{2,14},{4,0},{6,2},{8,4},{10,6},{12,8},{14,10},{1,13},{3,15... | collective-permute-start | bytes 712712 | tf_op jit(solution)/shard_map/ppermute | solution.py:93
  9.6 1.5 %collective-permute-start = (bf16[32,3712]{1,0:T(8,128)(2,1)}, bf16[32,3712]{1,0:T(8,128)(2,1)S(1)}, u32[]{:S(2)}, u32[]{:S(2)}) collective-permute-start(bf16[32,3712]{1,0:T(8,128)(2,1)} %pad_maximum_fusion.1), channel_id=1, source_target_pairs={{0,2},{2,0},{4,6},{6,4},{8,10},{10,8},{12,14},{14,12},{1,3},{3,1},... | collective-permute-start | bytes 712712 | tf_op jit(solution)/shard_map/ppermute | solution.py:97
  11.1 1.0 collective-permute-start.12
  12.1 4.0 %collective-permute-done.8 = bf16[32,3712]{1,0:T(8,128)(2,1)} collective-permute-done((bf16[32,3712]{1,0:T(8,128)(2,1)}, bf16[32,3712]{1,0:T(8,128)(2,1)}, u32[]{:S(2)}, u32[]{:S(2)}) %collective-permute-start.8) | collective-permute-done | bytes 237600 | tf_op jit(solution)/shard_map/ppermute | solution.py:93
  16.1 1.0 constant_dynamic-update-slice_fusion.1
  17.0 12.9 %collective-permute-done.12 = bf16[32,3712]{1,0:T(8,128)(2,1)S(1)} collective-permute-done((bf16[32,3712]{1,0:T(8,128)(2,1)}, bf16[32,3712]{1,0:T(8,128)(2,1)S(1)}, u32[]{:S(2)}, u32[]{:S(2)}) %collective-permute-start.12) | collective-permute-done | bytes 237600 | tf_op jit(solution)/shard_map/ppermute | solution.py:93
  30.7 1.5 %collective-permute-start.9 = (bf16[32,3712]{1,0:T(8,128)(2,1)}, bf16[32,3712]{1,0:T(8,128)(2,1)S(1)}, u32[]{:S(2)}, u32[]{:S(2)}) collective-permute-start(bf16[32,3712]{1,0:T(8,128)(2,1)} %collective-permute-done.8), channel_id=1, source_target_pairs={{0,2},{2,0},{4,6},{6,4},{8,10},{10,8},{12,14},{14,12},{1,3},{3,1},... | collective-permute-start | bytes 712712 | tf_op jit(solution)/shard_map/ppermute | solution.py:97
  33.8 5.8 %collective-permute-done.9 = bf16[32,3712]{1,0:T(8,128)(2,1)S(1)} collective-permute-done((bf16[32,3712]{1,0:T(8,128)(2,1)}, bf16[32,3712]{1,0:T(8,128)(2,1)S(1)}, u32[]{:S(2)}, u32[]{:S(2)}) %collective-permute-start.9) | collective-permute-done | bytes 237600 | tf_op jit(solution)/shard_map/ppermute | solution.py:97
  39.6 1.5 %collective-permute-start.2 = (bf16[32,3712]{1,0:T(8,128)(2,1)S(1)}, bf16[32,3712]{1,0:T(8,128)(2,1)S(1)}, u32[]{:S(2)}, u32[]{:S(2)}) collective-permute-start(bf16[32,3712]{1,0:T(8,128)(2,1)S(1)} %collective-permute-done.1), channel_id=1, source_target_pairs={{0,2},{2,0},{4,6},{6,4},{8,10},{10,8},{12,14},{14,12},{1,3},{3,1},... | collective-permute-start | bytes 712712 | tf_op jit(solution)/shard_map/ppermute | solution.py:97
  41.1 3.6 %collective-permute-done.13 = bf16[32,3712]{1,0:T(8,128)(2,1)S(1)} collective-permute-done((bf16[32,3712]{1,0:T(8,128)(2,1)}, bf16[32,3712]{1,0:T(8,128)(2,1)S(1)}, u32[]{:S(2)}, u32[]{:S(2)}) %collective-permute-start.13) | collective-permute-done | bytes 237600 | tf_op jit(solution)/shard_map/ppermute | solution.py:97
  44.9 3.4 %collective-permute-done.2 = bf16[32,3712]{1,0:T(8,128)(2,1)S(1)} collective-permute-done((bf16[32,3712]{1,0:T(8,128)(2,1)S(1)}, bf16[32,3712]{1,0:T(8,128)(2,1)S(1)}, u32[]{:S(2)}, u32[]{:S(2)}) %collective-permute-start.2) | collective-permute-done | bytes 237600 | tf_op jit(solution)/shard_map/ppermute | solution.py:97
  49.1 3.7 %fusion.53 = f32[64,3584]{1,0:T(8,128)} fusion(bf16[256,3584]{1,0:T(8,128)(2,1)} %param.11, bf16[3584,256]{1,0:T(8,128)(2,1)S(1)} %copy-done.1, bf16[64,3712]{1,0:T(8,128)(2,1)S(1)} %constant_dynamic-update-slice_fusion), kind=kOutput, calls=%fused_computation.59 | convolution fusion | flops 234962944 | bytes 5046272 | tf_op jit(solution)/shard_map/dot_general | solution.py:140
  52.8 3.7 %fusion.44 = f32[64,3584]{1,0:T(8,128)} fusion(bf16[256,3584]{1,0:T(8,128)(2,1)} %param.11, bf16[3584,256]{1,0:T(8,128)(2,1)S(1)} %copy-done.1, bf16[64,3712]{1,0:T(8,128)(2,1)S(1)} %constant_dynamic-update-slice_fusion.2), kind=kOutput, calls=%fused_computation.56 | convolution fusion | flops 234962944 | bytes 5046272 | tf_op jit(solution)/shard_map/dot_general | solution.py:140
  56.5 1.2 %pad_maximum_fusion = bf16[128,3712]{1,0:T(8,128)(2,1)S(1)} fusion(bf16[32,3712]{1,0:T(8,128)(2,1)} %copy-done.13, bf16[32,3712]{1,0:T(8,128)(2,1)} %copy-done.11, bf16[32,3712]{1,0:T(8,128)(2,1)} %copy-done.12, bf16[32,128]{1,0:T(8,128)(2,1)S(1)} %fusion.62, bf16[32,3584]{1,0:T(8,128)(2,1)S(1)} %fusion.12), kind=kLoop, calls=%fused_computation.9 | loop fusion | flops 4751360 | bytes 1900544 | tf_op jit(solution)/shard_map/concatenate | solution.py:131
  57.7 4.0 %fusion.35 = f32[128,3584]{1,0:T(8,128)} fusion(bf16[256,3584]{1,0:T(8,128)(2,1)} %param.11, bf16[3584,256]{1,0:T(8,128)(2,1)S(1)} %copy-done.1, bf16[128,3712]{1,0:T(8,128)(2,1)S(1)} %pad_maximum_fusion), kind=kOutput, calls=%fused_computation.51 | convolution fusion | flops 469925888 | bytes 6422528 | tf_op jit(solution)/shard_map/dot_general | solution.py:140
  61.7 3.9 %fusion.1 = bf16[128,3584]{1,0:T(8,128)(2,1)S(1)} fusion(f32[128,3584]{1,0:T(8,128)} %fusion.35, bf16[256,3584]{1,0:T(8,128)(2,1)} %collective-permute-done.4, f32[128]{0:T(128)S(1)} %select_reduce_fusion, bf16[3584,256]{1,0:T(8,128)(2,1)} %collective-permute-done.3, bf16[128,3712]{1,0:T(8,128)(2,1)S(1)} %pad_maximum_fusion), kind=kOutput, calls=%fused_computation.2 | convolution fusion | flops 471302144 | bytes 7340544 | tf_op jit(solution)/shard_map/dot_general | solution.py:140
  67.4 1.1 %collective-permute-start.5 = (bf16[32,3584]{1,0:T(8,128)(2,1)}, bf16[32,3584]{1,0:T(8,128)(2,1)}, u32[]{:S(2)}, u32[]{:S(2)}) collective-permute-start(bf16[32,3584]{1,0:T(8,128)(2,1)} %get-tuple-element.7), channel_id=1, source_target_pairs={{0,2},{2,0},{4,6},{6,4},{8,10},{10,8},{12,14},{14,12},{1,3},{3,1},... | collective-permute-start | bytes 688136 | tf_op jit(solution)/shard_map/ppermute | solution.py:97
  68.5 3.4 %fusion.4 = bf16[64,3584]{1,0:T(8,128)(2,1)S(1)} fusion(f32[64,3584]{1,0:T(8,128)S(1)} %copy-done.3, bf16[256,3584]{1,0:T(8,128)(2,1)} %collective-permute-done.4, f32[64]{0:T(128)S(1)} %get-tuple-element.5, bf16[3584,256]{1,0:T(8,128)(2,1)} %collective-permute-done.3, bf16[64,3712]{1,0:T(8,128)(2,1)S(1)} %constant_dynamic-update-slice_fusion), kind=kOutput, calls=%fused_computation.7 | convolution fusion | flops 235651072 | bytes 5505536 | tf_op jit(solution)/shard_map/dot_general | solution.py:140
  72.0 1.0 collective-permute-start.10
  73.0 3.4 %fusion.5 = bf16[64,3584]{1,0:T(8,128)(2,1)S(1)} fusion(f32[64,3584]{1,0:T(8,128)S(1)} %copy-done.2, bf16[256,3584]{1,0:T(8,128)(2,1)} %collective-permute-done.4, f32[64]{0:T(128)S(1)} %get-tuple-element.6, bf16[3584,256]{1,0:T(8,128)(2,1)} %collective-permute-done.3, bf16[64,3712]{1,0:T(8,128)(2,1)S(1)} %copy-done.7), kind=kOutput, calls=%fused_computation.8 | convolution fusion | flops 235651072 | bytes 5505536 | tf_op jit(solution)/shard_map/dot_general | solution.py:140
  76.5 1.1 %collective-permute-start.14 = (bf16[32,3584]{1,0:T(8,128)(2,1)S(1)}, bf16[32,3584]{1,0:T(8,128)(2,1)S(1)}, u32[]{:S(2)}, u32[]{:S(2)}) collective-permute-start(bf16[32,3584]{1,0:T(8,128)(2,1)S(1)} %slice_bitcast_fusion), channel_id=1, source_target_pairs={{0,2},{2,0},{4,6},{6,4},{8,10},{10,8},{12,14},{14,12},{1,3},{3,1},... | collective-permute-start | bytes 688136 | tf_op jit(solution)/shard_map/ppermute | solution.py:97
  77.7 1.0 fusion.19
  78.7 2.0 %collective-permute-start.7 = (bf16[32,3584]{1,0:T(8,128)(2,1)S(1)}, bf16[32,3584]{1,0:T(8,128)(2,1)S(1)}, u32[]{:S(2)}, u32[]{:S(2)}) collective-permute-start(bf16[32,3584]{1,0:T(8,128)(2,1)S(1)} %fusion.19), channel_id=1, source_target_pairs={{0,12},{2,14},{4,0},{6,2},{8,4},{10,6},{12,8},{14,10},{1,13},{3,15... | collective-permute-start | bytes 688136 | tf_op jit(solution)/shard_map/ppermute | solution.py:93
  80.6 4.5 %collective-permute-done.10 = bf16[32,3584]{1,0:T(8,128)(2,1)} collective-permute-done((bf16[32,3584]{1,0:T(8,128)(2,1)S(1)}, bf16[32,3584]{1,0:T(8,128)(2,1)}, u32[]{:S(2)}, u32[]{:S(2)}) %collective-permute-start.10) | collective-permute-done | bytes 229408 | tf_op jit(solution)/shard_map/ppermute | solution.py:97
  85.2 1.0 fusion.18
  86.3 1.3 %collective-permute-done.14 = bf16[32,3584]{1,0:T(8,128)(2,1)S(1)} collective-permute-done((bf16[32,3584]{1,0:T(8,128)(2,1)S(1)}, bf16[32,3584]{1,0:T(8,128)(2,1)S(1)}, u32[]{:S(2)}, u32[]{:S(2)}) %collective-permute-start.14) | collective-permute-done | bytes 229408 | tf_op jit(solution)/shard_map/ppermute | solution.py:97
  87.9 6.3 %collective-permute-done.11 = bf16[32,3584]{1,0:T(8,128)(2,1)S(1)} collective-permute-done((bf16[32,3584]{1,0:T(8,128)(2,1)S(1)}, bf16[32,3584]{1,0:T(8,128)(2,1)S(1)}, u32[]{:S(2)}, u32[]{:S(2)}) %collective-permute-start.11) | collective-permute-done | bytes 229408 | tf_op jit(solution)/shard_map/ppermute | solution.py:93
  94.2 6.4 %collective-permute-done.15 = bf16[32,3584]{1,0:T(8,128)(2,1)S(1)} collective-permute-done((bf16[32,3584]{1,0:T(8,128)(2,1)S(1)}, bf16[32,3584]{1,0:T(8,128)(2,1)S(1)}, u32[]{:S(2)}, u32[]{:S(2)}) %collective-permute-start.15) | collective-permute-done | bytes 229408 | tf_op jit(solution)/shard_map/ppermute | solution.py:93
  100.6 1.1 %fusion.16 = bf16[32,3584]{1,0:T(8,128)(2,1)S(1)} fusion(bf16[32,3584]{1,0:T(8,128)(2,1)S(1)} %collective-permute-done.15, bf16[32,3584]{1,0:T(8,128)(2,1)S(1)} %collective-permute-done.11, bf16[32,3584]{1,0:T(8,128)(2,1)S(1)} %collective-permute-done.7, bf16[32,3584]{1,0:T(8,128)(2,1)} %collective-permute-done.5, bf16[2,2,32,3584]{3,2,1,0:T(8,128)(2,1)S(1)} %bitcast.66, ...), kind=kLoop, calls=%fused_computation.23 | loop fusion | flops 1376256 | bytes 1605636 | tf_op jit(solution)/shard_map/convert_element_type | solution.py:155
  101.8 1.3 %collective-permute-done.16 = bf16[32,1792]{1,0:T(8,128)(2,1)S(1)} collective-permute-done((bf16[32,1792]{1,0:T(8,128)(2,1)S(1)}, bf16[32,1792]{1,0:T(8,128)(2,1)S(1)}, u32[]{:S(2)}, u32[]{:S(2)}) %collective-permute-start.16) | collective-permute-done | bytes 114720 | tf_op jit(solution)/shard_map/ppermute | solution.py:88
  (67 shorter events, 8.5 us)
Async XLA Ops:
  0.0 0.7 copy-start
  2.5 46.6 %copy-start.1 = (bf16[3584,256]{1,0:T(8,128)(2,1)S(1)}, bf16[3584,256]{1,0:T(8,128)(2,1)}, u32[]{:S(2)}) copy-start(bf16[3584,256]{1,0:T(8,128)(2,1)} %param.10) | copy-start | bytes 5505028
  4.5 11.6 %collective-permute-start.8 = (bf16[32,3712]{1,0:T(8,128)(2,1)}, bf16[32,3712]{1,0:T(8,128)(2,1)}, u32[]{:S(2)}, u32[]{:S(2)}) collective-permute-start(bf16[32,3712]{1,0:T(8,128)(2,1)} %pad_maximum_fusion.1), channel_id=1, source_target_pairs={{0,12},{2,14},{4,0},{6,2},{8,4},{10,6},{12,8},{14,10},{1,13},{3,15... | collective-permute-start | bytes 712712 | tf_op jit(solution)/shard_map/ppermute | solution.py:93
  9.6 23.6 %collective-permute-start.1 = (bf16[32,3712]{1,0:T(8,128)(2,1)}, bf16[32,3712]{1,0:T(8,128)(2,1)S(1)}, u32[]{:S(2)}, u32[]{:S(2)}) collective-permute-start(bf16[32,3712]{1,0:T(8,128)(2,1)} %pad_maximum_fusion.1), channel_id=1, source_target_pairs={{0,4},{2,6},{4,8},{6,10},{8,12},{10,14},{12,0},{14,2},{1,5},{3,7},... | collective-permute-start | bytes 712712 | tf_op jit(solution)/shard_map/ppermute | solution.py:93
  9.6 35.3 %collective-permute-start = (bf16[32,3712]{1,0:T(8,128)(2,1)}, bf16[32,3712]{1,0:T(8,128)(2,1)S(1)}, u32[]{:S(2)}, u32[]{:S(2)}) collective-permute-start(bf16[32,3712]{1,0:T(8,128)(2,1)} %pad_maximum_fusion.1), channel_id=1, source_target_pairs={{0,2},{2,0},{4,6},{6,4},{8,10},{10,8},{12,14},{14,12},{1,3},{3,1},... | collective-permute-start | bytes 712712 | tf_op jit(solution)/shard_map/ppermute | solution.py:97
  11.1 18.9 %collective-permute-start.12 = (bf16[32,3712]{1,0:T(8,128)(2,1)}, bf16[32,3712]{1,0:T(8,128)(2,1)S(1)}, u32[]{:S(2)}, u32[]{:S(2)}) collective-permute-start(bf16[32,3712]{1,0:T(8,128)(2,1)} %pad_maximum_fusion.1), channel_id=1, source_target_pairs={{0,8},{2,10},{4,12},{6,14},{8,0},{10,2},{12,4},{14,6},{1,9},{3,11}... | collective-permute-start | bytes 712712 | tf_op jit(solution)/shard_map/ppermute | solution.py:93
  12.1 49.6 %collective-permute-start.3 = (bf16[3584,256]{1,0:T(8,128)(2,1)}, bf16[3584,256]{1,0:T(8,128)(2,1)}, u32[]{:S(2)}, u32[]{:S(2)}) collective-permute-start(bf16[3584,256]{1,0:T(8,128)(2,1)} %param.10), channel_id=1, source_target_pairs={{0,1},{1,0},{2,3},{3,2},{4,5},{5,4},{6,7},{7,6},{8,9},{9,8},{10,11... | collective-permute-start | bytes 5505032 | tf_op jit(solution)/shard_map/ppermute | solution.py:88
  16.1 45.6 %collective-permute-start.4 = (bf16[256,3584]{1,0:T(8,128)(2,1)}, bf16[256,3584]{1,0:T(8,128)(2,1)}, u32[]{:S(2)}, u32[]{:S(2)}) collective-permute-start(bf16[256,3584]{1,0:T(8,128)(2,1)} %param.11), channel_id=1, source_target_pairs={{0,1},{1,0},{2,3},{3,2},{4,5},{5,4},{6,7},{7,6},{8,9},{9,8},{10,11... | collective-permute-start | bytes 5505032 | tf_op jit(solution)/shard_map/ppermute | solution.py:88
  30.0 0.7 copy-start.14
  30.7 8.9 %collective-permute-start.9 = (bf16[32,3712]{1,0:T(8,128)(2,1)}, bf16[32,3712]{1,0:T(8,128)(2,1)S(1)}, u32[]{:S(2)}, u32[]{:S(2)}) collective-permute-start(bf16[32,3712]{1,0:T(8,128)(2,1)} %collective-permute-done.8), channel_id=1, source_target_pairs={{0,2},{2,0},{4,6},{6,4},{8,10},{10,8},{12,14},{14,12},{1,3},{3,1},... | collective-permute-start | bytes 712712 | tf_op jit(solution)/shard_map/ppermute | solution.py:97
  33.1 19.6 %copy-start.11 = (bf16[32,3712]{1,0:T(8,128)(2,1)}, bf16[32,3712]{1,0:T(8,128)(2,1)S(1)}, u32[]{:S(2)}) copy-start(bf16[32,3712]{1,0:T(8,128)(2,1)S(1)} %collective-permute-done.1) | copy-start | bytes 712708
  33.1 11.5 %collective-permute-start.13 = (bf16[32,3712]{1,0:T(8,128)(2,1)}, bf16[32,3712]{1,0:T(8,128)(2,1)S(1)}, u32[]{:S(2)}, u32[]{:S(2)}) collective-permute-start(bf16[32,3712]{1,0:T(8,128)(2,1)} %copy-done.14), channel_id=1, source_target_pairs={{0,2},{2,0},{4,6},{6,4},{8,10},{10,8},{12,14},{14,12},{1,3},{3,1},... | collective-permute-start | bytes 712712 | tf_op jit(solution)/shard_map/ppermute | solution.py:97
  39.6 8.7 %collective-permute-start.2 = (bf16[32,3712]{1,0:T(8,128)(2,1)S(1)}, bf16[32,3712]{1,0:T(8,128)(2,1)S(1)}, u32[]{:S(2)}, u32[]{:S(2)}) collective-permute-start(bf16[32,3712]{1,0:T(8,128)(2,1)S(1)} %collective-permute-done.1), channel_id=1, source_target_pairs={{0,2},{2,0},{4,6},{6,4},{8,10},{10,8},{12,14},{14,12},{1,3},{3,1},... | collective-permute-start | bytes 712712 | tf_op jit(solution)/shard_map/ppermute | solution.py:97
  44.7 8.0 %copy-start.6 = (bf16[64,3712]{1,0:T(8,128)(2,1)}, bf16[64,3712]{1,0:T(8,128)(2,1)S(1)}, u32[]{:S(2)}) copy-start(bf16[64,3712]{1,0:T(8,128)(2,1)S(1)} %constant_dynamic-update-slice_fusion.2) | copy-start | bytes 1425412
  44.8 7.9 %copy-start.12 = (bf16[32,3712]{1,0:T(8,128)(2,1)}, bf16[32,3712]{1,0:T(8,128)(2,1)S(1)}, u32[]{:S(2)}) copy-start(bf16[32,3712]{1,0:T(8,128)(2,1)S(1)} %collective-permute-done) | copy-start | bytes 712708
  48.3 0.7 copy-start.13
  61.7 6.8 %copy-start.3 = (f32[64,3584]{1,0:T(8,128)S(1)}, f32[64,3584]{1,0:T(8,128)}, u32[]{:S(2)}) copy-start(f32[64,3584]{1,0:T(8,128)} %fusion.53) | copy-start | bytes 2752516
  65.6 2.9 %copy-start.4 = (bf16[128,3584]{1,0:T(8,128)(2,1)}, bf16[128,3584]{1,0:T(8,128)(2,1)S(1)}, u32[]{:S(2)}) copy-start(bf16[128,3584]{1,0:T(8,128)(2,1)S(1)} %fusion.1) | copy-start | bytes 2752516
  66.5 11.2 %collective-permute-start.6 = (bf16[32,3584]{1,0:T(8,128)(2,1)}, bf16[32,3584]{1,0:T(8,128)(2,1)}, u32[]{:S(2)}, u32[]{:S(2)}) collective-permute-start(bf16[32,3584]{1,0:T(8,128)(2,1)} %get-tuple-element.8), channel_id=1, source_target_pairs={{0,2},{2,0},{4,6},{6,4},{8,10},{10,8},{12,14},{14,12},{1,3},{3,1},... | collective-permute-start | bytes 688136 | tf_op jit(solution)/shard_map/ppermute | solution.py:97
  67.4 20.4 %collective-permute-start.5 = (bf16[32,3584]{1,0:T(8,128)(2,1)}, bf16[32,3584]{1,0:T(8,128)(2,1)}, u32[]{:S(2)}, u32[]{:S(2)}) collective-permute-start(bf16[32,3584]{1,0:T(8,128)(2,1)} %get-tuple-element.7), channel_id=1, source_target_pairs={{0,2},{2,0},{4,6},{6,4},{8,10},{10,8},{12,14},{14,12},{1,3},{3,1},... | collective-permute-start | bytes 688136 | tf_op jit(solution)/shard_map/ppermute | solution.py:97
  68.5 4.5 %copy-start.2 = (f32[64,3584]{1,0:T(8,128)S(1)}, f32[64,3584]{1,0:T(8,128)}, u32[]{:S(2)}) copy-start(f32[64,3584]{1,0:T(8,128)} %fusion.44) | copy-start | bytes 2752516
  68.5 4.5 %copy-start.7 = (bf16[64,3712]{1,0:T(8,128)(2,1)S(1)}, bf16[64,3712]{1,0:T(8,128)(2,1)}, u32[]{:S(2)}) copy-start(bf16[64,3712]{1,0:T(8,128)(2,1)} %copy-done.6) | copy-start | bytes 1425412
  72.0 1.0 %copy-start.8 = (bf16[64,3584]{1,0:T(8,128)(2,1)}, bf16[64,3584]{1,0:T(8,128)(2,1)S(1)}, u32[]{:S(2)}) copy-start(bf16[64,3584]{1,0:T(8,128)(2,1)S(1)} %fusion.4) | copy-start | bytes 1376260
  72.0 13.2 %collective-permute-start.10 = (bf16[32,3584]{1,0:T(8,128)(2,1)S(1)}, bf16[32,3584]{1,0:T(8,128)(2,1)}, u32[]{:S(2)}, u32[]{:S(2)}) collective-permute-start(bf16[32,3584]{1,0:T(8,128)(2,1)S(1)} %slice_bitcast_fusion.2), channel_id=1, source_target_pairs={{0,2},{2,0},{4,6},{6,4},{8,10},{10,8},{12,14},{14,12},{1,3},{3,1},... | collective-permute-start | bytes 688136 | tf_op jit(solution)/shard_map/ppermute | solution.py:97
  73.0 4.7 %copy-start.5 = (bf16[128,3584]{1,0:T(8,128)(2,1)S(1)}, bf16[128,3584]{1,0:T(8,128)(2,1)}, u32[]{:S(2)}) copy-start(bf16[128,3584]{1,0:T(8,128)(2,1)} %copy-done.4) | copy-start | bytes 2752516
  73.0 12.2 %copy-start.9 = (bf16[64,3584]{1,0:T(8,128)(2,1)S(1)}, bf16[64,3584]{1,0:T(8,128)(2,1)}, u32[]{:S(2)}) copy-start(bf16[64,3584]{1,0:T(8,128)(2,1)} %copy-done.8) | copy-start | bytes 1376260
  76.5 24.1 %copy-start.10 = (bf16[2,32,3584]{2,1,0:T(8,128)(2,1)S(1)}, bf16[2,32,3584]{2,1,0:T(8,128)(2,1)}, u32[]{:S(2)}) copy-start(bf16[2,32,3584]{2,1,0:T(8,128)(2,1)} %param.6) | copy-start | bytes 1376260
  76.5 11.0 %collective-permute-start.14 = (bf16[32,3584]{1,0:T(8,128)(2,1)S(1)}, bf16[32,3584]{1,0:T(8,128)(2,1)S(1)}, u32[]{:S(2)}, u32[]{:S(2)}) collective-permute-start(bf16[32,3584]{1,0:T(8,128)(2,1)S(1)} %slice_bitcast_fusion), channel_id=1, source_target_pairs={{0,2},{2,0},{4,6},{6,4},{8,10},{10,8},{12,14},{14,12},{1,3},{3,1},... | collective-permute-start | bytes 688136 | tf_op jit(solution)/shard_map/ppermute | solution.py:97
  78.7 9.2 %collective-permute-start.7 = (bf16[32,3584]{1,0:T(8,128)(2,1)S(1)}, bf16[32,3584]{1,0:T(8,128)(2,1)S(1)}, u32[]{:S(2)}, u32[]{:S(2)}) collective-permute-start(bf16[32,3584]{1,0:T(8,128)(2,1)S(1)} %fusion.19), channel_id=1, source_target_pairs={{0,12},{2,14},{4,0},{6,2},{8,4},{10,6},{12,8},{14,10},{1,13},{3,15... | collective-permute-start | bytes 688136 | tf_op jit(solution)/shard_map/ppermute | solution.py:93
  86.2 8.0 %collective-permute-start.11 = (bf16[32,3584]{1,0:T(8,128)(2,1)S(1)}, bf16[32,3584]{1,0:T(8,128)(2,1)S(1)}, u32[]{:S(2)}, u32[]{:S(2)}) collective-permute-start(bf16[32,3584]{1,0:T(8,128)(2,1)S(1)} %fusion.18), channel_id=1, source_target_pairs={{0,4},{2,6},{4,8},{6,10},{8,12},{10,14},{12,0},{14,2},{1,5},{3,7},... | collective-permute-start | bytes 688136 | tf_op jit(solution)/shard_map/ppermute | solution.py:93
  87.6 13.0 %collective-permute-start.15 = (bf16[32,3584]{1,0:T(8,128)(2,1)S(1)}, bf16[32,3584]{1,0:T(8,128)(2,1)S(1)}, u32[]{:S(2)}, u32[]{:S(2)}) collective-permute-start(bf16[32,3584]{1,0:T(8,128)(2,1)S(1)} %fusion.17), channel_id=1, source_target_pairs={{0,8},{2,10},{4,12},{6,14},{8,0},{10,2},{12,4},{14,6},{1,9},{3,11}... | collective-permute-start | bytes 688136 | tf_op jit(solution)/shard_map/ppermute | solution.py:93
  101.8 1.4 %collective-permute-start.16 = (bf16[32,1792]{1,0:T(8,128)(2,1)S(1)}, bf16[32,1792]{1,0:T(8,128)(2,1)S(1)}, u32[]{:S(2)}, u32[]{:S(2)}) collective-permute-start(bf16[32,1792]{1,0:T(8,128)(2,1)S(1)} %constant_dynamic-slice_fusion), channel_id=1, source_target_pairs={{0,1},{1,0},{2,3},{3,2},{4,5},{5,4},{6,7},{7,6},{8,9},{9,8},{10,11... | collective-permute-start | bytes 344072 | tf_op jit(solution)/shard_map/ppermute | solution.py:88

commit v2 on v0

--- a/solution.py
+++ b/solution.py
@@ -1,9 +1,16 @@
+import functools
+
 import jax
 import jax.numpy as jnp
 from jax import lax
+from jax.experimental import pallas as pl
+from jax.experimental.pallas import tpu as pltpu
 from jax.sharding import PartitionSpec as P
 
 EPS = 1e-06
+LANES = 128
+VMEM_BYTES = 24 << 20
+LITTLE = pl.CostEstimate(flops=1, bytes_accessed=1, transcendentals=0)
 
 
 def route_tables(routes_now, weight_now, n_dev, cap, span):
@@ -22,7 +29,7 @@
     return (select, weigh)
 
 
-def local(hidden, norm_gain, routes, route_weight, w_in, w_out):
+def packed_blocks(hidden, norm_gain, routes, route_weight, w_in, w_out):
     batches, rows, width = hidden.shape
     n_dev = lax.axis_size("dev")
     n_sub = lax.axis_size("sub")
@@ -83,6 +90,203 @@
     return layer_out
 
 
+def swap_cores(value):
+    return lax.ppermute(value, "sub", [(0, 1), (1, 0)])
+
+
+def along(value, step, experts):
+    pairs = [(2 * z + x, 2 * (z ^ step) + x) for z in range(experts) for x in range(2)]
+    return lax.ppermute(value, "dev", pairs)
+
+
+def across(value, n_dev):
+    return lax.ppermute(value, "dev", [(i, i ^ 1) for i in range(n_dev)])
+
+
+def in_vmem(value):
+    return pltpu.with_memory_space_constraint(value, pltpu.VMEM)
+
+
+def in_hbm(value):
+    return pltpu.with_memory_space_constraint(value, pltpu.HBM)
+
+
+def pack_kernel(experts, core_ref, hidden_ref, gain_ref, routes_ref, weight_ref, block_ref):
+    rows, width = hidden_ref.shape[1:]
+    gain = gain_ref[...].reshape(1, width)
+    hid = hidden_ref[0].astype(jnp.float32)
+    mean = jnp.sum(hid * hid, axis=1, keepdims=True) * (1.0 / width)
+    block_ref[:, :width] = (hid * lax.rsqrt(mean + EPS) * gain).astype(jnp.bfloat16)
+    lane = lax.broadcasted_iota(jnp.int32, (rows, LANES), 1)
+    gate = jnp.zeros((rows, LANES), jnp.float32)
+    for k in range(routes_ref.shape[1]):
+        named = routes_ref[0, k].reshape(rows, 1) == lane % experts
+        gate = gate + jnp.where(named, weight_ref[0, k].reshape(rows, 1), 0.0)
+    high = gate.astype(jnp.bfloat16).astype(jnp.float32)
+    tail = jnp.where(lane < experts, high, jnp.where(lane < 2 * experts, gate - high, 0.0))
+    block_ref[:, width:] = tail.astype(jnp.bfloat16)
+
+
+def pack(core, hidden, norm_gain, routes, route_weight, experts):
+    _, rows, width = hidden.shape
+    top = routes.shape[2]
+    own = lambda i, core: (core[0], 0, 0)
+    return pl.pallas_call(
+        functools.partial(pack_kernel, experts),
+        grid_spec=pltpu.PrefetchScalarGridSpec(
+            num_scalar_prefetch=1,
+            grid=(1,),
+            in_specs=[
+                pl.BlockSpec((1, rows, width), own),
+                pl.BlockSpec((width,), lambda i, core: (0,)),
+                pl.BlockSpec((1, top, rows), own),
+                pl.BlockSpec((1, top, rows), own),
+            ],
+            out_specs=pl.BlockSpec((rows, width + LANES), lambda i, core: (0, 0)),
+        ),
+        out_shape=pltpu.VMEM((rows, width + LANES), jnp.bfloat16),
+        compiler_params=pltpu.CompilerParams(vmem_limit_bytes=VMEM_BYTES),
+    )(
+        core.reshape(1),
+        in_hbm(hidden),
+        in_hbm(norm_gain),
+        in_hbm(routes.swapaxes(1, 2)),
+        in_hbm(route_weight.swapaxes(1, 2)),
+    )
+
+
+def load_kernel(count, *refs):
+    arrived = refs[-1]
+    sources, places = refs[:count], refs[-count - 1 : -1]
+    copies = [
+        pltpu.make_async_copy(source, place, arrived.at[i])
+        for i, (source, place) in enumerate(zip(sources, places))
+    ]
+    for copy in copies:
+        copy.start()
+    for copy in copies:
+        copy.wait()
+
+
+def load(arrays, after):
+    count = len(arrays)
+    return pl.pallas_call(
+        functools.partial(load_kernel, count),
+        in_specs=[pl.BlockSpec(memory_space=pltpu.HBM)] * count
+        + [pl.BlockSpec(memory_space=pl.ANY)] * len(after),
+        out_specs=[pl.BlockSpec(memory_space=pltpu.VMEM)] * count,
+        out_shape=[pltpu.VMEM(a.shape, a.dtype) for a in arrays],
+        scratch_shapes=[pltpu.SemaphoreType.DMA((count,))],
+        compiler_params=pltpu.CompilerParams(vmem_limit_bytes=VMEM_BYTES),
+    )(*[in_hbm(a) for a in arrays], *after)
+
+
+def expert_kernel(count, experts, *refs):
+    blocks, refs = refs[:count], refs[count:]
+    in_refs, down_refs, out_refs = refs[:2], refs[2:4], refs[-count:]
+    rows, width = out_refs[0].shape
+    x = jnp.concatenate([block[...] for block in blocks], axis=0)
+    lane = lax.broadcasted_iota(jnp.int32, x.shape[:1] + (LANES,), 1)
+    mine = lax.axis_index("dev") // 2
+    keep = (lane == mine) | (lane == mine + experts)
+    scale = jnp.sum(
+        jnp.where(keep, x[:, width:].astype(jnp.float32), 0.0), axis=1, keepdims=True
+    )
+    x = x[:, :width]
+    acts = []
+    for ref in in_refs:
+        inner = jnp.dot(x, ref[...], preferred_element_type=jnp.float32)
+        acts.append((inner / (1.0 + jnp.exp(-inner))).astype(jnp.bfloat16))
+    step = width // 4
+    for start in range(0, width, step):
+        out = sum(
+            jnp.dot(act, ref[:, start : start + step], preferred_element_type=jnp.float32)
+            for act, ref in zip(acts, down_refs)
+        )
+        out = (out * scale).astype(jnp.bfloat16)
+        for i, ref in enumerate(out_refs):
+            ref[:, start : start + step] = out[i * rows : (i + 1) * rows]
+
+
+def expert(blocks, weights, experts, after):
+    count = len(blocks)
+    rows, width = blocks[0].shape[0], weights[0].shape[0]
+    hidden_units = 2 * weights[0].shape[1]
+    whole = pl.BlockSpec(memory_space=pltpu.VMEM)
+    return pl.pallas_call(
+        functools.partial(expert_kernel, count, experts),
+        in_specs=[whole] * (count + 4) + [pl.BlockSpec(memory_space=pl.ANY)] * len(after),
+        out_specs=[whole] * count,
+        out_shape=[pltpu.VMEM((rows, width), jnp.bfloat16)] * count,
+        compiler_params=pltpu.CompilerParams(vmem_limit_bytes=VMEM_BYTES),
+    )(*[in_vmem(v) for v in (*blocks, *weights)], *after)
+
+
+def pass_after(value, after):
+    place = pl.BlockSpec(memory_space=pl.ANY)
+    return pl.pallas_call(
+        lambda value_ref, after_ref, out_ref: None,
+        in_specs=[place, place],
+        out_specs=place,
+        out_shape=jax.ShapeDtypeStruct(value.shape, value.dtype),
+        input_output_aliases={0: 0},
+        compiler_params=pltpu.CompilerParams(vmem_limit_bytes=VMEM_BYTES),
+    )(in_vmem(value), in_vmem(after))
+
+
+def whole_blocks(hidden, norm_gain, routes, route_weight, w_in, w_out):
+    batches, rows, width = hidden.shape
+    n_dev = lax.axis_size("dev")
+    experts = n_dev // 2
+    core = lax.axis_index("sub")
+    others = [swap_cores(w_in), swap_cores(w_out)]
+    block = pack(core, hidden, norm_gain, routes, route_weight, experts)
+
+    column, beside = {0: block}, {}
+    column[1] = along(block, 1, experts)
+    beside[0] = across(block, n_dev)
+    column[2] = along(block, 2, experts)
+    w_in, w_out, w_out_other = load([w_in, w_out, others[1]], [in_vmem(others[0]), in_vmem(beside[0])])
+    weights = [w_in, others[0], w_out, w_out_other]
+    column[1] = pass_after(column[1], w_in)
+    beside[1] = across(column[1], n_dev)
+    column[3] = along(column[2], 1, experts)
+    beside[2] = across(column[2], n_dev)
+    beside[3] = across(column[3], n_dev)
+
+    own, give = {}, {}
+    own[0], give[0], own[1], give[1] = expert(
+        [block, beside[0], column[1], beside[1]], weights, experts, []
+    )
+    back_own, back_give = along(own[1], 1, experts), along(give[1], 1, experts)
+    own[2], give[2] = expert([column[2], beside[2]], weights, experts, [own[0]])
+    own[3], give[3] = expert([column[3], beside[3]], weights, experts, [own[2], back_give])
+
+    result = lax.dynamic_index_in_dim(hidden, core, 0, keepdims=False).astype(jnp.float32)
+    result = result + own[0].astype(jnp.float32) + back_own.astype(jnp.float32)
+    for k in (2, 3):
+        total = own[k].astype(jnp.float32) + across(give[k], n_dev).astype(jnp.float32)
+        result = result + along(total.astype(jnp.bfloat16), k, experts).astype(jnp.float32)
+    passed_on = give[0].astype(jnp.float32) + back_give.astype(jnp.float32)
+    passed_on = across(passed_on.astype(jnp.bfloat16), n_dev)
+    result = (result + passed_on.astype(jnp.float32)).astype(jnp.bfloat16)
+
+    half = width // 2
+    kept = lax.dynamic_slice_in_dim(result, core * half, half, 1)
+    passed = swap_cores(lax.dynamic_slice_in_dim(result, (1 - core) * half, half, 1))
+    first = core == 0
+    return jnp.stack([jnp.where(first, kept, passed), jnp.where(first, passed, kept)])
+
+
+def local(hidden, norm_gain, routes, route_weight, w_in, w_out):
+    batches, rows, _ = hidden.shape
+    n_dev = lax.axis_size("dev")
+    cap = max(2, 2 * rows * routes.shape[2] // (n_dev // 2))
+    if cap >= rows and n_dev == 8 and batches == lax.axis_size("sub") == 2:
+        return whole_blocks(hidden, norm_gain, routes, route_weight, w_in, w_out)
+    return packed_blocks(hidden, norm_gain, routes, route_weight, w_in, w_out)
+
+
 def solution(mesh):
     placed = (
         P(None, ("groups", "dev"), None),

time: 222 us -> 60 us (0.27)
  waiting for transfers between devices: 161 us -> 31.8 us
  matrix products: 19.7 us -> 0 us
  between operations: 13.5 us -> 0.1 us
  Pallas kernels: 0 us -> 7.99 us
  other arithmetic: 5.56 us -> 1.1 us
    all_to_all x4 -> x0, waiting for transfers between devices: 154 us -> none  [the longest x2 77.6 us: dispatch(): lax.all_to_all(buffer, 'dev', split_axis=0, concat_axis=0, tiled=True)]
    ppermute x0 -> x17, waiting for transfers between devices: none -> 31.8 us  [the longest x7 18.1 us: across(): return lax.ppermute(value, 'dev', [(i, i ^ 1) for i in range(n_dev)])]
    all_to_all x4 -> x0, starting transfers between devices: 20.3 us -> none  [the longest x2 11.6 us: dispatch(): lax.all_to_all(buffer, 'dev', split_axis=0, concat_axis=0, tiled=True)]
    dot_general x6 -> x0, matrix products: 19.7 us -> none  [the longest x2 10.9 us: run_expert(): jnp.dot(act, w_out, preferred_element_type=jnp.float32).astype(jnp.bfloat16)]
    ppermute x0 -> x17, starting transfers between devices: none -> 18.9 us  [the longest x7 10.1 us: along(): return lax.ppermute(value, 'dev', pairs)]
    pallas_call x0 -> x6, Pallas kernels: none -> 7.99 us  [the longest x3 4.23 us: expert(): pl.pallas_call(functools.partial(expert_kernel, count, experts), in_specs...]
    reduce_scatter x1 -> x0, waiting for transfers between devices: 6.98 us -> none  [local(): lax.psum_scatter(jnp.stack(terms).astype(jnp.bfloat16), 'sub', scatter_di...]
    convert_element_type x3 -> x4, other arithmetic: 2.95 us -> 0.35 us  [the longest x1 0.18 us: whole_blocks(): result = (result + passed_on.astype(jnp.float32)).astype(jnp.bfloat16)]
  transfers between devices with their start and end apart: 5 -> 17, of which waited for: 5 -> 11; matrix products, arithmetic and copies ran while one was open for 7% -> 0% of each run, Pallas kernels for 0% -> 13%
where the time goes in v2:
time: 60 us; the launch traced here: 59.9 us
  waiting for transfers between devices  31.8 us (53%)
  starting transfers between devices  18.9 us (31%)
  Pallas kernels  7.99 us (13%)
  other arithmetic  1.1 us (2%)
    ppermute x7, waiting for transfers between devices, across(): return lax.ppermute(value, 'dev', [(i, i ^ 1) for i in range(n_dev)])  18.1 us
    ppermute x7, waiting for transfers between devices, along(): return lax.ppermute(value, 'dev', pairs)  12.3 us
    ppermute x7, starting transfers between devices, along(): return lax.ppermute(value, 'dev', pairs)  10.1 us
    ppermute x7, starting transfers between devices, across(): return lax.ppermute(value, 'dev', [(i, i ^ 1) for i in range(n_dev)])  8.15 us
    pallas_call x3, Pallas kernels, expert(): pl.pallas_call(functools.partial(expert_kernel, count, experts), in_specs...  4.23 us
    pallas_call x1, Pallas kernels, load(): pl.pallas_call(functools.partial(load_kernel, count), in_specs=[pl.BlockS...  2.63 us
    ppermute x3, waiting for transfers between devices, swap_cores(): return lax.ppermute(value, 'sub', [(0, 1), (1, 0)])  1.31 us
  transfers between devices with their start and end apart: 17, of which 11 were waited for; matrix products, arithmetic and copies ran while one was open for 0% of the time, Pallas kernels for 13%

profile of v2, /device:TPU:0, one launch (start us, length us, event | category | flops | bytes accessed | tf_op | source)
XLA Modules:
  0.0 59.9 jit_solution(8689794410542436640)
XLA Ops:
  0.0 0.5 collective-permute-start.3
  0.5 1.1 %shard_map.64.refs_0_ = bf16[32,3712]{1,0:T(8,128)(2,1)S(1)} custom-call(s32[1]{0:T(128)} %bitcast.1.core_ref, bf16[2,32,3584]{2,1,0:T(8,128)(2,1)} %hidden_ref.1, f32[3584]{0:T(1024)} %gain_ref.1, s32[2,2,32]{2,1,0:T(2,128)} %bitcast.10, f32[2,2,32]{2,1,0:T(2,128)} %bitcast.11), custom_call_target="tpu_custom_call" | custom-call | tf_op jit(solution)/shard_map/pallas_call | solution.py:134
  1.6 3.0 %collective-permute-start = (bf16[32,3712]{1,0:T(8,128)(2,1)S(1)}, bf16[32,3712]{1,0:T(8,128)(2,1)S(1)}, u32[]{:S(2)}, u32[]{:S(2)}) collective-permute-start(bf16[32,3712]{1,0:T(8,128)(2,1)S(1)} %shard_map.64.refs_0_), channel_id=1, source_target_pairs={{0,2},{2,0},{4,6},{6,4},{8,10},{10,8},{12,14},{14,12},{1,3},{3,1},... | collective-permute-start | bytes 712712 | tf_op jit(solution)/shard_map/ppermute | solution.py:103
  4.7 1.6 %collective-permute-start.1 = (bf16[32,3712]{1,0:T(8,128)(2,1)S(1)}, bf16[32,3712]{1,0:T(8,128)(2,1)S(1)}, u32[]{:S(2)}, u32[]{:S(2)}) collective-permute-start(bf16[32,3712]{1,0:T(8,128)(2,1)S(1)} %shard_map.64.refs_0_), channel_id=1, source_target_pairs={{0,4},{2,6},{4,0},{6,2},{8,12},{10,14},{12,8},{14,10},{1,5},{3,7},... | collective-permute-start | bytes 712712 | tf_op jit(solution)/shard_map/ppermute | solution.py:99
  6.2 2.6 %collective-permute-start.6 = (bf16[32,3712]{1,0:T(8,128)(2,1)S(1)}, bf16[32,3712]{1,0:T(8,128)(2,1)S(1)}, u32[]{:S(2)}, u32[]{:S(2)}) collective-permute-start(bf16[32,3712]{1,0:T(8,128)(2,1)S(1)} %shard_map.64.refs_0_), channel_id=1, source_target_pairs={{0,8},{2,10},{4,12},{6,14},{8,0},{10,2},{12,4},{14,6},{1,9},{3,11}... | collective-permute-start | bytes 712712 | tf_op jit(solution)/shard_map/ppermute | solution.py:99
  8.8 1.8 %collective-permute-done.refs_4_.refs_1_ = bf16[32,3712]{1,0:T(8,128)(2,1)S(1)} collective-permute-done((bf16[32,3712]{1,0:T(8,128)(2,1)S(1)}, bf16[32,3712]{1,0:T(8,128)(2,1)S(1)}, u32[]{:S(2)}, u32[]{:S(2)}) %collective-permute-start) | collective-permute-done | bytes 237600 | tf_op jit(solution)/shard_map/ppermute | solution.py:103
  10.6 2.6 %shard_map.65 = (bf16[3584,256]{1,0:T(8,128)(2,1)S(1)}, bf16[256,3584]{1,0:T(8,128)(2,1)S(1)}, bf16[256,3584]{1,0:T(8,128)(2,1)S(1)}) custom-call(bf16[3584,256]{1,0:T(8,128)(2,1)} %refs_0_.1, bf16[256,3584]{1,0:T(8,128)(2,1)} %refs_1_.1, bf16[256,3584]{1,0:T(8,128)(2,1)} %collective-permute-done.2.refs_2_, ...), custom_call_target="tpu_custom_call" | custom-call | tf_op jit(solution)/shard_map/pallas_call | solution.py:173
  13.2 3.8 %collective-permute-done.1.value_ref = bf16[32,3712]{1,0:T(8,128)(2,1)S(1)} collective-permute-done((bf16[32,3712]{1,0:T(8,128)(2,1)S(1)}, bf16[32,3712]{1,0:T(8,128)(2,1)S(1)}, u32[]{:S(2)}, u32[]{:S(2)}) %collective-permute-start.1) | collective-permute-done | bytes 237600 | tf_op jit(solution)/shard_map/ppermute | solution.py:99
  17.0 0.4 collective-permute-start.4
  17.4 2.0 %collective-permute-done.6.refs_0_ = bf16[32,3712]{1,0:T(8,128)(2,1)S(1)} collective-permute-done((bf16[32,3712]{1,0:T(8,128)(2,1)S(1)}, bf16[32,3712]{1,0:T(8,128)(2,1)S(1)}, u32[]{:S(2)}, u32[]{:S(2)}) %collective-permute-start.6) | collective-permute-done | bytes 237600 | tf_op jit(solution)/shard_map/ppermute | solution.py:99
  19.4 0.5 collective-permute-start.7
  19.9 0.4 collective-permute-start.10
  20.4 5.4 %collective-permute-done.4.refs_3_ = bf16[32,3712]{1,0:T(8,128)(2,1)S(1)} collective-permute-done((bf16[32,3712]{1,0:T(8,128)(2,1)S(1)}, bf16[32,3712]{1,0:T(8,128)(2,1)S(1)}, u32[]{:S(2)}, u32[]{:S(2)}) %collective-permute-start.4) | collective-permute-done | bytes 237600 | tf_op jit(solution)/shard_map/ppermute | solution.py:103
  25.8 1.4 %shard_map.67 = (bf16[32,3584]{1,0:T(8,128)(2,1)S(1)}, bf16[32,3584]{1,0:T(8,128)(2,1)S(1)}, bf16[32,3584]{1,0:T(8,128)(2,1)S(1)}, bf16[32,3584]{1,0:T(8,128)(2,1)S(1)}) custom-call(bf16[32,3712]{1,0:T(8,128)(2,1)S(1)} %shard_map.64.refs_0_, bf16[32,3712]{1,0:T(8,128)(2,1)S(1)} %collective-permute-done.refs_4_.refs_1_, ...), custom_call_target="tpu_custom_call" | custom-call | tf_op jit(solution)/shard_map/pallas_call | solution.py:216
  27.1 1.5 %collective-permute-done.7.refs_1_ = bf16[32,3712]{1,0:T(8,128)(2,1)S(1)} collective-permute-done((bf16[32,3712]{1,0:T(8,128)(2,1)S(1)}, bf16[32,3712]{1,0:T(8,128)(2,1)S(1)}, u32[]{:S(2)}, u32[]{:S(2)}) %collective-permute-start.7) | collective-permute-done | bytes 237600 | tf_op jit(solution)/shard_map/ppermute | solution.py:103
  28.6 1.4 %shard_map.68 = (bf16[32,3584]{1,0:T(8,128)(2,1)S(1)}, bf16[32,3584]{1,0:T(8,128)(2,1)S(1)}) custom-call(bf16[32,3712]{1,0:T(8,128)(2,1)S(1)} %collective-permute-done.6.refs_0_, bf16[32,3712]{1,0:T(8,128)(2,1)S(1)} %collective-permute-done.7.refs_1_, bf16[3584,256]{1,0:T(8,128)(2,1)S(1)} %get-tuple-element.16.after_ref.refs_4_.refs_2_, ...), custom_call_target="tpu_custom_call" | custom-call | tf_op jit(solution)/shard_map/pallas_call | solution.py:216
  30.1 0.7 %collective-permute-start.8 = (bf16[32,3584]{1,0:T(8,128)(2,1)S(1)}, bf16[32,3584]{1,0:T(8,128)(2,1)S(1)}, u32[]{:S(2)}, u32[]{:S(2)}) collective-permute-start(bf16[32,3584]{1,0:T(8,128)(2,1)S(1)} %get-tuple-element.22), channel_id=1, source_target_pairs={{0,2},{2,0},{4,6},{6,4},{8,10},{10,8},{12,14},{14,12},{1,3},{3,1},... | collective-permute-start | bytes 688136 | tf_op jit(solution)/shard_map/ppermute | solution.py:103
  30.8 1.3 %collective-permute-start.11 = (bf16[32,3712]{1,0:T(8,128)(2,1)S(1)}, bf16[32,3712]{1,0:T(8,128)(2,1)S(1)}, u32[]{:S(2)}, u32[]{:S(2)}) collective-permute-start(bf16[32,3712]{1,0:T(8,128)(2,1)S(1)} %collective-permute-done.10.refs_0_), channel_id=1, source_target_pairs={{0,2},{2,0},{4,6},{6,4},{8,10},{10,8},{12,14},{14,12},{1,3},{3,1},... | collective-permute-start | bytes 712712 | tf_op jit(solution)/shard_map/ppermute | solution.py:103
  32.2 2.0 %collective-permute-start.5 = (bf16[32,3584]{1,0:T(8,128)(2,1)S(1)}, bf16[32,3584]{1,0:T(8,128)(2,1)S(1)}, u32[]{:S(2)}, u32[]{:S(2)}) collective-permute-start(bf16[32,3584]{1,0:T(8,128)(2,1)S(1)} %get-tuple-element.20), channel_id=1, source_target_pairs={{0,4},{2,6},{4,0},{6,2},{8,12},{10,14},{12,8},{14,10},{1,5},{3,7},... | collective-permute-start | bytes 688136 | tf_op jit(solution)/shard_map/ppermute | solution.py:99
  34.2 3.9 %collective-permute-done.8 = bf16[32,3584]{1,0:T(8,128)(2,1)S(1)} collective-permute-done((bf16[32,3584]{1,0:T(8,128)(2,1)S(1)}, bf16[32,3584]{1,0:T(8,128)(2,1)S(1)}, u32[]{:S(2)}, u32[]{:S(2)}) %collective-permute-start.8) | collective-permute-done | bytes 229408 | tf_op jit(solution)/shard_map/ppermute | solution.py:103
  38.2 0.8 %collective-permute-start.9 = (bf16[32,3584]{1,0:T(8,128)(2,1)S(1)}, bf16[32,3584]{1,0:T(8,128)(2,1)S(1)}, u32[]{:S(2)}, u32[]{:S(2)}) collective-permute-start(bf16[32,3584]{1,0:T(8,128)(2,1)S(1)} %add_convert_fusion.2), channel_id=1, source_target_pairs={{0,8},{2,10},{4,12},{6,14},{8,0},{10,2},{12,4},{14,6},{1,9},{3,11}... | collective-permute-start | bytes 688136 | tf_op jit(solution)/shard_map/ppermute | solution.py:99
  39.0 1.7 %collective-permute-done.11.refs_1_ = bf16[32,3712]{1,0:T(8,128)(2,1)S(1)} collective-permute-done((bf16[32,3712]{1,0:T(8,128)(2,1)S(1)}, bf16[32,3712]{1,0:T(8,128)(2,1)S(1)}, u32[]{:S(2)}, u32[]{:S(2)}) %collective-permute-start.11) | collective-permute-done | bytes 237600 | tf_op jit(solution)/shard_map/ppermute | solution.py:103
  40.7 1.3 %collective-permute-done.12.refs_7_ = bf16[32,3584]{1,0:T(8,128)(2,1)S(1)} collective-permute-done((bf16[32,3584]{1,0:T(8,128)(2,1)S(1)}, bf16[32,3584]{1,0:T(8,128)(2,1)S(1)}, u32[]{:S(2)}, u32[]{:S(2)}) %collective-permute-start.12) | collective-permute-done | bytes 229408 | tf_op jit(solution)/shard_map/ppermute | solution.py:99
  42.0 1.4 %shard_map.69 = (bf16[32,3584]{1,0:T(8,128)(2,1)S(1)}, bf16[32,3584]{1,0:T(8,128)(2,1)S(1)}) custom-call(bf16[32,3712]{1,0:T(8,128)(2,1)S(1)} %collective-permute-done.10.refs_0_, bf16[32,3712]{1,0:T(8,128)(2,1)S(1)} %collective-permute-done.11.refs_1_, bf16[3584,256]{1,0:T(8,128)(2,1)S(1)} %get-tuple-element.16.after_ref.refs_4_.refs_2_, ...), custom_call_target="tpu_custom_call" | custom-call | tf_op jit(solution)/shard_map/pallas_call | solution.py:216
  43.4 1.1 %collective-permute-start.13 = (bf16[32,3584]{1,0:T(8,128)(2,1)S(1)}, bf16[32,3584]{1,0:T(8,128)(2,1)S(1)}, u32[]{:S(2)}, u32[]{:S(2)}) collective-permute-start(bf16[32,3584]{1,0:T(8,128)(2,1)S(1)} %get-tuple-element.25), channel_id=1, source_target_pairs={{0,2},{2,0},{4,6},{6,4},{8,10},{10,8},{12,14},{14,12},{1,3},{3,1},... | collective-permute-start | bytes 688136 | tf_op jit(solution)/shard_map/ppermute | solution.py:103
  44.5 1.1 %collective-permute-start.15 = (bf16[32,3584]{1,0:T(8,128)(2,1)S(1)}, bf16[32,3584]{1,0:T(8,128)(2,1)S(1)}, u32[]{:S(2)}, u32[]{:S(2)}) collective-permute-start(bf16[32,3584]{1,0:T(8,128)(2,1)S(1)} %add_convert_fusion), channel_id=1, source_target_pairs={{0,2},{2,0},{4,6},{6,4},{8,10},{10,8},{12,14},{14,12},{1,3},{3,1},... | collective-permute-start | bytes 688136 | tf_op jit(solution)/shard_map/ppermute | solution.py:103
  45.6 3.9 %collective-permute-done.13 = bf16[32,3584]{1,0:T(8,128)(2,1)S(1)} collective-permute-done((bf16[32,3584]{1,0:T(8,128)(2,1)S(1)}, bf16[32,3584]{1,0:T(8,128)(2,1)S(1)}, u32[]{:S(2)}, u32[]{:S(2)}) %collective-permute-start.13) | collective-permute-done | bytes 229408 | tf_op jit(solution)/shard_map/ppermute | solution.py:103
  49.5 2.7 %collective-permute-start.14 = (bf16[32,3584]{1,0:T(8,128)(2,1)S(1)}, bf16[32,3584]{1,0:T(8,128)(2,1)S(1)}, u32[]{:S(2)}, u32[]{:S(2)}) collective-permute-start(bf16[32,3584]{1,0:T(8,128)(2,1)S(1)} %add_convert_fusion.1), channel_id=1, source_target_pairs={{0,12},{2,14},{4,8},{6,10},{8,4},{10,6},{12,0},{14,2},{1,13},{3,15... | collective-permute-start | bytes 688136 | tf_op jit(solution)/shard_map/ppermute | solution.py:99
  52.3 5.3 %collective-permute-done.14 = bf16[32,3584]{1,0:T(8,128)(2,1)S(1)} collective-permute-done((bf16[32,3584]{1,0:T(8,128)(2,1)S(1)}, bf16[32,3584]{1,0:T(8,128)(2,1)S(1)}, u32[]{:S(2)}, u32[]{:S(2)}) %collective-permute-start.14) | collective-permute-done | bytes 229408 | tf_op jit(solution)/shard_map/ppermute | solution.py:99
  57.5 0.2 fusion.4
  57.8 1.3 %collective-permute-done.16 = bf16[32,1792]{1,0:T(8,128)(2,1)S(1)} collective-permute-done((bf16[32,1792]{1,0:T(8,128)(2,1)S(1)}, bf16[32,1792]{1,0:T(8,128)(2,1)S(1)}, u32[]{:S(2)}, u32[]{:S(2)}) %collective-permute-start.16) | collective-permute-done | bytes 114720 | tf_op jit(solution)/shard_map/ppermute | solution.py:94
  59.2 0.7 %pad_maximum_fusion = bf16[2,32,1792]{2,1,0:T(8,128)(2,1)} fusion(bf16[1,32,1792]{2,1,0:T(8,128)(2,1)S(1)} %get-tuple-element.28, bf16[1,32,1792]{2,1,0:T(8,128)(2,1)S(1)} %get-tuple-element.27), kind=kLoop, calls=%fused_computation.9 | loop fusion | flops 114688 | bytes 458752 | tf_op jit(solution)/shard_map/stack | solution.py:278
  (17 shorter events, 0.4 us)
Async XLA Ops:
  0.0 10.6 %collective-permute-start.3 = (bf16[3584,256]{1,0:T(8,128)(2,1)}, bf16[3584,256]{1,0:T(8,128)(2,1)S(1)}, u32[]{:S(2)}, u32[]{:S(2)}) collective-permute-start(bf16[3584,256]{1,0:T(8,128)(2,1)} %refs_0_.1), channel_id=1, source_target_pairs={{0,1},{1,0},{2,3},{3,2},{4,5},{5,4},{6,7},{7,6},{8,9},{9,8},{10,11... | collective-permute-start | bytes 5505032 | tf_op jit(solution)/shard_map/ppermute | solution.py:94
  0.5 10.1 %collective-permute-start.2 = (bf16[256,3584]{1,0:T(8,128)(2,1)}, bf16[256,3584]{1,0:T(8,128)(2,1)}, u32[]{:S(2)}, u32[]{:S(2)}) collective-permute-start(bf16[256,3584]{1,0:T(8,128)(2,1)} %refs_1_.1), channel_id=1, source_target_pairs={{0,1},{1,0},{2,3},{3,2},{4,5},{5,4},{6,7},{7,6},{8,9},{9,8},{10,11... | collective-permute-start | bytes 5505032 | tf_op jit(solution)/shard_map/ppermute | solution.py:94
  1.6 9.0 %collective-permute-start = (bf16[32,3712]{1,0:T(8,128)(2,1)S(1)}, bf16[32,3712]{1,0:T(8,128)(2,1)S(1)}, u32[]{:S(2)}, u32[]{:S(2)}) collective-permute-start(bf16[32,3712]{1,0:T(8,128)(2,1)S(1)} %shard_map.64.refs_0_), channel_id=1, source_target_pairs={{0,2},{2,0},{4,6},{6,4},{8,10},{10,8},{12,14},{14,12},{1,3},{3,1},... | collective-permute-start | bytes 712712 | tf_op jit(solution)/shard_map/ppermute | solution.py:103
  4.7 12.4 %collective-permute-start.1 = (bf16[32,3712]{1,0:T(8,128)(2,1)S(1)}, bf16[32,3712]{1,0:T(8,128)(2,1)S(1)}, u32[]{:S(2)}, u32[]{:S(2)}) collective-permute-start(bf16[32,3712]{1,0:T(8,128)(2,1)S(1)} %shard_map.64.refs_0_), channel_id=1, source_target_pairs={{0,4},{2,6},{4,0},{6,2},{8,12},{10,14},{12,8},{14,10},{1,5},{3,7},... | collective-permute-start | bytes 712712 | tf_op jit(solution)/shard_map/ppermute | solution.py:99
  6.2 13.2 %collective-permute-start.6 = (bf16[32,3712]{1,0:T(8,128)(2,1)S(1)}, bf16[32,3712]{1,0:T(8,128)(2,1)S(1)}, u32[]{:S(2)}, u32[]{:S(2)}) collective-permute-start(bf16[32,3712]{1,0:T(8,128)(2,1)S(1)} %shard_map.64.refs_0_), channel_id=1, source_target_pairs={{0,8},{2,10},{4,12},{6,14},{8,0},{10,2},{12,4},{14,6},{1,9},{3,11}... | collective-permute-start | bytes 712712 | tf_op jit(solution)/shard_map/ppermute | solution.py:99
  17.0 8.7 %collective-permute-start.4 = (bf16[32,3712]{1,0:T(8,128)(2,1)S(1)}, bf16[32,3712]{1,0:T(8,128)(2,1)S(1)}, u32[]{:S(2)}, u32[]{:S(2)}) collective-permute-start(bf16[32,3712]{1,0:T(8,128)(2,1)S(1)} %shard_map.66.refs_2_), channel_id=1, source_target_pairs={{0,2},{2,0},{4,6},{6,4},{8,10},{10,8},{12,14},{14,12},{1,3},{3,1},... | collective-permute-start | bytes 712712 | tf_op jit(solution)/shard_map/ppermute | solution.py:103
  19.4 9.2 %collective-permute-start.7 = (bf16[32,3712]{1,0:T(8,128)(2,1)S(1)}, bf16[32,3712]{1,0:T(8,128)(2,1)S(1)}, u32[]{:S(2)}, u32[]{:S(2)}) collective-permute-start(bf16[32,3712]{1,0:T(8,128)(2,1)S(1)} %collective-permute-done.6.refs_0_), channel_id=1, source_target_pairs={{0,2},{2,0},{4,6},{6,4},{8,10},{10,8},{12,14},{14,12},{1,3},{3,1},... | collective-permute-start | bytes 712712 | tf_op jit(solution)/shard_map/ppermute | solution.py:103
  19.9 10.9 %collective-permute-start.10 = (bf16[32,3712]{1,0:T(8,128)(2,1)S(1)}, bf16[32,3712]{1,0:T(8,128)(2,1)S(1)}, u32[]{:S(2)}, u32[]{:S(2)}) collective-permute-start(bf16[32,3712]{1,0:T(8,128)(2,1)S(1)} %collective-permute-done.6.refs_0_), channel_id=1, source_target_pairs={{0,4},{2,6},{4,0},{6,2},{8,12},{10,14},{12,8},{14,10},{1,5},{3,7},... | collective-permute-start | bytes 712712 | tf_op jit(solution)/shard_map/ppermute | solution.py:99
  30.1 8.0 %collective-permute-start.8 = (bf16[32,3584]{1,0:T(8,128)(2,1)S(1)}, bf16[32,3584]{1,0:T(8,128)(2,1)S(1)}, u32[]{:S(2)}, u32[]{:S(2)}) collective-permute-start(bf16[32,3584]{1,0:T(8,128)(2,1)S(1)} %get-tuple-element.22), channel_id=1, source_target_pairs={{0,2},{2,0},{4,6},{6,4},{8,10},{10,8},{12,14},{14,12},{1,3},{3,1},... | collective-permute-start | bytes 688136 | tf_op jit(solution)/shard_map/ppermute | solution.py:103
  30.8 9.8 %collective-permute-start.11 = (bf16[32,3712]{1,0:T(8,128)(2,1)S(1)}, bf16[32,3712]{1,0:T(8,128)(2,1)S(1)}, u32[]{:S(2)}, u32[]{:S(2)}) collective-permute-start(bf16[32,3712]{1,0:T(8,128)(2,1)S(1)} %collective-permute-done.10.refs_0_), channel_id=1, source_target_pairs={{0,2},{2,0},{4,6},{6,4},{8,10},{10,8},{12,14},{14,12},{1,3},{3,1},... | collective-permute-start | bytes 712712 | tf_op jit(solution)/shard_map/ppermute | solution.py:103
  32.2 9.8 %collective-permute-start.12 = (bf16[32,3584]{1,0:T(8,128)(2,1)S(1)}, bf16[32,3584]{1,0:T(8,128)(2,1)S(1)}, u32[]{:S(2)}, u32[]{:S(2)}) collective-permute-start(bf16[32,3584]{1,0:T(8,128)(2,1)S(1)} %get-tuple-element.23), channel_id=1, source_target_pairs={{0,4},{2,6},{4,0},{6,2},{8,12},{10,14},{12,8},{14,10},{1,5},{3,7},... | collective-permute-start | bytes 688136 | tf_op jit(solution)/shard_map/ppermute | solution.py:99
  32.2 20.1 %collective-permute-start.5 = (bf16[32,3584]{1,0:T(8,128)(2,1)S(1)}, bf16[32,3584]{1,0:T(8,128)(2,1)S(1)}, u32[]{:S(2)}, u32[]{:S(2)}) collective-permute-start(bf16[32,3584]{1,0:T(8,128)(2,1)S(1)} %get-tuple-element.20), channel_id=1, source_target_pairs={{0,4},{2,6},{4,0},{6,2},{8,12},{10,14},{12,8},{14,10},{1,5},{3,7},... | collective-permute-start | bytes 688136 | tf_op jit(solution)/shard_map/ppermute | solution.py:99
  38.2 19.3 %copy-start = (bf16[2,32,3584]{2,1,0:T(8,128)(2,1)S(1)}, bf16[2,32,3584]{2,1,0:T(8,128)(2,1)}, u32[]{:S(2)}) copy-start(bf16[2,32,3584]{2,1,0:T(8,128)(2,1)} %hidden_ref.1) | copy-start | bytes 1376260
  38.2 14.1 %collective-permute-start.9 = (bf16[32,3584]{1,0:T(8,128)(2,1)S(1)}, bf16[32,3584]{1,0:T(8,128)(2,1)S(1)}, u32[]{:S(2)}, u32[]{:S(2)}) collective-permute-start(bf16[32,3584]{1,0:T(8,128)(2,1)S(1)} %add_convert_fusion.2), channel_id=1, source_target_pairs={{0,8},{2,10},{4,12},{6,14},{8,0},{10,2},{12,4},{14,6},{1,9},{3,11}... | collective-permute-start | bytes 688136 | tf_op jit(solution)/shard_map/ppermute | solution.py:99
  43.4 6.1 %collective-permute-start.13 = (bf16[32,3584]{1,0:T(8,128)(2,1)S(1)}, bf16[32,3584]{1,0:T(8,128)(2,1)S(1)}, u32[]{:S(2)}, u32[]{:S(2)}) collective-permute-start(bf16[32,3584]{1,0:T(8,128)(2,1)S(1)} %get-tuple-element.25), channel_id=1, source_target_pairs={{0,2},{2,0},{4,6},{6,4},{8,10},{10,8},{12,14},{14,12},{1,3},{3,1},... | collective-permute-start | bytes 688136 | tf_op jit(solution)/shard_map/ppermute | solution.py:103
  44.5 7.7 %collective-permute-start.15 = (bf16[32,3584]{1,0:T(8,128)(2,1)S(1)}, bf16[32,3584]{1,0:T(8,128)(2,1)S(1)}, u32[]{:S(2)}, u32[]{:S(2)}) collective-permute-start(bf16[32,3584]{1,0:T(8,128)(2,1)S(1)} %add_convert_fusion), channel_id=1, source_target_pairs={{0,2},{2,0},{4,6},{6,4},{8,10},{10,8},{12,14},{14,12},{1,3},{3,1},... | collective-permute-start | bytes 688136 | tf_op jit(solution)/shard_map/ppermute | solution.py:103
  49.5 8.0 %collective-permute-start.14 = (bf16[32,3584]{1,0:T(8,128)(2,1)S(1)}, bf16[32,3584]{1,0:T(8,128)(2,1)S(1)}, u32[]{:S(2)}, u32[]{:S(2)}) collective-permute-start(bf16[32,3584]{1,0:T(8,128)(2,1)S(1)} %add_convert_fusion.1), channel_id=1, source_target_pairs={{0,12},{2,14},{4,8},{6,10},{8,4},{10,6},{12,0},{14,2},{1,13},{3,15... | collective-permute-start | bytes 688136 | tf_op jit(solution)/shard_map/ppermute | solution.py:99
  57.7 1.4 %collective-permute-start.16 = (bf16[32,1792]{1,0:T(8,128)(2,1)S(1)}, bf16[32,1792]{1,0:T(8,128)(2,1)S(1)}, u32[]{:S(2)}, u32[]{:S(2)}) collective-permute-start(bf16[32,1792]{1,0:T(8,128)(2,1)S(1)} %constant_dynamic-slice_fusion), channel_id=1, source_target_pairs={{0,1},{1,0},{2,3},{3,2},{4,5},{5,4},{6,7},{7,6},{8,9},{9,8},{10,11... | collective-permute-start | bytes 344072 | tf_op jit(solution)/shard_map/ppermute | solution.py:94

commit v3 on v2

--- a/solution.py
+++ b/solution.py
@@ -9,8 +9,8 @@
 
 EPS = 1e-06
 LANES = 128
-VMEM_BYTES = 24 << 20
-LITTLE = pl.CostEstimate(flops=1, bytes_accessed=1, transcendentals=0)
+TOKEN = (8, LANES)
+VMEM_BYTES = 16 << 20
 
 
 def route_tables(routes_now, weight_now, n_dev, cap, span):
@@ -90,6 +90,14 @@
     return layer_out
 
 
+def in_vmem(value):
+    return pltpu.with_memory_space_constraint(value, pltpu.VMEM)
+
+
+def in_hbm(value):
+    return pltpu.with_memory_space_constraint(value, pltpu.HBM)
+
+
 def swap_cores(value):
     return lax.ppermute(value, "sub", [(0, 1), (1, 0)])
 
@@ -99,16 +107,42 @@
     return lax.ppermute(value, "dev", pairs)
 
 
+def along_to_core(value, step, experts, other):
+    pairs = [
+        (4 * z + 2 * x + s, 4 * (z ^ step) + 2 * x + (s ^ other))
+        for z in range(experts)
+        for x in range(2)
+        for s in range(2)
+    ]
+    return lax.ppermute(value, ("dev", "sub"), pairs)
+
+
 def across(value, n_dev):
     return lax.ppermute(value, "dev", [(i, i ^ 1) for i in range(n_dev)])
 
 
-def in_vmem(value):
-    return pltpu.with_memory_space_constraint(value, pltpu.VMEM)
-
-
-def in_hbm(value):
-    return pltpu.with_memory_space_constraint(value, pltpu.HBM)
+def kernel_call(kernel, operands, outs, after=(), hbm=0, scratch=()):
+    vmem = pl.BlockSpec(memory_space=pltpu.VMEM)
+    kept = [pl.BlockSpec(memory_space=pltpu.HBM)] * hbm + [vmem] * (len(operands) - hbm)
+    count = len(operands)
+
+    def body(*refs):
+        kernel(*refs[:count], *refs[count + len(after) : count + len(after) + len(outs)], *refs[count + len(after) + len(outs) + 1 :])
+        refs[count + len(after) + len(outs)][...] = jnp.zeros(TOKEN, jnp.float32)
+
+    *given, token = pl.pallas_call(
+        body,
+        in_specs=kept + [pl.BlockSpec(memory_space=pl.ANY)] * len(after),
+        out_specs=[vmem] * (len(outs) + 1),
+        out_shape=[pltpu.VMEM(shape, dtype) for shape, dtype in [*outs, (TOKEN, jnp.float32)]],
+        scratch_shapes=scratch,
+        compiler_params=pltpu.CompilerParams(vmem_limit_bytes=VMEM_BYTES),
+    )(
+        *[in_hbm(v) for v in operands[:hbm]],
+        *[in_vmem(v) for v in operands[hbm:]],
+        *[in_vmem(v) for v in after],
+    )
+    return given, token
 
 
 def pack_kernel(experts, core_ref, hidden_ref, gain_ref, routes_ref, weight_ref, block_ref):
@@ -155,123 +189,157 @@
     )
 
 
-def load_kernel(count, *refs):
-    arrived = refs[-1]
-    sources, places = refs[:count], refs[-count - 1 : -1]
-    copies = [
-        pltpu.make_async_copy(source, place, arrived.at[i])
-        for i, (source, place) in enumerate(zip(sources, places))
-    ]
-    for copy in copies:
-        copy.start()
-    for copy in copies:
-        copy.wait()
-
-
 def load(arrays, after):
     count = len(arrays)
-    return pl.pallas_call(
-        functools.partial(load_kernel, count),
-        in_specs=[pl.BlockSpec(memory_space=pltpu.HBM)] * count
-        + [pl.BlockSpec(memory_space=pl.ANY)] * len(after),
-        out_specs=[pl.BlockSpec(memory_space=pltpu.VMEM)] * count,
-        out_shape=[pltpu.VMEM(a.shape, a.dtype) for a in arrays],
-        scratch_shapes=[pltpu.SemaphoreType.DMA((count,))],
-        compiler_params=pltpu.CompilerParams(vmem_limit_bytes=VMEM_BYTES),
-    )(*[in_hbm(a) for a in arrays], *after)
-
-
-def expert_kernel(count, experts, *refs):
-    blocks, refs = refs[:count], refs[count:]
-    in_refs, down_refs, out_refs = refs[:2], refs[2:4], refs[-count:]
-    rows, width = out_refs[0].shape
-    x = jnp.concatenate([block[...] for block in blocks], axis=0)
-    lane = lax.broadcasted_iota(jnp.int32, x.shape[:1] + (LANES,), 1)
-    mine = lax.axis_index("dev") // 2
-    keep = (lane == mine) | (lane == mine + experts)
-    scale = jnp.sum(
-        jnp.where(keep, x[:, width:].astype(jnp.float32), 0.0), axis=1, keepdims=True
-    )
-    x = x[:, :width]
-    acts = []
-    for ref in in_refs:
-        inner = jnp.dot(x, ref[...], preferred_element_type=jnp.float32)
-        acts.append((inner / (1.0 + jnp.exp(-inner))).astype(jnp.bfloat16))
-    step = width // 4
-    for start in range(0, width, step):
-        out = sum(
-            jnp.dot(act, ref[:, start : start + step], preferred_element_type=jnp.float32)
-            for act, ref in zip(acts, down_refs)
-        )
-        out = (out * scale).astype(jnp.bfloat16)
-        for i, ref in enumerate(out_refs):
-            ref[:, start : start + step] = out[i * rows : (i + 1) * rows]
+
+    def kernel(*refs):
+        arrived = refs[-1]
+        copies = [
+            pltpu.make_async_copy(source, place, arrived.at[i])
+            for i, (source, place) in enumerate(zip(refs[:count], refs[count:-1]))
+        ]
+        for copy in copies:
+            copy.start()
+        for copy in copies:
+            copy.wait()
+
+    outs = [(a.shape, a.dtype) for a in arrays]
+    return kernel_call(kernel, arrays, outs, after, count, [pltpu.SemaphoreType.DMA((count,))])
 
 
 def expert(blocks, weights, experts, after):
     count = len(blocks)
     rows, width = blocks[0].shape[0], weights[0].shape[0]
-    hidden_units = 2 * weights[0].shape[1]
-    whole = pl.BlockSpec(memory_space=pltpu.VMEM)
+
+    def kernel(*refs):
+        ups, downs, out_refs = refs[count : count + 2], refs[count + 2 : count + 4], refs[count + 4 :]
+        x = jnp.concatenate([block[...] for block in refs[:count]], axis=0)
+        lane = lax.broadcasted_iota(jnp.int32, (count * rows, LANES), 1)
+        mine = lax.axis_index("dev") // 2
+        keep = (lane == mine) | (lane == mine + experts)
+        gates = x[:, width:].astype(jnp.float32)
+        scale = jnp.sum(jnp.where(keep, gates, 0.0), axis=1, keepdims=True)
+        x = x[:, :width]
+        acts = []
+        for ref in ups:
+            inner = jnp.dot(x, ref[...], preferred_element_type=jnp.float32)
+            acts.append((inner / (1.0 + jnp.exp(-inner))).astype(jnp.bfloat16))
+        step = width // 4
+        for start in range(0, width, step):
+            out = sum(
+                jnp.dot(act, ref[:, start : start + step], preferred_element_type=jnp.float32)
+                for act, ref in zip(acts, downs)
+            )
+            out = (out * scale).astype(jnp.bfloat16)
+            for i, ref in enumerate(out_refs):
+                ref[:, start : start + step] = out[i * rows : (i + 1) * rows]
+
+    return kernel_call(
+        kernel, [*blocks, *weights], [((rows, width), jnp.bfloat16)] * count, after
+    )
+
+
+def add(terms, after=(), dtype=jnp.bfloat16):
+    def kernel(*refs):
+        total = refs[0][...].astype(jnp.float32)
+        for ref in refs[1:-1]:
+            total = total + ref[...].astype(jnp.float32)
+        refs[-1][...] = total.astype(dtype)
+
+    (total,), token = kernel_call(kernel, terms, [(terms[0].shape, dtype)], after)
+    return total, token
+
+
+def add_halves(terms, dtype, after=()):
+    rows, width = terms[0].shape
+    half = width // 2
+
+    def kernel(*refs):
+        core = lax.axis_index("sub")
+        for which, out_ref in ((core, refs[-2]), (1 - core, refs[-1])):
+            place = pl.ds(pl.multiple_of(which * half, LANES), half)
+            total = refs[0][:, place].astype(jnp.float32)
+            for ref in refs[1:-2]:
+                total = total + ref[:, place].astype(jnp.float32)
+            out_ref[...] = total.astype(dtype)
+
+    return kernel_call(kernel, terms, [((rows, half), dtype)] * 2, after)
+
+
+def finish(kept, passed):
+    def kernel(*refs):
+        core = lax.axis_index("sub")
+        out_ref = refs[-1]
+        for place, refs in ((core, refs[: len(kept)]), (1 - core, refs[len(kept) : -1])):
+            total = refs[0][...].astype(jnp.float32)
+            for ref in refs[1:]:
+                total = total + ref[...].astype(jnp.float32)
+            out_ref[place] = total.astype(jnp.bfloat16)
+
+    terms = [*kept, *passed]
+    vmem = pl.BlockSpec(memory_space=pltpu.VMEM)
     return pl.pallas_call(
-        functools.partial(expert_kernel, count, experts),
-        in_specs=[whole] * (count + 4) + [pl.BlockSpec(memory_space=pl.ANY)] * len(after),
-        out_specs=[whole] * count,
-        out_shape=[pltpu.VMEM((rows, width), jnp.bfloat16)] * count,
+        kernel,
+        in_specs=[vmem] * len(terms),
+        out_specs=vmem,
+        out_shape=jax.ShapeDtypeStruct((2, *kept[0].shape), jnp.bfloat16),
         compiler_params=pltpu.CompilerParams(vmem_limit_bytes=VMEM_BYTES),
-    )(*[in_vmem(v) for v in (*blocks, *weights)], *after)
+    )(*[in_vmem(v) for v in terms])
 
 
 def pass_after(value, after):
     place = pl.BlockSpec(memory_space=pl.ANY)
     return pl.pallas_call(
-        lambda value_ref, after_ref, out_ref: None,
-        in_specs=[place, place],
+        lambda *refs: None,
+        in_specs=[place] * (1 + len(after)),
         out_specs=place,
         out_shape=jax.ShapeDtypeStruct(value.shape, value.dtype),
         input_output_aliases={0: 0},
         compiler_params=pltpu.CompilerParams(vmem_limit_bytes=VMEM_BYTES),
-    )(in_vmem(value), in_vmem(after))
+    )(in_vmem(value), *[in_vmem(v) for v in after])
 
 
 def whole_blocks(hidden, norm_gain, routes, route_weight, w_in, w_out):
-    batches, rows, width = hidden.shape
     n_dev = lax.axis_size("dev")
     experts = n_dev // 2
     core = lax.axis_index("sub")
     others = [swap_cores(w_in), swap_cores(w_out)]
     block = pack(core, hidden, norm_gain, routes, route_weight, experts)
-
     column, beside = {0: block}, {}
-    column[1] = along(block, 1, experts)
     beside[0] = across(block, n_dev)
     column[2] = along(block, 2, experts)
-    w_in, w_out, w_out_other = load([w_in, w_out, others[1]], [in_vmem(others[0]), in_vmem(beside[0])])
+    column[1] = along(block, 1, experts)
+    (w_in, w_out, w_out_other), loaded = load([w_in, w_out, others[1]], [others[0], beside[0]])
     weights = [w_in, others[0], w_out, w_out_other]
-    column[1] = pass_after(column[1], w_in)
-    beside[1] = across(column[1], n_dev)
+    column[2] = pass_after(column[2], [loaded, column[1]])
     column[3] = along(column[2], 1, experts)
     beside[2] = across(column[2], n_dev)
     beside[3] = across(column[3], n_dev)
-
-    own, give = {}, {}
-    own[0], give[0], own[1], give[1] = expert(
-        [block, beside[0], column[1], beside[1]], weights, experts, []
+    again, _ = add([beside[0]], [column[3]])
+    beside[1] = along(again, 1, experts)
+
+    own, give, there = {}, {}, {}
+    (own[2], give[2]), token = expert([column[2], beside[2]], weights, experts, [column[3]])
+    there[2] = across(give[2], n_dev)
+    (own[0], give[0], own[1], give[1]), token = expert(
+        [block, beside[0], column[1], beside[1]], weights, experts, [token]
     )
     back_own, back_give = along(own[1], 1, experts), along(give[1], 1, experts)
-    own[2], give[2] = expert([column[2], beside[2]], weights, experts, [own[0]])
-    own[3], give[3] = expert([column[3], beside[3]], weights, experts, [own[2], back_give])
-
+    (own[3], give[3]), token = expert([column[3], beside[3]], weights, experts, [token])
+    there[3] = across(give[3], n_dev)
+    total, token = add([own[2], there[2]], [token])
+    from_2 = along(total, 2, experts)
+    total, token = add([own[3], there[3]], [token])
+    last = along(total, 3, experts)
+    total, _ = add([give[0], back_give], [token])
+    there[0] = across(total, n_dev)
+    partial, _ = add([own[0], back_own, from_2, last], [], jnp.float32)
+    rows, width = own[0].shape
+    half = width // 2
     result = lax.dynamic_index_in_dim(hidden, core, 0, keepdims=False).astype(jnp.float32)
-    result = result + own[0].astype(jnp.float32) + back_own.astype(jnp.float32)
-    for k in (2, 3):
-        total = own[k].astype(jnp.float32) + across(give[k], n_dev).astype(jnp.float32)
-        result = result + along(total.astype(jnp.bfloat16), k, experts).astype(jnp.float32)
-    passed_on = give[0].astype(jnp.float32) + back_give.astype(jnp.float32)
-    passed_on = across(passed_on.astype(jnp.bfloat16), n_dev)
-    result = (result + passed_on.astype(jnp.float32)).astype(jnp.bfloat16)
-
-    half = width // 2
+    for part in (partial, there[0]):
+        result = result + part.astype(jnp.float32)
+    result = result.astype(jnp.bfloat16)
     kept = lax.dynamic_slice_in_dim(result, core * half, half, 1)
     passed = swap_cores(lax.dynamic_slice_in_dim(result, (1 - core) * half, half, 1))
     first = core == 0

time: 60 us -> 57.8 us (0.963)
  waiting for transfers between devices: 31.8 us -> 29.6 us
  Pallas kernels: 7.99 us -> 9.96 us
  starting transfers between devices: 18.9 us -> 17 us
    ppermute x7 -> x6, waiting for transfers between devices: 18.1 us -> 7.58 us  [across(): return lax.ppermute(value, 'dev', [(i, i ^ 1) for i in range(n_dev)])]
    ppermute x7 -> x8, waiting for transfers between devices: 12.3 us -> 20.7 us  [along(): return lax.ppermute(value, 'dev', pairs)]
    pallas_call x5 -> x10, Pallas kernels: 6.87 us -> 8.84 us  [the longest x9 8.84 us: kernel_call(): pl.pallas_call(body, in_specs=kept + [pl.BlockSpec(memory_space=pl.ANY)]...]
    ppermute x7 -> x8, starting transfers between devices: 10.1 us -> 8.35 us  [along(): return lax.ppermute(value, 'dev', pairs)]
    ppermute x7 -> x6, starting transfers between devices: 8.15 us -> 8.06 us  [across(): return lax.ppermute(value, 'dev', [(i, i ^ 1) for i in range(n_dev)])]
  transfers between devices with their start and end apart: 17 -> 17, of which waited for: 11 -> 12; matrix products, arithmetic and copies ran while one was open for 0% -> 0% of each run, Pallas kernels for 13% -> 17%
where the time goes in v3:
time: 57.8 us; the launch traced here: 57.5 us
  waiting for transfers between devices  29.6 us (51%)
  starting transfers between devices  17 us (29%)
  Pallas kernels  9.96 us (17%)
  other arithmetic  0.83 us (1%)
    ppermute x8, waiting for transfers between devices, along(): return lax.ppermute(value, 'dev', pairs)  20.7 us
    pallas_call x9, Pallas kernels, kernel_call(): pl.pallas_call(body, in_specs=kept + [pl.BlockSpec(memory_space=pl.ANY)]...  8.84 us
    ppermute x8, starting transfers between devices, along(): return lax.ppermute(value, 'dev', pairs)  8.35 us
    ppermute x6, starting transfers between devices, across(): return lax.ppermute(value, 'dev', [(i, i ^ 1) for i in range(n_dev)])  8.06 us
    ppermute x6, waiting for transfers between devices, across(): return lax.ppermute(value, 'dev', [(i, i ^ 1) for i in range(n_dev)])  7.58 us
    ppermute x3, waiting for transfers between devices, swap_cores(): return lax.ppermute(value, 'sub', [(0, 1), (1, 0)])  1.31 us
  transfers between devices with their start and end apart: 17, of which 12 were waited for; matrix products, arithmetic and copies ran while one was open for 0% of the time, Pallas kernels for 17%

profile of v3, /device:TPU:0, one launch (start us, length us, event | category | flops | bytes accessed | tf_op | source)
XLA Modules:
  0.0 57.5 jit_solution(7279730654166048058)
XLA Ops:
  0.5 1.1 %shard_map.64.refs_0_ = bf16[32,3712]{1,0:T(8,128)(2,1)S(1)} custom-call(s32[1]{0:T(128)} %bitcast.1.core_ref, bf16[2,32,3584]{2,1,0:T(8,128)(2,1)} %hidden_ref.1, f32[3584]{0:T(1024)} %gain_ref.1, s32[2,2,32]{2,1,0:T(2,128)} %bitcast.10, f32[2,2,32]{2,1,0:T(2,128)} %bitcast.11), custom_call_target="tpu_custom_call" | custom-call | tf_op jit(solution)/shard_map/pallas_call | solution.py:168
  1.6 3.0 %collective-permute-start = (bf16[32,3712]{1,0:T(8,128)(2,1)S(1)}, bf16[32,3712]{1,0:T(8,128)(2,1)S(1)}, u32[]{:S(2)}, u32[]{:S(2)}) collective-permute-start(bf16[32,3712]{1,0:T(8,128)(2,1)S(1)} %shard_map.64.refs_0_), channel_id=1, source_target_pairs={{0,2},{2,0},{4,6},{6,4},{8,10},{10,8},{12,14},{14,12},{1,3},{3,1},... | collective-permute-start | bytes 712712 | tf_op jit(solution)/shard_map/ppermute | solution.py:121
  4.7 1.6 %collective-permute-start.1 = (bf16[32,3712]{1,0:T(8,128)(2,1)S(1)}, bf16[32,3712]{1,0:T(8,128)(2,1)S(1)}, u32[]{:S(2)}, u32[]{:S(2)}) collective-permute-start(bf16[32,3712]{1,0:T(8,128)(2,1)S(1)} %shard_map.64.refs_0_), channel_id=1, source_target_pairs={{0,4},{2,6},{4,0},{6,2},{8,12},{10,14},{12,8},{14,10},{1,5},{3,7},... | collective-permute-start | bytes 712712 | tf_op jit(solution)/shard_map/ppermute | solution.py:107
  6.2 2.6 %collective-permute-start.2 = (bf16[32,3712]{1,0:T(8,128)(2,1)S(1)}, bf16[32,3712]{1,0:T(8,128)(2,1)S(1)}, u32[]{:S(2)}, u32[]{:S(2)}) collective-permute-start(bf16[32,3712]{1,0:T(8,128)(2,1)S(1)} %shard_map.64.refs_0_), channel_id=1, source_target_pairs={{0,8},{2,10},{4,12},{6,14},{8,0},{10,2},{12,4},{14,6},{1,9},{3,11}... | collective-permute-start | bytes 712712 | tf_op jit(solution)/shard_map/ppermute | solution.py:107
  8.8 1.8 %collective-permute-done.refs_4_.refs_0_.refs_1_ = bf16[32,3712]{1,0:T(8,128)(2,1)S(1)} collective-permute-done((bf16[32,3712]{1,0:T(8,128)(2,1)S(1)}, bf16[32,3712]{1,0:T(8,128)(2,1)S(1)}, u32[]{:S(2)}, u32[]{:S(2)}) %collective-permute-start) | collective-permute-done | bytes 237600 | tf_op jit(solution)/shard_map/ppermute | solution.py:121
  10.6 2.6 %shard_map.65 = (bf16[3584,256]{1,0:T(8,128)(2,1)S(1)}, bf16[256,3584]{1,0:T(8,128)(2,1)S(1)}, bf16[256,3584]{1,0:T(8,128)(2,1)S(1)}, f32[8,128]{1,0:T(8,128)S(1)}) custom-call(bf16[3584,256]{1,0:T(8,128)(2,1)} %refs_0_.1, bf16[256,3584]{1,0:T(8,128)(2,1)} %refs_1_.1, bf16[256,3584]{1,0:T(8,128)(2,1)} %collective-permute-done.3.refs_2_, ...), custom_call_target="tpu_custom_call" | custom-call | tf_op jit(solution)/shard_map/pallas_call | solution.py:133
  13.2 3.8 %collective-permute-done.1.refs_2_ = bf16[32,3712]{1,0:T(8,128)(2,1)S(1)} collective-permute-done((bf16[32,3712]{1,0:T(8,128)(2,1)S(1)}, bf16[32,3712]{1,0:T(8,128)(2,1)S(1)}, u32[]{:S(2)}, u32[]{:S(2)}) %collective-permute-start.1) | collective-permute-done | bytes 237600 | tf_op jit(solution)/shard_map/ppermute | solution.py:107
  17.0 2.4 %collective-permute-done.2.refs_0_ = bf16[32,3712]{1,0:T(8,128)(2,1)S(1)} collective-permute-done((bf16[32,3712]{1,0:T(8,128)(2,1)S(1)}, bf16[32,3712]{1,0:T(8,128)(2,1)S(1)}, u32[]{:S(2)}, u32[]{:S(2)}) %collective-permute-start.2) | collective-permute-done | bytes 237600 | tf_op jit(solution)/shard_map/ppermute | solution.py:107
  19.8 0.5 collective-permute-start.7
  20.4 5.1 %collective-permute-done.5.refs_1_.refs_6_.refs_0_ = bf16[32,3712]{1,0:T(8,128)(2,1)S(1)} collective-permute-done((bf16[32,3712]{1,0:T(8,128)(2,1)S(1)}, bf16[32,3712]{1,0:T(8,128)(2,1)S(1)}, u32[]{:S(2)}, u32[]{:S(2)}) %collective-permute-start.5) | collective-permute-done | bytes 237600 | tf_op jit(solution)/shard_map/ppermute | solution.py:107
  25.5 0.6 %shard_map.67 = (bf16[32,3712]{1,0:T(8,128)(2,1)S(1)}, f32[8,128]{1,0:T(8,128)}) custom-call(bf16[32,3712]{1,0:T(8,128)(2,1)S(1)} %collective-permute-done.refs_4_.refs_0_.refs_1_, bf16[32,3712]{1,0:T(8,128)(2,1)S(1)} %collective-permute-done.5.refs_1_.refs_6_.refs_0_), custom_call_target="tpu_custom_call" | custom-call | tf_op jit(solution)/shard_map/pallas_call | solution.py:133
  26.1 0.8 %collective-permute-start.6 = (bf16[32,3712]{1,0:T(8,128)(2,1)S(1)}, bf16[32,3712]{1,0:T(8,128)(2,1)S(1)}, u32[]{:S(2)}, u32[]{:S(2)}) collective-permute-start(bf16[32,3712]{1,0:T(8,128)(2,1)S(1)} %get-tuple-element.28), channel_id=1, source_target_pairs={{0,4},{2,6},{4,0},{6,2},{8,12},{10,14},{12,8},{14,10},{1,5},{3,7},... | collective-permute-start | bytes 712712 | tf_op jit(solution)/shard_map/ppermute | solution.py:107
  26.9 0.5 collective-permute-start.10
  27.4 1.4 %shard_map.68 = (bf16[32,3584]{1,0:T(8,128)(2,1)S(1)}, bf16[32,3584]{1,0:T(8,128)(2,1)S(1)}, f32[8,128]{1,0:T(8,128)S(1)}) custom-call(bf16[32,3712]{1,0:T(8,128)(2,1)S(1)} %shard_map.66.refs_0_, bf16[32,3712]{1,0:T(8,128)(2,1)S(1)} %collective-permute-done.7.refs_1_, bf16[3584,256]{1,0:T(8,128)(2,1)S(1)} %get-tuple-element.29.refs_2_.refs_4_, ...), custom_call_target="tpu_custom_call" | custom-call | tf_op jit(solution)/shard_map/pallas_call | solution.py:133
  28.9 1.6 %collective-permute-start.9 = (bf16[32,3584]{1,0:T(8,128)(2,1)S(1)}, bf16[32,3584]{1,0:T(8,128)(2,1)S(1)}, u32[]{:S(2)}, u32[]{:S(2)}) collective-permute-start(bf16[32,3584]{1,0:T(8,128)(2,1)S(1)} %get-tuple-element.36), channel_id=1, source_target_pairs={{0,2},{2,0},{4,6},{6,4},{8,10},{10,8},{12,14},{14,12},{1,3},{3,1},... | collective-permute-start | bytes 688136 | tf_op jit(solution)/shard_map/ppermute | solution.py:121
  30.4 1.8 %collective-permute-done.6.refs_3_ = bf16[32,3712]{1,0:T(8,128)(2,1)S(1)} collective-permute-done((bf16[32,3712]{1,0:T(8,128)(2,1)S(1)}, bf16[32,3712]{1,0:T(8,128)(2,1)S(1)}, u32[]{:S(2)}, u32[]{:S(2)}) %collective-permute-start.6) | collective-permute-done | bytes 237600 | tf_op jit(solution)/shard_map/ppermute | solution.py:107
  32.2 1.4 %shard_map.69 = (bf16[32,3584]{1,0:T(8,128)(2,1)S(1)}, bf16[32,3584]{1,0:T(8,128)(2,1)S(1)}, bf16[32,3584]{1,0:T(8,128)(2,1)S(1)}, bf16[32,3584]{1,0:T(8,128)(2,1)S(1)}, f32[8,128]{1,0:T(8,128)S(1)}) custom-call(bf16[32,3712]{1,0:T(8,128)(2,1)S(1)} %shard_map.64.refs_0_, bf16[32,3712]{1,0:T(8,128)(2,1)S(1)} %collective-permute-done.refs_4_.refs_0_.refs_1_, ...), custom_call_target="tpu_custom_call" | custom-call | tf_op jit(solution)/shard_map/pallas_call | solution.py:133
  33.6 2.0 %collective-permute-done.10.refs_1_ = bf16[32,3712]{1,0:T(8,128)(2,1)S(1)} collective-permute-done((bf16[32,3712]{1,0:T(8,128)(2,1)S(1)}, bf16[32,3712]{1,0:T(8,128)(2,1)S(1)}, u32[]{:S(2)}, u32[]{:S(2)}) %collective-permute-start.10) | collective-permute-done | bytes 237600 | tf_op jit(solution)/shard_map/ppermute | solution.py:121
  35.6 1.4 %shard_map.70 = (bf16[32,3584]{1,0:T(8,128)(2,1)S(1)}, bf16[32,3584]{1,0:T(8,128)(2,1)S(1)}, f32[8,128]{1,0:T(8,128)S(1)}) custom-call(bf16[32,3712]{1,0:T(8,128)(2,1)S(1)} %collective-permute-done.5.refs_1_.refs_6_.refs_0_, bf16[32,3712]{1,0:T(8,128)(2,1)S(1)} %collective-permute-done.10.refs_1_, bf16[3584,256]{1,0:T(8,128)(2,1)S(1)} %get-tuple-element.29.refs_2_.refs_4_, ...), custom_call_target="tpu_custom_call" | custom-call | tf_op jit(solution)/shard_map/pallas_call | solution.py:133
  37.1 0.5 collective-permute-start.12
  37.6 2.0 %collective-permute-done.9.refs_1_ = bf16[32,3584]{1,0:T(8,128)(2,1)S(1)} collective-permute-done((bf16[32,3584]{1,0:T(8,128)(2,1)S(1)}, bf16[32,3584]{1,0:T(8,128)(2,1)S(1)}, u32[]{:S(2)}, u32[]{:S(2)}) %collective-permute-start.9) | collective-permute-done | bytes 229408 | tf_op jit(solution)/shard_map/ppermute | solution.py:121
  39.6 1.6 %collective-permute-start.11 = (bf16[32,3584]{1,0:T(8,128)(2,1)S(1)}, bf16[32,3584]{1,0:T(8,128)(2,1)S(1)}, u32[]{:S(2)}, u32[]{:S(2)}) collective-permute-start(bf16[32,3584]{1,0:T(8,128)(2,1)S(1)} %get-tuple-element.39), channel_id=1, source_target_pairs={{0,8},{2,10},{4,12},{6,14},{8,0},{10,2},{12,4},{14,6},{1,9},{3,11}... | collective-permute-start | bytes 688136 | tf_op jit(solution)/shard_map/ppermute | solution.py:107
  41.4 1.8 %collective-permute-done.12.refs_1_ = bf16[32,3584]{1,0:T(8,128)(2,1)S(1)} collective-permute-done((bf16[32,3584]{1,0:T(8,128)(2,1)S(1)}, bf16[32,3584]{1,0:T(8,128)(2,1)S(1)}, u32[]{:S(2)}, u32[]{:S(2)}) %collective-permute-start.12) | collective-permute-done | bytes 229408 | tf_op jit(solution)/shard_map/ppermute | solution.py:121
  43.2 1.2 %collective-permute-start.13 = (bf16[32,3584]{1,0:T(8,128)(2,1)S(1)}, bf16[32,3584]{1,0:T(8,128)(2,1)S(1)}, u32[]{:S(2)}, u32[]{:S(2)}) collective-permute-start(bf16[32,3584]{1,0:T(8,128)(2,1)S(1)} %get-tuple-element.43), channel_id=1, source_target_pairs={{0,12},{2,14},{4,8},{6,10},{8,4},{10,6},{12,0},{14,2},{1,13},{3,15... | collective-permute-start | bytes 688136 | tf_op jit(solution)/shard_map/ppermute | solution.py:107
  44.4 2.7 %collective-permute-done.14.refs_1_ = bf16[32,3584]{1,0:T(8,128)(2,1)S(1)} collective-permute-done((bf16[32,3584]{1,0:T(8,128)(2,1)S(1)}, bf16[32,3584]{1,0:T(8,128)(2,1)S(1)}, u32[]{:S(2)}, u32[]{:S(2)}) %collective-permute-start.14) | collective-permute-done | bytes 229408 | tf_op jit(solution)/shard_map/ppermute | solution.py:107
  47.1 0.6 %shard_map.74 = (bf16[32,3584]{1,0:T(8,128)(2,1)S(1)}, f32[8,128]{1,0:T(8,128)}) custom-call(bf16[32,3584]{1,0:T(8,128)(2,1)S(1)} %get-tuple-element.45.refs_0_, bf16[32,3584]{1,0:T(8,128)(2,1)S(1)} %collective-permute-done.14.refs_1_, f32[8,128]{1,0:T(8,128)S(1)} %get-tuple-element.47.refs_2_), custom_call_target="tpu_custom_call" | custom-call | tf_op jit(solution)/shard_map/pallas_call | solution.py:133
  47.7 1.9 %collective-permute-start.15 = (bf16[32,3584]{1,0:T(8,128)(2,1)S(1)}, bf16[32,3584]{1,0:T(8,128)(2,1)S(1)}, u32[]{:S(2)}, u32[]{:S(2)}) collective-permute-start(bf16[32,3584]{1,0:T(8,128)(2,1)S(1)} %get-tuple-element.48), channel_id=1, source_target_pairs={{0,2},{2,0},{4,6},{6,4},{8,10},{10,8},{12,14},{14,12},{1,3},{3,1},... | collective-permute-start | bytes 688136 | tf_op jit(solution)/shard_map/ppermute | solution.py:121
  49.6 2.4 %collective-permute-done.11.refs_2_ = bf16[32,3584]{1,0:T(8,128)(2,1)S(1)} collective-permute-done((bf16[32,3584]{1,0:T(8,128)(2,1)S(1)}, bf16[32,3584]{1,0:T(8,128)(2,1)S(1)}, u32[]{:S(2)}, u32[]{:S(2)}) %collective-permute-start.11) | collective-permute-done | bytes 229408 | tf_op jit(solution)/shard_map/ppermute | solution.py:107
  52.0 2.6 %collective-permute-done.13.refs_3_ = bf16[32,3584]{1,0:T(8,128)(2,1)S(1)} collective-permute-done((bf16[32,3584]{1,0:T(8,128)(2,1)S(1)}, bf16[32,3584]{1,0:T(8,128)(2,1)S(1)}, u32[]{:S(2)}, u32[]{:S(2)}) %collective-permute-start.13) | collective-permute-done | bytes 229408 | tf_op jit(solution)/shard_map/ppermute | solution.py:107
  54.6 0.6 %shard_map.73 = (f32[32,3584]{1,0:T(8,128)S(1)}, f32[8,128]{1,0:T(8,128)}) custom-call(bf16[32,3584]{1,0:T(8,128)(2,1)S(1)} %get-tuple-element.33.refs_0_, bf16[32,3584]{1,0:T(8,128)(2,1)S(1)} %collective-permute-done.8.refs_1_, bf16[32,3584]{1,0:T(8,128)(2,1)S(1)} %collective-permute-done.11.refs_2_, bf16[32,3584]{1,0:T(8,128)(2,1)S(1)} %collective-permute-done.13.refs_3_), custom_call_target="tpu_custom_call" | custom-call | tf_op jit(solution)/shard_map/pallas_call | solution.py:133
  55.4 1.3 %collective-permute-done.16 = bf16[32,1792]{1,0:T(8,128)(2,1)S(1)} collective-permute-done((bf16[32,1792]{1,0:T(8,128)(2,1)S(1)}, bf16[32,1792]{1,0:T(8,128)(2,1)S(1)}, u32[]{:S(2)}, u32[]{:S(2)}) %collective-permute-start.16) | collective-permute-done | bytes 114720 | tf_op jit(solution)/shard_map/ppermute | solution.py:102
  56.8 0.7 %pad_maximum_fusion = bf16[2,32,1792]{2,1,0:T(8,128)(2,1)} fusion(bf16[1,32,1792]{2,1,0:T(8,128)(2,1)S(1)} %get-tuple-element.50, bf16[1,32,1792]{2,1,0:T(8,128)(2,1)S(1)} %get-tuple-element.49), kind=kLoop, calls=%fused_computation.3 | loop fusion | flops 114688 | bytes 458752 | tf_op jit(solution)/shard_map/stack | solution.py:346
  (19 shorter events, 1.5 us)
Async XLA Ops:
  0.0 10.6 %collective-permute-start.4 = (bf16[3584,256]{1,0:T(8,128)(2,1)}, bf16[3584,256]{1,0:T(8,128)(2,1)S(1)}, u32[]{:S(2)}, u32[]{:S(2)}) collective-permute-start(bf16[3584,256]{1,0:T(8,128)(2,1)} %refs_0_.1), channel_id=1, source_target_pairs={{0,1},{1,0},{2,3},{3,2},{4,5},{5,4},{6,7},{7,6},{8,9},{9,8},{10,11... | collective-permute-start | bytes 5505032 | tf_op jit(solution)/shard_map/ppermute | solution.py:102
  0.5 10.1 %collective-permute-start.3 = (bf16[256,3584]{1,0:T(8,128)(2,1)}, bf16[256,3584]{1,0:T(8,128)(2,1)}, u32[]{:S(2)}, u32[]{:S(2)}) collective-permute-start(bf16[256,3584]{1,0:T(8,128)(2,1)} %refs_1_.1), channel_id=1, source_target_pairs={{0,1},{1,0},{2,3},{3,2},{4,5},{5,4},{6,7},{7,6},{8,9},{9,8},{10,11... | collective-permute-start | bytes 5505032 | tf_op jit(solution)/shard_map/ppermute | solution.py:102
  1.6 9.0 %collective-permute-start = (bf16[32,3712]{1,0:T(8,128)(2,1)S(1)}, bf16[32,3712]{1,0:T(8,128)(2,1)S(1)}, u32[]{:S(2)}, u32[]{:S(2)}) collective-permute-start(bf16[32,3712]{1,0:T(8,128)(2,1)S(1)} %shard_map.64.refs_0_), channel_id=1, source_target_pairs={{0,2},{2,0},{4,6},{6,4},{8,10},{10,8},{12,14},{14,12},{1,3},{3,1},... | collective-permute-start | bytes 712712 | tf_op jit(solution)/shard_map/ppermute | solution.py:121
  4.7 12.4 %collective-permute-start.1 = (bf16[32,3712]{1,0:T(8,128)(2,1)S(1)}, bf16[32,3712]{1,0:T(8,128)(2,1)S(1)}, u32[]{:S(2)}, u32[]{:S(2)}) collective-permute-start(bf16[32,3712]{1,0:T(8,128)(2,1)S(1)} %shard_map.64.refs_0_), channel_id=1, source_target_pairs={{0,4},{2,6},{4,0},{6,2},{8,12},{10,14},{12,8},{14,10},{1,5},{3,7},... | collective-permute-start | bytes 712712 | tf_op jit(solution)/shard_map/ppermute | solution.py:107
  6.2 13.2 %collective-permute-start.2 = (bf16[32,3712]{1,0:T(8,128)(2,1)S(1)}, bf16[32,3712]{1,0:T(8,128)(2,1)S(1)}, u32[]{:S(2)}, u32[]{:S(2)}) collective-permute-start(bf16[32,3712]{1,0:T(8,128)(2,1)S(1)} %shard_map.64.refs_0_), channel_id=1, source_target_pairs={{0,8},{2,10},{4,12},{6,14},{8,0},{10,2},{12,4},{14,6},{1,9},{3,11}... | collective-permute-start | bytes 712712 | tf_op jit(solution)/shard_map/ppermute | solution.py:107
  19.4 6.1 %collective-permute-start.5 = (bf16[32,3712]{1,0:T(8,128)(2,1)S(1)}, bf16[32,3712]{1,0:T(8,128)(2,1)S(1)}, u32[]{:S(2)}, u32[]{:S(2)}) collective-permute-start(bf16[32,3712]{1,0:T(8,128)(2,1)S(1)} %shard_map.66.refs_0_), channel_id=1, source_target_pairs={{0,4},{2,6},{4,0},{6,2},{8,12},{10,14},{12,8},{14,10},{1,5},{3,7},... | collective-permute-start | bytes 712712 | tf_op jit(solution)/shard_map/ppermute | solution.py:107
  19.8 7.6 %collective-permute-start.7 = (bf16[32,3712]{1,0:T(8,128)(2,1)S(1)}, bf16[32,3712]{1,0:T(8,128)(2,1)S(1)}, u32[]{:S(2)}, u32[]{:S(2)}) collective-permute-start(bf16[32,3712]{1,0:T(8,128)(2,1)S(1)} %shard_map.66.refs_0_), channel_id=1, source_target_pairs={{0,2},{2,0},{4,6},{6,4},{8,10},{10,8},{12,14},{14,12},{1,3},{3,1},... | collective-permute-start | bytes 712712 | tf_op jit(solution)/shard_map/ppermute | solution.py:121
  26.1 6.1 %collective-permute-start.6 = (bf16[32,3712]{1,0:T(8,128)(2,1)S(1)}, bf16[32,3712]{1,0:T(8,128)(2,1)S(1)}, u32[]{:S(2)}, u32[]{:S(2)}) collective-permute-start(bf16[32,3712]{1,0:T(8,128)(2,1)S(1)} %get-tuple-element.28), channel_id=1, source_target_pairs={{0,4},{2,6},{4,0},{6,2},{8,12},{10,14},{12,8},{14,10},{1,5},{3,7},... | collective-permute-start | bytes 712712 | tf_op jit(solution)/shard_map/ppermute | solution.py:107
  26.9 8.7 %collective-permute-start.10 = (bf16[32,3712]{1,0:T(8,128)(2,1)S(1)}, bf16[32,3712]{1,0:T(8,128)(2,1)S(1)}, u32[]{:S(2)}, u32[]{:S(2)}) collective-permute-start(bf16[32,3712]{1,0:T(8,128)(2,1)S(1)} %collective-permute-done.5.refs_1_.refs_6_.refs_0_), channel_id=1, source_target_pairs={{0,2},{2,0},{4,6},{6,4},{8,10},{10,8},{12,14},{14,12},{1,3},{3,1},... | collective-permute-start | bytes 712712 | tf_op jit(solution)/shard_map/ppermute | solution.py:121
  28.9 10.7 %collective-permute-start.9 = (bf16[32,3584]{1,0:T(8,128)(2,1)S(1)}, bf16[32,3584]{1,0:T(8,128)(2,1)S(1)}, u32[]{:S(2)}, u32[]{:S(2)}) collective-permute-start(bf16[32,3584]{1,0:T(8,128)(2,1)S(1)} %get-tuple-element.36), channel_id=1, source_target_pairs={{0,2},{2,0},{4,6},{6,4},{8,10},{10,8},{12,14},{14,12},{1,3},{3,1},... | collective-permute-start | bytes 688136 | tf_op jit(solution)/shard_map/ppermute | solution.py:121
  37.1 18.2 %copy-start = (bf16[2,32,3584]{2,1,0:T(8,128)(2,1)S(1)}, bf16[2,32,3584]{2,1,0:T(8,128)(2,1)}, u32[]{:S(2)}) copy-start(bf16[2,32,3584]{2,1,0:T(8,128)(2,1)} %hidden_ref.1) | copy-start | bytes 1376260
  37.1 6.1 %collective-permute-start.12 = (bf16[32,3584]{1,0:T(8,128)(2,1)S(1)}, bf16[32,3584]{1,0:T(8,128)(2,1)S(1)}, u32[]{:S(2)}, u32[]{:S(2)}) collective-permute-start(bf16[32,3584]{1,0:T(8,128)(2,1)S(1)} %get-tuple-element.41), channel_id=1, source_target_pairs={{0,2},{2,0},{4,6},{6,4},{8,10},{10,8},{12,14},{14,12},{1,3},{3,1},... | collective-permute-start | bytes 688136 | tf_op jit(solution)/shard_map/ppermute | solution.py:121
  37.6 9.5 %collective-permute-start.14 = (bf16[32,3584]{1,0:T(8,128)(2,1)S(1)}, bf16[32,3584]{1,0:T(8,128)(2,1)S(1)}, u32[]{:S(2)}, u32[]{:S(2)}) collective-permute-start(bf16[32,3584]{1,0:T(8,128)(2,1)S(1)} %get-tuple-element.46), channel_id=1, source_target_pairs={{0,4},{2,6},{4,0},{6,2},{8,12},{10,14},{12,8},{14,10},{1,5},{3,7},... | collective-permute-start | bytes 688136 | tf_op jit(solution)/shard_map/ppermute | solution.py:107
  39.6 12.4 %collective-permute-start.11 = (bf16[32,3584]{1,0:T(8,128)(2,1)S(1)}, bf16[32,3584]{1,0:T(8,128)(2,1)S(1)}, u32[]{:S(2)}, u32[]{:S(2)}) collective-permute-start(bf16[32,3584]{1,0:T(8,128)(2,1)S(1)} %get-tuple-element.39), channel_id=1, source_target_pairs={{0,8},{2,10},{4,12},{6,14},{8,0},{10,2},{12,4},{14,6},{1,9},{3,11}... | collective-permute-start | bytes 688136 | tf_op jit(solution)/shard_map/ppermute | solution.py:107
  41.2 10.8 %collective-permute-start.8 = (bf16[32,3584]{1,0:T(8,128)(2,1)S(1)}, bf16[32,3584]{1,0:T(8,128)(2,1)S(1)}, u32[]{:S(2)}, u32[]{:S(2)}) collective-permute-start(bf16[32,3584]{1,0:T(8,128)(2,1)S(1)} %get-tuple-element.34), channel_id=1, source_target_pairs={{0,4},{2,6},{4,0},{6,2},{8,12},{10,14},{12,8},{14,10},{1,5},{3,7},... | collective-permute-start | bytes 688136 | tf_op jit(solution)/shard_map/ppermute | solution.py:107
  43.2 11.4 %collective-permute-start.13 = (bf16[32,3584]{1,0:T(8,128)(2,1)S(1)}, bf16[32,3584]{1,0:T(8,128)(2,1)S(1)}, u32[]{:S(2)}, u32[]{:S(2)}) collective-permute-start(bf16[32,3584]{1,0:T(8,128)(2,1)S(1)} %get-tuple-element.43), channel_id=1, source_target_pairs={{0,12},{2,14},{4,8},{6,10},{8,4},{10,6},{12,0},{14,2},{1,13},{3,15... | collective-permute-start | bytes 688136 | tf_op jit(solution)/shard_map/ppermute | solution.py:107
  47.7 7.6 %collective-permute-start.15 = (bf16[32,3584]{1,0:T(8,128)(2,1)S(1)}, bf16[32,3584]{1,0:T(8,128)(2,1)S(1)}, u32[]{:S(2)}, u32[]{:S(2)}) collective-permute-start(bf16[32,3584]{1,0:T(8,128)(2,1)S(1)} %get-tuple-element.48), channel_id=1, source_target_pairs={{0,2},{2,0},{4,6},{6,4},{8,10},{10,8},{12,14},{14,12},{1,3},{3,1},... | collective-permute-start | bytes 688136 | tf_op jit(solution)/shard_map/ppermute | solution.py:121
  55.4 1.4 %collective-permute-start.16 = (bf16[32,1792]{1,0:T(8,128)(2,1)S(1)}, bf16[32,1792]{1,0:T(8,128)(2,1)S(1)}, u32[]{:S(2)}, u32[]{:S(2)}) collective-permute-start(bf16[32,1792]{1,0:T(8,128)(2,1)S(1)} %constant_dynamic-slice_fusion), channel_id=1, source_target_pairs={{0,1},{1,0},{2,3},{3,2},{4,5},{5,4},{6,7},{7,6},{8,9},{9,8},{10,11... | collective-permute-start | bytes 344072 | tf_op jit(solution)/shard_map/ppermute | solution.py:102

commit v4 on v3

--- a/solution.py
+++ b/solution.py
@@ -107,16 +107,6 @@
     return lax.ppermute(value, "dev", pairs)
 
 
-def along_to_core(value, step, experts, other):
-    pairs = [
-        (4 * z + 2 * x + s, 4 * (z ^ step) + 2 * x + (s ^ other))
-        for z in range(experts)
-        for x in range(2)
-        for s in range(2)
-    ]
-    return lax.ppermute(value, ("dev", "sub"), pairs)
-
-
 def across(value, n_dev):
     return lax.ppermute(value, "dev", [(i, i ^ 1) for i in range(n_dev)])
 
@@ -125,10 +115,12 @@
     vmem = pl.BlockSpec(memory_space=pltpu.VMEM)
     kept = [pl.BlockSpec(memory_space=pltpu.HBM)] * hbm + [vmem] * (len(operands) - hbm)
     count = len(operands)
+    first = count + len(after)
+    last = first + len(outs)
 
     def body(*refs):
-        kernel(*refs[:count], *refs[count + len(after) : count + len(after) + len(outs)], *refs[count + len(after) + len(outs) + 1 :])
-        refs[count + len(after) + len(outs)][...] = jnp.zeros(TOKEN, jnp.float32)
+        kernel(*refs[:count], *refs[first:last], *refs[last + 1 :])
+        refs[last][...] = jnp.zeros(TOKEN, jnp.float32)
 
     *given, token = pl.pallas_call(
         body,
@@ -207,7 +199,7 @@
     return kernel_call(kernel, arrays, outs, after, count, [pltpu.SemaphoreType.DMA((count,))])
 
 
-def expert(blocks, weights, experts, after):
+def expert(blocks, weights, experts, after=()):
     count = len(blocks)
     rows, width = blocks[0].shape[0], weights[0].shape[0]
 
@@ -234,9 +226,8 @@
             for i, ref in enumerate(out_refs):
                 ref[:, start : start + step] = out[i * rows : (i + 1) * rows]
 
-    return kernel_call(
-        kernel, [*blocks, *weights], [((rows, width), jnp.bfloat16)] * count, after
-    )
+    outs = [((rows, width), jnp.bfloat16)] * count
+    return kernel_call(kernel, [*blocks, *weights], outs, after)
 
 
 def add(terms, after=(), dtype=jnp.bfloat16):
@@ -250,41 +241,27 @@
     return total, token
 
 
-def add_halves(terms, dtype, after=()):
-    rows, width = terms[0].shape
-    half = width // 2
-
-    def kernel(*refs):
+def place(value, other, out=None):
+    shape = (2, *value.shape)
+    given = [value] if out is None else [value, out]
+
+    def kernel(value_ref, *refs):
+        out_ref, arrived = refs[-2:]
         core = lax.axis_index("sub")
-        for which, out_ref in ((core, refs[-2]), (1 - core, refs[-1])):
-            place = pl.ds(pl.multiple_of(which * half, LANES), half)
-            total = refs[0][:, place].astype(jnp.float32)
-            for ref in refs[1:-2]:
-                total = total + ref[:, place].astype(jnp.float32)
-            out_ref[...] = total.astype(dtype)
-
-    return kernel_call(kernel, terms, [((rows, half), dtype)] * 2, after)
-
-
-def finish(kept, passed):
-    def kernel(*refs):
-        core = lax.axis_index("sub")
-        out_ref = refs[-1]
-        for place, refs in ((core, refs[: len(kept)]), (1 - core, refs[len(kept) : -1])):
-            total = refs[0][...].astype(jnp.float32)
-            for ref in refs[1:]:
-                total = total + ref[...].astype(jnp.float32)
-            out_ref[place] = total.astype(jnp.bfloat16)
-
-    terms = [*kept, *passed]
-    vmem = pl.BlockSpec(memory_space=pltpu.VMEM)
+        copy = pltpu.make_async_copy(value_ref, out_ref.at[1 - core if other else core], arrived)
+        copy.start()
+        copy.wait()
+
     return pl.pallas_call(
         kernel,
-        in_specs=[vmem] * len(terms),
-        out_specs=vmem,
-        out_shape=jax.ShapeDtypeStruct((2, *kept[0].shape), jnp.bfloat16),
+        in_specs=[pl.BlockSpec(memory_space=pltpu.VMEM)]
+        + [pl.BlockSpec(memory_space=pltpu.HBM)] * (len(given) - 1),
+        out_specs=pl.BlockSpec(memory_space=pltpu.HBM),
+        out_shape=jax.ShapeDtypeStruct(shape, value.dtype),
+        scratch_shapes=[pltpu.SemaphoreType.DMA],
+        input_output_aliases={} if out is None else {1: 0},
         compiler_params=pltpu.CompilerParams(vmem_limit_bytes=VMEM_BYTES),
-    )(*[in_vmem(v) for v in terms])
+    )(in_vmem(value), *given[1:])
 
 
 def pass_after(value, after):
@@ -305,11 +282,11 @@
     core = lax.axis_index("sub")
     others = [swap_cores(w_in), swap_cores(w_out)]
     block = pack(core, hidden, norm_gain, routes, route_weight, experts)
-    column, beside = {0: block}, {}
+    column, beside, own, give, there = {0: block}, {}, {}, {}, {}
     beside[0] = across(block, n_dev)
     column[2] = along(block, 2, experts)
     column[1] = along(block, 1, experts)
-    (w_in, w_out, w_out_other), loaded = load([w_in, w_out, others[1]], [others[0], beside[0]])
+    (w_in, w_out, w_out_other), loaded = load([w_in, w_out, others[1]], [others[0]])
     weights = [w_in, others[0], w_out, w_out_other]
     column[2] = pass_after(column[2], [loaded, column[1]])
     column[3] = along(column[2], 1, experts)
@@ -318,8 +295,7 @@
     again, _ = add([beside[0]], [column[3]])
     beside[1] = along(again, 1, experts)
 
-    own, give, there = {}, {}, {}
-    (own[2], give[2]), token = expert([column[2], beside[2]], weights, experts, [column[3]])
+    (own[2], give[2]), token = expert([column[2], beside[2]], weights, experts)
     there[2] = across(give[2], n_dev)
     (own[0], give[0], own[1], give[1]), token = expert(
         [block, beside[0], column[1], beside[1]], weights, experts, [token]
@@ -330,20 +306,18 @@
     total, token = add([own[2], there[2]], [token])
     from_2 = along(total, 2, experts)
     total, token = add([own[3], there[3]], [token])
-    last = along(total, 3, experts)
+    from_3 = along(total, 3, experts)
     total, _ = add([give[0], back_give], [token])
     there[0] = across(total, n_dev)
-    partial, _ = add([own[0], back_own, from_2, last], [], jnp.float32)
-    rows, width = own[0].shape
-    half = width // 2
+
+    partial, _ = add([own[0], back_own, from_2], dtype=jnp.float32)
+    partial, _ = add([partial, from_3], dtype=jnp.float32)
+    half = hidden.shape[2] // 2
     result = lax.dynamic_index_in_dim(hidden, core, 0, keepdims=False).astype(jnp.float32)
-    for part in (partial, there[0]):
-        result = result + part.astype(jnp.float32)
-    result = result.astype(jnp.bfloat16)
+    result = (result + partial + there[0].astype(jnp.float32)).astype(jnp.bfloat16)
     kept = lax.dynamic_slice_in_dim(result, core * half, half, 1)
     passed = swap_cores(lax.dynamic_slice_in_dim(result, (1 - core) * half, half, 1))
-    first = core == 0
-    return jnp.stack([jnp.where(first, kept, passed), jnp.where(first, passed, kept)])
+    return place(passed, True, place(kept, False))
 
 
 def local(hidden, norm_gain, routes, route_weight, w_in, w_out):

time: 57.8 us -> 57.4 us (level)
  waiting for transfers between devices: 29.6 us -> 26.8 us
  Pallas kernels: 9.96 us -> 11.9 us
  starting transfers between devices: 17 us -> 18.2 us
  other arithmetic: 0.83 us -> 0.07 us
    ppermute x6, waiting for transfers between devices: 7.58 us -> 4.6 us  [across(): return lax.ppermute(value, 'dev', [(i, i ^ 1) for i in range(n_dev)])]
    ppermute x8, starting transfers between devices: 8.35 us -> 10.8 us  [along(): return lax.ppermute(value, 'dev', pairs)]
    pallas_call x0 -> x2, Pallas kernels: none -> 1.32 us  [place(): pl.pallas_call(kernel, in_specs=[pl.BlockSpec(memory_space=pltpu.VMEM)] +...]
    ppermute x6, starting transfers between devices: 8.06 us -> 6.91 us  [across(): return lax.ppermute(value, 'dev', [(i, i ^ 1) for i in range(n_dev)])]
    ppermute x8, waiting for transfers between devices: 20.7 us -> 21.6 us  [along(): return lax.ppermute(value, 'dev', pairs)]
    another operation x2 -> x0, other arithmetic: 0.75 us -> none  [whole_blocks(): jnp.stack([jnp.where(first, kept, passed), jnp.where(first, passed, kept)])]
    ppermute x3, waiting for transfers between devices: 1.31 us -> 0.65 us  [swap_cores(): return lax.ppermute(value, 'sub', [(0, 1), (1, 0)])]
    pallas_call x9 -> x10, Pallas kernels: 8.84 us -> 9.48 us  [kernel_call(): pl.pallas_call(body, in_specs=kept + [pl.BlockSpec(memory_space=pl.ANY)]...]
  transfers between devices with their start and end apart: 17 -> 17, of which waited for: 12 -> 11; matrix products, arithmetic and copies ran while one was open for 0% -> 0% of each run, Pallas kernels for 17% -> 20%
where the time goes in v4:
time: 57.4 us; the launch traced here: 57.2 us
  waiting for transfers between devices  26.8 us (47%)
  starting transfers between devices  18.2 us (32%)
  Pallas kernels  11.9 us (21%)
    ppermute x8, waiting for transfers between devices, along(): return lax.ppermute(value, 'dev', pairs)  21.6 us
    ppermute x8, starting transfers between devices, along(): return lax.ppermute(value, 'dev', pairs)  10.8 us
    pallas_call x10, Pallas kernels, kernel_call(): pl.pallas_call(body, in_specs=kept + [pl.BlockSpec(memory_space=pl.ANY)]...  9.48 us
    ppermute x6, starting transfers between devices, across(): return lax.ppermute(value, 'dev', [(i, i ^ 1) for i in range(n_dev)])  6.91 us
    ppermute x6, waiting for transfers between devices, across(): return lax.ppermute(value, 'dev', [(i, i ^ 1) for i in range(n_dev)])  4.6 us
    pallas_call x2, Pallas kernels, place(): pl.pallas_call(kernel, in_specs=[pl.BlockSpec(memory_space=pltpu.VMEM)] +...  1.32 us
  transfers between devices with their start and end apart: 17, of which 11 were waited for; matrix products, arithmetic and copies ran while one was open for 0% of the time, Pallas kernels for 20%

profile of v4, /device:TPU:0, one launch (start us, length us, event | category | flops | bytes accessed | tf_op | source)
XLA Modules:
  0.0 57.2 jit_solution(4542559601937383273)
XLA Ops:
  0.5 1.1 %shard_map.64.refs_0_ = bf16[32,3712]{1,0:T(8,128)(2,1)S(1)} custom-call(s32[1]{0:T(128)} %bitcast.1.core_ref, bf16[2,32,3584]{2,1,0:T(8,128)(2,1)} %hidden_ref.1, f32[3584]{0:T(1024)} %gain_ref.1, s32[2,2,32]{2,1,0:T(2,128)} %bitcast.6, f32[2,2,32]{2,1,0:T(2,128)} %bitcast.7), custom_call_target="tpu_custom_call" | custom-call | tf_op jit(solution)/shard_map/pallas_call | solution.py:160
  1.6 3.1 %collective-permute-start.1 = (bf16[32,3712]{1,0:T(8,128)(2,1)S(1)}, bf16[32,3712]{1,0:T(8,128)(2,1)S(1)}, u32[]{:S(2)}, u32[]{:S(2)}) collective-permute-start(bf16[32,3712]{1,0:T(8,128)(2,1)S(1)} %shard_map.64.refs_0_), channel_id=1, source_target_pairs={{0,4},{2,6},{4,0},{6,2},{8,12},{10,14},{12,8},{14,10},{1,5},{3,7},... | collective-permute-start | bytes 712712 | tf_op jit(solution)/shard_map/ppermute | solution.py:107
  4.7 2.6 %collective-permute-start.2 = (bf16[32,3712]{1,0:T(8,128)(2,1)S(1)}, bf16[32,3712]{1,0:T(8,128)(2,1)S(1)}, u32[]{:S(2)}, u32[]{:S(2)}) collective-permute-start(bf16[32,3712]{1,0:T(8,128)(2,1)S(1)} %shard_map.64.refs_0_), channel_id=1, source_target_pairs={{0,8},{2,10},{4,12},{6,14},{8,0},{10,2},{12,4},{14,6},{1,9},{3,11}... | collective-permute-start | bytes 712712 | tf_op jit(solution)/shard_map/ppermute | solution.py:107
  7.3 1.5 %collective-permute-start = (bf16[32,3712]{1,0:T(8,128)(2,1)S(1)}, bf16[32,3712]{1,0:T(8,128)(2,1)S(1)}, u32[]{:S(2)}, u32[]{:S(2)}) collective-permute-start(bf16[32,3712]{1,0:T(8,128)(2,1)S(1)} %shard_map.64.refs_0_), channel_id=1, source_target_pairs={{0,2},{2,0},{4,6},{6,4},{8,10},{10,8},{12,14},{14,12},{1,3},{3,1},... | collective-permute-start | bytes 712712 | tf_op jit(solution)/shard_map/ppermute | solution.py:111
  8.8 2.6 %shard_map.65 = (bf16[3584,256]{1,0:T(8,128)(2,1)S(1)}, bf16[256,3584]{1,0:T(8,128)(2,1)S(1)}, bf16[256,3584]{1,0:T(8,128)(2,1)S(1)}, f32[8,128]{1,0:T(8,128)S(1)}) custom-call(bf16[3584,256]{1,0:T(8,128)(2,1)} %refs_0_.1, bf16[256,3584]{1,0:T(8,128)(2,1)} %refs_1_.1, bf16[256,3584]{1,0:T(8,128)(2,1)} %collective-permute-done.3.refs_2_, ...), custom_call_target="tpu_custom_call" | custom-call | tf_op jit(solution)/shard_map/pallas_call | solution.py:125
  11.5 4.2 %collective-permute-done.1.refs_2_ = bf16[32,3712]{1,0:T(8,128)(2,1)S(1)} collective-permute-done((bf16[32,3712]{1,0:T(8,128)(2,1)S(1)}, bf16[32,3712]{1,0:T(8,128)(2,1)S(1)}, u32[]{:S(2)}, u32[]{:S(2)}) %collective-permute-start.1) | collective-permute-done | bytes 237600 | tf_op jit(solution)/shard_map/ppermute | solution.py:107
  15.7 2.5 %collective-permute-done.2.refs_0_ = bf16[32,3712]{1,0:T(8,128)(2,1)S(1)} collective-permute-done((bf16[32,3712]{1,0:T(8,128)(2,1)S(1)}, bf16[32,3712]{1,0:T(8,128)(2,1)S(1)}, u32[]{:S(2)}, u32[]{:S(2)}) %collective-permute-start.2) | collective-permute-done | bytes 237600 | tf_op jit(solution)/shard_map/ppermute | solution.py:107
  18.6 1.5 %collective-permute-start.7 = (bf16[32,3712]{1,0:T(8,128)(2,1)S(1)}, bf16[32,3712]{1,0:T(8,128)(2,1)S(1)}, u32[]{:S(2)}, u32[]{:S(2)}) collective-permute-start(bf16[32,3712]{1,0:T(8,128)(2,1)S(1)} %shard_map.66.refs_0_), channel_id=1, source_target_pairs={{0,2},{2,0},{4,6},{6,4},{8,10},{10,8},{12,14},{14,12},{1,3},{3,1},... | collective-permute-start | bytes 712712 | tf_op jit(solution)/shard_map/ppermute | solution.py:111
  20.1 4.2 %collective-permute-done.5.refs_1_.refs_0_ = bf16[32,3712]{1,0:T(8,128)(2,1)S(1)} collective-permute-done((bf16[32,3712]{1,0:T(8,128)(2,1)S(1)}, bf16[32,3712]{1,0:T(8,128)(2,1)S(1)}, u32[]{:S(2)}, u32[]{:S(2)}) %collective-permute-start.5) | collective-permute-done | bytes 237600 | tf_op jit(solution)/shard_map/ppermute | solution.py:107
  24.3 0.6 %shard_map.67 = (bf16[32,3712]{1,0:T(8,128)(2,1)S(1)}, f32[8,128]{1,0:T(8,128)}) custom-call(bf16[32,3712]{1,0:T(8,128)(2,1)S(1)} %collective-permute-done.refs_0_.refs_1_, bf16[32,3712]{1,0:T(8,128)(2,1)S(1)} %collective-permute-done.5.refs_1_.refs_0_), custom_call_target="tpu_custom_call" | custom-call | tf_op jit(solution)/shard_map/pallas_call | solution.py:125
  24.9 1.1 %collective-permute-start.6 = (bf16[32,3712]{1,0:T(8,128)(2,1)S(1)}, bf16[32,3712]{1,0:T(8,128)(2,1)S(1)}, u32[]{:S(2)}, u32[]{:S(2)}) collective-permute-start(bf16[32,3712]{1,0:T(8,128)(2,1)S(1)} %get-tuple-element.29), channel_id=1, source_target_pairs={{0,4},{2,6},{4,0},{6,2},{8,12},{10,14},{12,8},{14,10},{1,5},{3,7},... | collective-permute-start | bytes 712712 | tf_op jit(solution)/shard_map/ppermute | solution.py:107
  26.0 1.5 %collective-permute-start.10 = (bf16[32,3712]{1,0:T(8,128)(2,1)S(1)}, bf16[32,3712]{1,0:T(8,128)(2,1)S(1)}, u32[]{:S(2)}, u32[]{:S(2)}) collective-permute-start(bf16[32,3712]{1,0:T(8,128)(2,1)S(1)} %collective-permute-done.5.refs_1_.refs_0_), channel_id=1, source_target_pairs={{0,2},{2,0},{4,6},{6,4},{8,10},{10,8},{12,14},{14,12},{1,3},{3,1},... | collective-permute-start | bytes 712712 | tf_op jit(solution)/shard_map/ppermute | solution.py:111
  27.5 1.4 %shard_map.68 = (bf16[32,3584]{1,0:T(8,128)(2,1)S(1)}, bf16[32,3584]{1,0:T(8,128)(2,1)S(1)}, f32[8,128]{1,0:T(8,128)S(1)}) custom-call(bf16[32,3712]{1,0:T(8,128)(2,1)S(1)} %shard_map.66.refs_0_, bf16[32,3712]{1,0:T(8,128)(2,1)S(1)} %collective-permute-done.7.refs_1_, bf16[3584,256]{1,0:T(8,128)(2,1)S(1)} %get-tuple-element.30.refs_2_.refs_4_, ...), custom_call_target="tpu_custom_call" | custom-call | tf_op jit(solution)/shard_map/pallas_call | solution.py:125
  29.6 1.5 %collective-permute-done.6.refs_3_ = bf16[32,3712]{1,0:T(8,128)(2,1)S(1)} collective-permute-done((bf16[32,3712]{1,0:T(8,128)(2,1)S(1)}, bf16[32,3712]{1,0:T(8,128)(2,1)S(1)}, u32[]{:S(2)}, u32[]{:S(2)}) %collective-permute-start.6) | collective-permute-done | bytes 237600 | tf_op jit(solution)/shard_map/ppermute | solution.py:107
  31.0 1.4 %shard_map.69 = (bf16[32,3584]{1,0:T(8,128)(2,1)S(1)}, bf16[32,3584]{1,0:T(8,128)(2,1)S(1)}, bf16[32,3584]{1,0:T(8,128)(2,1)S(1)}, bf16[32,3584]{1,0:T(8,128)(2,1)S(1)}, f32[8,128]{1,0:T(8,128)S(1)}) custom-call(bf16[32,3712]{1,0:T(8,128)(2,1)S(1)} %shard_map.64.refs_0_, bf16[32,3712]{1,0:T(8,128)(2,1)S(1)} %collective-permute-done.refs_0_.refs_1_, ...), custom_call_target="tpu_custom_call" | custom-call | tf_op jit(solution)/shard_map/pallas_call | solution.py:125
  32.4 2.2 %collective-permute-done.10.refs_1_ = bf16[32,3712]{1,0:T(8,128)(2,1)S(1)} collective-permute-done((bf16[32,3712]{1,0:T(8,128)(2,1)S(1)}, bf16[32,3712]{1,0:T(8,128)(2,1)S(1)}, u32[]{:S(2)}, u32[]{:S(2)}) %collective-permute-start.10) | collective-permute-done | bytes 237600 | tf_op jit(solution)/shard_map/ppermute | solution.py:111
  34.6 1.4 %shard_map.70 = (bf16[32,3584]{1,0:T(8,128)(2,1)S(1)}, bf16[32,3584]{1,0:T(8,128)(2,1)S(1)}, f32[8,128]{1,0:T(8,128)S(1)}) custom-call(bf16[32,3712]{1,0:T(8,128)(2,1)S(1)} %collective-permute-done.5.refs_1_.refs_0_, bf16[32,3712]{1,0:T(8,128)(2,1)S(1)} %collective-permute-done.10.refs_1_, bf16[3584,256]{1,0:T(8,128)(2,1)S(1)} %get-tuple-element.30.refs_2_.refs_4_, ...), custom_call_target="tpu_custom_call" | custom-call | tf_op jit(solution)/shard_map/pallas_call | solution.py:125
  36.0 1.7 %collective-permute-start.12 = (bf16[32,3584]{1,0:T(8,128)(2,1)S(1)}, bf16[32,3584]{1,0:T(8,128)(2,1)S(1)}, u32[]{:S(2)}, u32[]{:S(2)}) collective-permute-start(bf16[32,3584]{1,0:T(8,128)(2,1)S(1)} %get-tuple-element.43), channel_id=1, source_target_pairs={{0,2},{2,0},{4,6},{6,4},{8,10},{10,8},{12,14},{14,12},{1,3},{3,1},... | collective-permute-start | bytes 688136 | tf_op jit(solution)/shard_map/ppermute | solution.py:111
  37.8 1.4 %collective-permute-done.9.refs_1_ = bf16[32,3584]{1,0:T(8,128)(2,1)S(1)} collective-permute-done((bf16[32,3584]{1,0:T(8,128)(2,1)S(1)}, bf16[32,3584]{1,0:T(8,128)(2,1)S(1)}, u32[]{:S(2)}, u32[]{:S(2)}) %collective-permute-start.9) | collective-permute-done | bytes 229408 | tf_op jit(solution)/shard_map/ppermute | solution.py:111
  39.2 0.8 %collective-permute-start.11 = (bf16[32,3584]{1,0:T(8,128)(2,1)S(1)}, bf16[32,3584]{1,0:T(8,128)(2,1)S(1)}, u32[]{:S(2)}, u32[]{:S(2)}) collective-permute-start(bf16[32,3584]{1,0:T(8,128)(2,1)S(1)} %get-tuple-element.40), channel_id=1, source_target_pairs={{0,8},{2,10},{4,12},{6,14},{8,0},{10,2},{12,4},{14,6},{1,9},{3,11}... | collective-permute-start | bytes 688136 | tf_op jit(solution)/shard_map/ppermute | solution.py:107
  40.0 1.1 %collective-permute-start.8 = (bf16[32,3584]{1,0:T(8,128)(2,1)S(1)}, bf16[32,3584]{1,0:T(8,128)(2,1)S(1)}, u32[]{:S(2)}, u32[]{:S(2)}) collective-permute-start(bf16[32,3584]{1,0:T(8,128)(2,1)S(1)} %get-tuple-element.35), channel_id=1, source_target_pairs={{0,4},{2,6},{4,0},{6,2},{8,12},{10,14},{12,8},{14,10},{1,5},{3,7},... | collective-permute-start | bytes 688136 | tf_op jit(solution)/shard_map/ppermute | solution.py:107
  41.1 1.0 %collective-permute-done.12.refs_1_ = bf16[32,3584]{1,0:T(8,128)(2,1)S(1)} collective-permute-done((bf16[32,3584]{1,0:T(8,128)(2,1)S(1)}, bf16[32,3584]{1,0:T(8,128)(2,1)S(1)}, u32[]{:S(2)}, u32[]{:S(2)}) %collective-permute-start.12) | collective-permute-done | bytes 229408 | tf_op jit(solution)/shard_map/ppermute | solution.py:111
  42.2 1.6 %collective-permute-start.13 = (bf16[32,3584]{1,0:T(8,128)(2,1)S(1)}, bf16[32,3584]{1,0:T(8,128)(2,1)S(1)}, u32[]{:S(2)}, u32[]{:S(2)}) collective-permute-start(bf16[32,3584]{1,0:T(8,128)(2,1)S(1)} %get-tuple-element.45), channel_id=1, source_target_pairs={{0,12},{2,14},{4,8},{6,10},{8,4},{10,6},{12,0},{14,2},{1,13},{3,15... | collective-permute-start | bytes 688136 | tf_op jit(solution)/shard_map/ppermute | solution.py:107
  43.8 2.1 %collective-permute-done.14.refs_1_ = bf16[32,3584]{1,0:T(8,128)(2,1)S(1)} collective-permute-done((bf16[32,3584]{1,0:T(8,128)(2,1)S(1)}, bf16[32,3584]{1,0:T(8,128)(2,1)S(1)}, u32[]{:S(2)}, u32[]{:S(2)}) %collective-permute-start.14) | collective-permute-done | bytes 229408 | tf_op jit(solution)/shard_map/ppermute | solution.py:107
  45.9 0.6 %shard_map.75 = (bf16[32,3584]{1,0:T(8,128)(2,1)S(1)}, f32[8,128]{1,0:T(8,128)}) custom-call(bf16[32,3584]{1,0:T(8,128)(2,1)S(1)} %get-tuple-element.47.refs_0_, bf16[32,3584]{1,0:T(8,128)(2,1)S(1)} %collective-permute-done.14.refs_1_, f32[8,128]{1,0:T(8,128)S(1)} %get-tuple-element.49.refs_2_), custom_call_target="tpu_custom_call" | custom-call | tf_op jit(solution)/shard_map/pallas_call | solution.py:125
  46.7 5.1 %collective-permute-done.11.refs_2_ = bf16[32,3584]{1,0:T(8,128)(2,1)S(1)} collective-permute-done((bf16[32,3584]{1,0:T(8,128)(2,1)S(1)}, bf16[32,3584]{1,0:T(8,128)(2,1)S(1)}, u32[]{:S(2)}, u32[]{:S(2)}) %collective-permute-start.11) | collective-permute-done | bytes 229408 | tf_op jit(solution)/shard_map/ppermute | solution.py:107
  51.7 0.6 %shard_map.72 = (f32[32,3584]{1,0:T(8,128)S(1)}, f32[8,128]{1,0:T(8,128)}) custom-call(bf16[32,3584]{1,0:T(8,128)(2,1)S(1)} %get-tuple-element.34.refs_0_, bf16[32,3584]{1,0:T(8,128)(2,1)S(1)} %collective-permute-done.8.refs_1_, bf16[32,3584]{1,0:T(8,128)(2,1)S(1)} %collective-permute-done.11.refs_2_), custom_call_target="tpu_custom_call" | custom-call | tf_op jit(solution)/shard_map/pallas_call | solution.py:125
  52.3 2.0 %collective-permute-done.13.refs_1_ = bf16[32,3584]{1,0:T(8,128)(2,1)S(1)} collective-permute-done((bf16[32,3584]{1,0:T(8,128)(2,1)S(1)}, bf16[32,3584]{1,0:T(8,128)(2,1)S(1)}, u32[]{:S(2)}, u32[]{:S(2)}) %collective-permute-start.13) | collective-permute-done | bytes 229408 | tf_op jit(solution)/shard_map/ppermute | solution.py:107
  54.4 0.6 %shard_map.74 = (f32[32,3584]{1,0:T(8,128)S(1)}, f32[8,128]{1,0:T(8,128)}) custom-call(f32[32,3584]{1,0:T(8,128)S(1)} %get-tuple-element.41.refs_0_, bf16[32,3584]{1,0:T(8,128)(2,1)S(1)} %collective-permute-done.13.refs_1_), custom_call_target="tpu_custom_call" | custom-call | tf_op jit(solution)/shard_map/pallas_call | solution.py:125
  55.2 0.7 %shard_map.76.refs_0_ = bf16[2,32,1792]{2,1,0:T(8,128)(2,1)} custom-call(bf16[32,1792]{1,0:T(8,128)(2,1)S(1)} %get-tuple-element.51.value_ref), custom_call_target="tpu_custom_call" | custom-call | tf_op jit(solution)/shard_map/pallas_call | solution.py:255
  55.9 0.6 %collective-permute-done.16.value_ref = bf16[32,1792]{1,0:T(8,128)(2,1)S(1)} collective-permute-done((bf16[32,1792]{1,0:T(8,128)(2,1)S(1)}, bf16[32,1792]{1,0:T(8,128)(2,1)S(1)}, u32[]{:S(2)}, u32[]{:S(2)}) %collective-permute-start.16) | collective-permute-done | bytes 114720 | tf_op jit(solution)/shard_map/ppermute | solution.py:102
  56.5 0.7 %shard_map.77 = bf16[2,32,1792]{2,1,0:T(8,128)(2,1)} custom-call(bf16[32,1792]{1,0:T(8,128)(2,1)S(1)} %collective-permute-done.16.value_ref, bf16[2,32,1792]{2,1,0:T(8,128)(2,1)} %shard_map.76.refs_0_), custom_call_target="tpu_custom_call", output_to_operand_aliasing={{}: (1, {})} | custom-call | tf_op jit(solution)/shard_map/pallas_call | solution.py:255
  (20 shorter events, 2.0 us)
Async XLA Ops:
  0.0 8.8 %collective-permute-start.4 = (bf16[3584,256]{1,0:T(8,128)(2,1)}, bf16[3584,256]{1,0:T(8,128)(2,1)S(1)}, u32[]{:S(2)}, u32[]{:S(2)}) collective-permute-start(bf16[3584,256]{1,0:T(8,128)(2,1)} %refs_0_.1), channel_id=1, source_target_pairs={{0,1},{1,0},{2,3},{3,2},{4,5},{5,4},{6,7},{7,6},{8,9},{9,8},{10,11... | collective-permute-start | bytes 5505032 | tf_op jit(solution)/shard_map/ppermute | solution.py:102
  0.5 8.4 %collective-permute-start.3 = (bf16[256,3584]{1,0:T(8,128)(2,1)}, bf16[256,3584]{1,0:T(8,128)(2,1)}, u32[]{:S(2)}, u32[]{:S(2)}) collective-permute-start(bf16[256,3584]{1,0:T(8,128)(2,1)} %refs_1_.1), channel_id=1, source_target_pairs={{0,1},{1,0},{2,3},{3,2},{4,5},{5,4},{6,7},{7,6},{8,9},{9,8},{10,11... | collective-permute-start | bytes 5505032 | tf_op jit(solution)/shard_map/ppermute | solution.py:102
  1.6 14.0 %collective-permute-start.1 = (bf16[32,3712]{1,0:T(8,128)(2,1)S(1)}, bf16[32,3712]{1,0:T(8,128)(2,1)S(1)}, u32[]{:S(2)}, u32[]{:S(2)}) collective-permute-start(bf16[32,3712]{1,0:T(8,128)(2,1)S(1)} %shard_map.64.refs_0_), channel_id=1, source_target_pairs={{0,4},{2,6},{4,0},{6,2},{8,12},{10,14},{12,8},{14,10},{1,5},{3,7},... | collective-permute-start | bytes 712712 | tf_op jit(solution)/shard_map/ppermute | solution.py:107
  4.7 13.4 %collective-permute-start.2 = (bf16[32,3712]{1,0:T(8,128)(2,1)S(1)}, bf16[32,3712]{1,0:T(8,128)(2,1)S(1)}, u32[]{:S(2)}, u32[]{:S(2)}) collective-permute-start(bf16[32,3712]{1,0:T(8,128)(2,1)S(1)} %shard_map.64.refs_0_), channel_id=1, source_target_pairs={{0,8},{2,10},{4,12},{6,14},{8,0},{10,2},{12,4},{14,6},{1,9},{3,11}... | collective-permute-start | bytes 712712 | tf_op jit(solution)/shard_map/ppermute | solution.py:107
  7.3 12.8 %collective-permute-start = (bf16[32,3712]{1,0:T(8,128)(2,1)S(1)}, bf16[32,3712]{1,0:T(8,128)(2,1)S(1)}, u32[]{:S(2)}, u32[]{:S(2)}) collective-permute-start(bf16[32,3712]{1,0:T(8,128)(2,1)S(1)} %shard_map.64.refs_0_), channel_id=1, source_target_pairs={{0,2},{2,0},{4,6},{6,4},{8,10},{10,8},{12,14},{14,12},{1,3},{3,1},... | collective-permute-start | bytes 712712 | tf_op jit(solution)/shard_map/ppermute | solution.py:111
  18.2 6.1 %collective-permute-start.5 = (bf16[32,3712]{1,0:T(8,128)(2,1)S(1)}, bf16[32,3712]{1,0:T(8,128)(2,1)S(1)}, u32[]{:S(2)}, u32[]{:S(2)}) collective-permute-start(bf16[32,3712]{1,0:T(8,128)(2,1)S(1)} %shard_map.66.refs_0_), channel_id=1, source_target_pairs={{0,4},{2,6},{4,0},{6,2},{8,12},{10,14},{12,8},{14,10},{1,5},{3,7},... | collective-permute-start | bytes 712712 | tf_op jit(solution)/shard_map/ppermute | solution.py:107
  18.6 8.9 %collective-permute-start.7 = (bf16[32,3712]{1,0:T(8,128)(2,1)S(1)}, bf16[32,3712]{1,0:T(8,128)(2,1)S(1)}, u32[]{:S(2)}, u32[]{:S(2)}) collective-permute-start(bf16[32,3712]{1,0:T(8,128)(2,1)S(1)} %shard_map.66.refs_0_), channel_id=1, source_target_pairs={{0,2},{2,0},{4,6},{6,4},{8,10},{10,8},{12,14},{14,12},{1,3},{3,1},... | collective-permute-start | bytes 712712 | tf_op jit(solution)/shard_map/ppermute | solution.py:111
  24.9 6.1 %collective-permute-start.6 = (bf16[32,3712]{1,0:T(8,128)(2,1)S(1)}, bf16[32,3712]{1,0:T(8,128)(2,1)S(1)}, u32[]{:S(2)}, u32[]{:S(2)}) collective-permute-start(bf16[32,3712]{1,0:T(8,128)(2,1)S(1)} %get-tuple-element.29), channel_id=1, source_target_pairs={{0,4},{2,6},{4,0},{6,2},{8,12},{10,14},{12,8},{14,10},{1,5},{3,7},... | collective-permute-start | bytes 712712 | tf_op jit(solution)/shard_map/ppermute | solution.py:107
  26.0 8.6 %collective-permute-start.10 = (bf16[32,3712]{1,0:T(8,128)(2,1)S(1)}, bf16[32,3712]{1,0:T(8,128)(2,1)S(1)}, u32[]{:S(2)}, u32[]{:S(2)}) collective-permute-start(bf16[32,3712]{1,0:T(8,128)(2,1)S(1)} %collective-permute-done.5.refs_1_.refs_0_), channel_id=1, source_target_pairs={{0,2},{2,0},{4,6},{6,4},{8,10},{10,8},{12,14},{14,12},{1,3},{3,1},... | collective-permute-start | bytes 712712 | tf_op jit(solution)/shard_map/ppermute | solution.py:111
  29.0 10.2 %collective-permute-start.9 = (bf16[32,3584]{1,0:T(8,128)(2,1)S(1)}, bf16[32,3584]{1,0:T(8,128)(2,1)S(1)}, u32[]{:S(2)}, u32[]{:S(2)}) collective-permute-start(bf16[32,3584]{1,0:T(8,128)(2,1)S(1)} %get-tuple-element.37), channel_id=1, source_target_pairs={{0,2},{2,0},{4,6},{6,4},{8,10},{10,8},{12,14},{14,12},{1,3},{3,1},... | collective-permute-start | bytes 688136 | tf_op jit(solution)/shard_map/ppermute | solution.py:111
  36.0 19.0 %copy-start = (bf16[2,32,3584]{2,1,0:T(8,128)(2,1)S(1)}, bf16[2,32,3584]{2,1,0:T(8,128)(2,1)}, u32[]{:S(2)}) copy-start(bf16[2,32,3584]{2,1,0:T(8,128)(2,1)} %hidden_ref.1) | copy-start | bytes 1376260
  36.0 6.1 %collective-permute-start.12 = (bf16[32,3584]{1,0:T(8,128)(2,1)S(1)}, bf16[32,3584]{1,0:T(8,128)(2,1)S(1)}, u32[]{:S(2)}, u32[]{:S(2)}) collective-permute-start(bf16[32,3584]{1,0:T(8,128)(2,1)S(1)} %get-tuple-element.43), channel_id=1, source_target_pairs={{0,2},{2,0},{4,6},{6,4},{8,10},{10,8},{12,14},{14,12},{1,3},{3,1},... | collective-permute-start | bytes 688136 | tf_op jit(solution)/shard_map/ppermute | solution.py:111
  37.7 8.2 %collective-permute-start.14 = (bf16[32,3584]{1,0:T(8,128)(2,1)S(1)}, bf16[32,3584]{1,0:T(8,128)(2,1)S(1)}, u32[]{:S(2)}, u32[]{:S(2)}) collective-permute-start(bf16[32,3584]{1,0:T(8,128)(2,1)S(1)} %get-tuple-element.48), channel_id=1, source_target_pairs={{0,4},{2,6},{4,0},{6,2},{8,12},{10,14},{12,8},{14,10},{1,5},{3,7},... | collective-permute-start | bytes 688136 | tf_op jit(solution)/shard_map/ppermute | solution.py:107
  39.2 12.5 %collective-permute-start.11 = (bf16[32,3584]{1,0:T(8,128)(2,1)S(1)}, bf16[32,3584]{1,0:T(8,128)(2,1)S(1)}, u32[]{:S(2)}, u32[]{:S(2)}) collective-permute-start(bf16[32,3584]{1,0:T(8,128)(2,1)S(1)} %get-tuple-element.40), channel_id=1, source_target_pairs={{0,8},{2,10},{4,12},{6,14},{8,0},{10,2},{12,4},{14,6},{1,9},{3,11}... | collective-permute-start | bytes 688136 | tf_op jit(solution)/shard_map/ppermute | solution.py:107
  40.0 11.7 %collective-permute-start.8 = (bf16[32,3584]{1,0:T(8,128)(2,1)S(1)}, bf16[32,3584]{1,0:T(8,128)(2,1)S(1)}, u32[]{:S(2)}, u32[]{:S(2)}) collective-permute-start(bf16[32,3584]{1,0:T(8,128)(2,1)S(1)} %get-tuple-element.35), channel_id=1, source_target_pairs={{0,4},{2,6},{4,0},{6,2},{8,12},{10,14},{12,8},{14,10},{1,5},{3,7},... | collective-permute-start | bytes 688136 | tf_op jit(solution)/shard_map/ppermute | solution.py:107
  42.2 12.2 %collective-permute-start.13 = (bf16[32,3584]{1,0:T(8,128)(2,1)S(1)}, bf16[32,3584]{1,0:T(8,128)(2,1)S(1)}, u32[]{:S(2)}, u32[]{:S(2)}) collective-permute-start(bf16[32,3584]{1,0:T(8,128)(2,1)S(1)} %get-tuple-element.45), channel_id=1, source_target_pairs={{0,12},{2,14},{4,8},{6,10},{8,4},{10,6},{12,0},{14,2},{1,13},{3,15... | collective-permute-start | bytes 688136 | tf_op jit(solution)/shard_map/ppermute | solution.py:107
  46.5 8.5 %collective-permute-start.15 = (bf16[32,3584]{1,0:T(8,128)(2,1)S(1)}, bf16[32,3584]{1,0:T(8,128)(2,1)S(1)}, u32[]{:S(2)}, u32[]{:S(2)}) collective-permute-start(bf16[32,3584]{1,0:T(8,128)(2,1)S(1)} %get-tuple-element.50), channel_id=1, source_target_pairs={{0,2},{2,0},{4,6},{6,4},{8,10},{10,8},{12,14},{14,12},{1,3},{3,1},... | collective-permute-start | bytes 688136 | tf_op jit(solution)/shard_map/ppermute | solution.py:111
  55.2 1.4 %collective-permute-start.16 = (bf16[32,1792]{1,0:T(8,128)(2,1)S(1)}, bf16[32,1792]{1,0:T(8,128)(2,1)S(1)}, u32[]{:S(2)}, u32[]{:S(2)}) collective-permute-start(bf16[32,1792]{1,0:T(8,128)(2,1)S(1)} %get-tuple-element.52), channel_id=1, source_target_pairs={{0,1},{1,0},{2,3},{3,2},{4,5},{5,4},{6,7},{7,6},{8,9},{9,8},{10,11... | collective-permute-start | bytes 344072 | tf_op jit(solution)/shard_map/ppermute | solution.py:102

commit v5 on v4

--- a/solution.py
+++ b/solution.py
@@ -111,7 +111,7 @@
     return lax.ppermute(value, "dev", [(i, i ^ 1) for i in range(n_dev)])
 
 
-def kernel_call(kernel, operands, outs, after=(), hbm=0, scratch=()):
+def kernel_call(kernel, operands, outs, after=(), hbm=0, scratch=(), end=True):
     vmem = pl.BlockSpec(memory_space=pltpu.VMEM)
     kept = [pl.BlockSpec(memory_space=pltpu.HBM)] * hbm + [vmem] * (len(operands) - hbm)
     count = len(operands)
@@ -119,14 +119,16 @@
     last = first + len(outs)
 
     def body(*refs):
-        kernel(*refs[:count], *refs[first:last], *refs[last + 1 :])
-        refs[last][...] = jnp.zeros(TOKEN, jnp.float32)
-
-    *given, token = pl.pallas_call(
+        kernel(*refs[:count], *refs[first:last], *refs[last + end :])
+        if end:
+            refs[last][...] = jnp.zeros(TOKEN, jnp.float32)
+
+    tokens = [(TOKEN, jnp.float32)] * end
+    given = pl.pallas_call(
         body,
         in_specs=kept + [pl.BlockSpec(memory_space=pl.ANY)] * len(after),
-        out_specs=[vmem] * (len(outs) + 1),
-        out_shape=[pltpu.VMEM(shape, dtype) for shape, dtype in [*outs, (TOKEN, jnp.float32)]],
+        out_specs=[vmem] * (len(outs) + end),
+        out_shape=[pltpu.VMEM(shape, dtype) for shape, dtype in [*outs, *tokens]],
         scratch_shapes=scratch,
         compiler_params=pltpu.CompilerParams(vmem_limit_bytes=VMEM_BYTES),
     )(
@@ -134,7 +136,7 @@
         *[in_vmem(v) for v in operands[hbm:]],
         *[in_vmem(v) for v in after],
     )
-    return given, token
+    return given[: len(outs)], given[-1] if end else None
 
 
 def pack_kernel(experts, core_ref, hidden_ref, gain_ref, routes_ref, weight_ref, block_ref):
@@ -230,14 +232,14 @@
     return kernel_call(kernel, [*blocks, *weights], outs, after)
 
 
-def add(terms, after=(), dtype=jnp.bfloat16):
+def add(terms, after=(), dtype=jnp.bfloat16, end=False):
     def kernel(*refs):
         total = refs[0][...].astype(jnp.float32)
         for ref in refs[1:-1]:
             total = total + ref[...].astype(jnp.float32)
         refs[-1][...] = total.astype(dtype)
 
-    (total,), token = kernel_call(kernel, terms, [(terms[0].shape, dtype)], after)
+    (total,), token = kernel_call(kernel, terms, [(terms[0].shape, dtype)], after, end=end)
     return total, token
 
 
@@ -303,9 +305,9 @@
     back_own, back_give = along(own[1], 1, experts), along(give[1], 1, experts)
     (own[3], give[3]), token = expert([column[3], beside[3]], weights, experts, [token])
     there[3] = across(give[3], n_dev)
-    total, token = add([own[2], there[2]], [token])
+    total, token = add([own[2], there[2]], [token], end=True)
     from_2 = along(total, 2, experts)
-    total, token = add([own[3], there[3]], [token])
+    total, token = add([own[3], there[3]], [token], end=True)
     from_3 = along(total, 3, experts)
     total, _ = add([give[0], back_give], [token])
     there[0] = across(total, n_dev)

time: 57.4 us -> 56.8 us (0.990)
  Pallas kernels: 11.9 us -> 9.64 us
  waiting for transfers between devices: 26.8 us -> 27.9 us
  starting transfers between devices: 18.2 us -> 18.8 us
    pallas_call x10, Pallas kernels: 9.48 us -> 7.2 us  [kernel_call(): pl.pallas_call(body, in_specs=kept + [pl.BlockSpec(memory_space=pl.ANY)]...]
    ppermute x8, waiting for transfers between devices: 21.6 us -> 23.2 us  [along(): return lax.ppermute(value, 'dev', pairs)]
    ppermute x8, starting transfers between devices: 10.8 us -> 11.4 us  [along(): return lax.ppermute(value, 'dev', pairs)]
  transfers between devices with their start and end apart: 17 -> 17, of which waited for: 11 -> 11; matrix products, arithmetic and copies ran while one was open for 0% -> 0% of each run, Pallas kernels for 20% -> 16%
where the time goes in v5:
time: 56.8 us; the launch traced here: 56.6 us
  waiting for transfers between devices  27.9 us (49%)
  starting transfers between devices  18.8 us (33%)
  Pallas kernels  9.64 us (17%)
    ppermute x8, waiting for transfers between devices, along(): return lax.ppermute(value, 'dev', pairs)  23.2 us
    ppermute x8, starting transfers between devices, along(): return lax.ppermute(value, 'dev', pairs)  11.4 us
    pallas_call x10, Pallas kernels, kernel_call(): pl.pallas_call(body, in_specs=kept + [pl.BlockSpec(memory_space=pl.ANY)]...  7.2 us
    ppermute x6, starting transfers between devices, across(): return lax.ppermute(value, 'dev', [(i, i ^ 1) for i in range(n_dev)])  6.84 us
    ppermute x6, waiting for transfers between devices, across(): return lax.ppermute(value, 'dev', [(i, i ^ 1) for i in range(n_dev)])  4.07 us
    pallas_call x2, Pallas kernels, place(): pl.pallas_call(kernel, in_specs=[pl.BlockSpec(memory_space=pltpu.VMEM)] +...  1.32 us
  transfers between devices with their start and end apart: 17, of which 11 were waited for; matrix products, arithmetic and copies ran while one was open for 0% of the time, Pallas kernels for 16%

profile of v5, /device:TPU:0, one launch (start us, length us, event | category | flops | bytes accessed | tf_op | source)
XLA Modules:
  0.0 56.6 jit_solution(4836400811336888686)
XLA Ops:
  0.0 0.5 collective-permute-start.4
  0.5 1.1 %shard_map.64.refs_0_ = bf16[32,3712]{1,0:T(8,128)(2,1)S(1)} custom-call(s32[1]{0:T(128)} %bitcast.1.core_ref, bf16[2,32,3584]{2,1,0:T(8,128)(2,1)} %hidden_ref.1, f32[3584]{0:T(1024)} %gain_ref.1, s32[2,2,32]{2,1,0:T(2,128)} %bitcast.6, f32[2,2,32]{2,1,0:T(2,128)} %bitcast.7), custom_call_target="tpu_custom_call" | custom-call | tf_op jit(solution)/shard_map/pallas_call | solution.py:162
  1.6 3.1 %collective-permute-start.1 = (bf16[32,3712]{1,0:T(8,128)(2,1)S(1)}, bf16[32,3712]{1,0:T(8,128)(2,1)S(1)}, u32[]{:S(2)}, u32[]{:S(2)}) collective-permute-start(bf16[32,3712]{1,0:T(8,128)(2,1)S(1)} %shard_map.64.refs_0_), channel_id=1, source_target_pairs={{0,4},{2,6},{4,0},{6,2},{8,12},{10,14},{12,8},{14,10},{1,5},{3,7},... | collective-permute-start | bytes 712712 | tf_op jit(solution)/shard_map/ppermute | solution.py:107
  4.7 2.6 %collective-permute-start.2 = (bf16[32,3712]{1,0:T(8,128)(2,1)S(1)}, bf16[32,3712]{1,0:T(8,128)(2,1)S(1)}, u32[]{:S(2)}, u32[]{:S(2)}) collective-permute-start(bf16[32,3712]{1,0:T(8,128)(2,1)S(1)} %shard_map.64.refs_0_), channel_id=1, source_target_pairs={{0,8},{2,10},{4,12},{6,14},{8,0},{10,2},{12,4},{14,6},{1,9},{3,11}... | collective-permute-start | bytes 712712 | tf_op jit(solution)/shard_map/ppermute | solution.py:107
  7.3 1.5 %collective-permute-start = (bf16[32,3712]{1,0:T(8,128)(2,1)S(1)}, bf16[32,3712]{1,0:T(8,128)(2,1)S(1)}, u32[]{:S(2)}, u32[]{:S(2)}) collective-permute-start(bf16[32,3712]{1,0:T(8,128)(2,1)S(1)} %shard_map.64.refs_0_), channel_id=1, source_target_pairs={{0,2},{2,0},{4,6},{6,4},{8,10},{10,8},{12,14},{14,12},{1,3},{3,1},... | collective-permute-start | bytes 712712 | tf_op jit(solution)/shard_map/ppermute | solution.py:111
  8.8 2.6 %shard_map.65 = (bf16[3584,256]{1,0:T(8,128)(2,1)S(1)}, bf16[256,3584]{1,0:T(8,128)(2,1)S(1)}, bf16[256,3584]{1,0:T(8,128)(2,1)S(1)}, f32[8,128]{1,0:T(8,128)S(1)}) custom-call(bf16[3584,256]{1,0:T(8,128)(2,1)} %refs_0_.1, bf16[256,3584]{1,0:T(8,128)(2,1)} %refs_1_.1, bf16[256,3584]{1,0:T(8,128)(2,1)} %collective-permute-done.3.refs_2_, ...), custom_call_target="tpu_custom_call" | custom-call | tf_op jit(solution)/shard_map/pallas_call | solution.py:127
  11.5 4.2 %collective-permute-done.1.refs_2_ = bf16[32,3712]{1,0:T(8,128)(2,1)S(1)} collective-permute-done((bf16[32,3712]{1,0:T(8,128)(2,1)S(1)}, bf16[32,3712]{1,0:T(8,128)(2,1)S(1)}, u32[]{:S(2)}, u32[]{:S(2)}) %collective-permute-start.1) | collective-permute-done | bytes 237600 | tf_op jit(solution)/shard_map/ppermute | solution.py:107
  15.7 2.5 %collective-permute-done.2.refs_0_ = bf16[32,3712]{1,0:T(8,128)(2,1)S(1)} collective-permute-done((bf16[32,3712]{1,0:T(8,128)(2,1)S(1)}, bf16[32,3712]{1,0:T(8,128)(2,1)S(1)}, u32[]{:S(2)}, u32[]{:S(2)}) %collective-permute-start.2) | collective-permute-done | bytes 237600 | tf_op jit(solution)/shard_map/ppermute | solution.py:107
  18.2 0.4 collective-permute-start.5
  18.6 1.5 %collective-permute-start.7 = (bf16[32,3712]{1,0:T(8,128)(2,1)S(1)}, bf16[32,3712]{1,0:T(8,128)(2,1)S(1)}, u32[]{:S(2)}, u32[]{:S(2)}) collective-permute-start(bf16[32,3712]{1,0:T(8,128)(2,1)S(1)} %shard_map.66.refs_0_), channel_id=1, source_target_pairs={{0,2},{2,0},{4,6},{6,4},{8,10},{10,8},{12,14},{14,12},{1,3},{3,1},... | collective-permute-start | bytes 712712 | tf_op jit(solution)/shard_map/ppermute | solution.py:111
  20.1 4.2 %collective-permute-done.5.refs_1_.refs_0_ = bf16[32,3712]{1,0:T(8,128)(2,1)S(1)} collective-permute-done((bf16[32,3712]{1,0:T(8,128)(2,1)S(1)}, bf16[32,3712]{1,0:T(8,128)(2,1)S(1)}, u32[]{:S(2)}, u32[]{:S(2)}) %collective-permute-start.5) | collective-permute-done | bytes 237600 | tf_op jit(solution)/shard_map/ppermute | solution.py:107
  24.3 1.2 %collective-permute-start.6 = (bf16[32,3712]{1,0:T(8,128)(2,1)S(1)}, bf16[32,3712]{1,0:T(8,128)(2,1)S(1)}, u32[]{:S(2)}, u32[]{:S(2)}) collective-permute-start(bf16[32,3712]{1,0:T(8,128)(2,1)S(1)} %shard_map.67), channel_id=1, source_target_pairs={{0,4},{2,6},{4,0},{6,2},{8,12},{10,14},{12,8},{14,10},{1,5},{3,7},... | collective-permute-start | bytes 712712 | tf_op jit(solution)/shard_map/ppermute | solution.py:107
  25.5 1.5 %collective-permute-start.10 = (bf16[32,3712]{1,0:T(8,128)(2,1)S(1)}, bf16[32,3712]{1,0:T(8,128)(2,1)S(1)}, u32[]{:S(2)}, u32[]{:S(2)}) collective-permute-start(bf16[32,3712]{1,0:T(8,128)(2,1)S(1)} %collective-permute-done.5.refs_1_.refs_0_), channel_id=1, source_target_pairs={{0,2},{2,0},{4,6},{6,4},{8,10},{10,8},{12,14},{14,12},{1,3},{3,1},... | collective-permute-start | bytes 712712 | tf_op jit(solution)/shard_map/ppermute | solution.py:111
  27.0 1.4 %shard_map.68 = (bf16[32,3584]{1,0:T(8,128)(2,1)S(1)}, bf16[32,3584]{1,0:T(8,128)(2,1)S(1)}, f32[8,128]{1,0:T(8,128)S(1)}) custom-call(bf16[32,3712]{1,0:T(8,128)(2,1)S(1)} %shard_map.66.refs_0_, bf16[32,3712]{1,0:T(8,128)(2,1)S(1)} %collective-permute-done.7.refs_1_, bf16[3584,256]{1,0:T(8,128)(2,1)S(1)} %get-tuple-element.25.refs_2_.refs_4_, ...), custom_call_target="tpu_custom_call" | custom-call | tf_op jit(solution)/shard_map/pallas_call | solution.py:127
  28.4 0.6 %collective-permute-start.9 = (bf16[32,3584]{1,0:T(8,128)(2,1)S(1)}, bf16[32,3584]{1,0:T(8,128)(2,1)S(1)}, u32[]{:S(2)}, u32[]{:S(2)}) collective-permute-start(bf16[32,3584]{1,0:T(8,128)(2,1)S(1)} %get-tuple-element.32), channel_id=1, source_target_pairs={{0,2},{2,0},{4,6},{6,4},{8,10},{10,8},{12,14},{14,12},{1,3},{3,1},... | collective-permute-start | bytes 688136 | tf_op jit(solution)/shard_map/ppermute | solution.py:111
  29.0 1.5 %collective-permute-done.6.refs_3_ = bf16[32,3712]{1,0:T(8,128)(2,1)S(1)} collective-permute-done((bf16[32,3712]{1,0:T(8,128)(2,1)S(1)}, bf16[32,3712]{1,0:T(8,128)(2,1)S(1)}, u32[]{:S(2)}, u32[]{:S(2)}) %collective-permute-start.6) | collective-permute-done | bytes 237600 | tf_op jit(solution)/shard_map/ppermute | solution.py:107
  30.5 1.4 %shard_map.69 = (bf16[32,3584]{1,0:T(8,128)(2,1)S(1)}, bf16[32,3584]{1,0:T(8,128)(2,1)S(1)}, bf16[32,3584]{1,0:T(8,128)(2,1)S(1)}, bf16[32,3584]{1,0:T(8,128)(2,1)S(1)}, f32[8,128]{1,0:T(8,128)S(1)}) custom-call(bf16[32,3712]{1,0:T(8,128)(2,1)S(1)} %shard_map.64.refs_0_, bf16[32,3712]{1,0:T(8,128)(2,1)S(1)} %collective-permute-done.refs_0_.refs_1_, ...), custom_call_target="tpu_custom_call" | custom-call | tf_op jit(solution)/shard_map/pallas_call | solution.py:127
  31.9 2.2 %collective-permute-done.10.refs_1_ = bf16[32,3712]{1,0:T(8,128)(2,1)S(1)} collective-permute-done((bf16[32,3712]{1,0:T(8,128)(2,1)S(1)}, bf16[32,3712]{1,0:T(8,128)(2,1)S(1)}, u32[]{:S(2)}, u32[]{:S(2)}) %collective-permute-start.10) | collective-permute-done | bytes 237600 | tf_op jit(solution)/shard_map/ppermute | solution.py:111
  34.1 1.4 %shard_map.70 = (bf16[32,3584]{1,0:T(8,128)(2,1)S(1)}, bf16[32,3584]{1,0:T(8,128)(2,1)S(1)}, f32[8,128]{1,0:T(8,128)S(1)}) custom-call(bf16[32,3712]{1,0:T(8,128)(2,1)S(1)} %collective-permute-done.5.refs_1_.refs_0_, bf16[32,3712]{1,0:T(8,128)(2,1)S(1)} %collective-permute-done.10.refs_1_, bf16[3584,256]{1,0:T(8,128)(2,1)S(1)} %get-tuple-element.25.refs_2_.refs_4_, ...), custom_call_target="tpu_custom_call" | custom-call | tf_op jit(solution)/shard_map/pallas_call | solution.py:127
  35.5 1.7 %collective-permute-start.12 = (bf16[32,3584]{1,0:T(8,128)(2,1)S(1)}, bf16[32,3584]{1,0:T(8,128)(2,1)S(1)}, u32[]{:S(2)}, u32[]{:S(2)}) collective-permute-start(bf16[32,3584]{1,0:T(8,128)(2,1)S(1)} %get-tuple-element.37), channel_id=1, source_target_pairs={{0,2},{2,0},{4,6},{6,4},{8,10},{10,8},{12,14},{14,12},{1,3},{3,1},... | collective-permute-start | bytes 688136 | tf_op jit(solution)/shard_map/ppermute | solution.py:111
  37.2 1.4 %collective-permute-done.9.refs_1_ = bf16[32,3584]{1,0:T(8,128)(2,1)S(1)} collective-permute-done((bf16[32,3584]{1,0:T(8,128)(2,1)S(1)}, bf16[32,3584]{1,0:T(8,128)(2,1)S(1)}, u32[]{:S(2)}, u32[]{:S(2)}) %collective-permute-start.9) | collective-permute-done | bytes 229408 | tf_op jit(solution)/shard_map/ppermute | solution.py:111
  38.7 1.3 %collective-permute-start.11 = (bf16[32,3584]{1,0:T(8,128)(2,1)S(1)}, bf16[32,3584]{1,0:T(8,128)(2,1)S(1)}, u32[]{:S(2)}, u32[]{:S(2)}) collective-permute-start(bf16[32,3584]{1,0:T(8,128)(2,1)S(1)} %get-tuple-element.35), channel_id=1, source_target_pairs={{0,8},{2,10},{4,12},{6,14},{8,0},{10,2},{12,4},{14,6},{1,9},{3,11}... | collective-permute-start | bytes 688136 | tf_op jit(solution)/shard_map/ppermute | solution.py:107
  40.0 1.1 %collective-permute-start.8 = (bf16[32,3584]{1,0:T(8,128)(2,1)S(1)}, bf16[32,3584]{1,0:T(8,128)(2,1)S(1)}, u32[]{:S(2)}, u32[]{:S(2)}) collective-permute-start(bf16[32,3584]{1,0:T(8,128)(2,1)S(1)} %get-tuple-element.30), channel_id=1, source_target_pairs={{0,4},{2,6},{4,0},{6,2},{8,12},{10,14},{12,8},{14,10},{1,5},{3,7},... | collective-permute-start | bytes 688136 | tf_op jit(solution)/shard_map/ppermute | solution.py:107
  41.1 0.5 collective-permute-done.12.refs_1_
  41.6 1.6 %collective-permute-start.13 = (bf16[32,3584]{1,0:T(8,128)(2,1)S(1)}, bf16[32,3584]{1,0:T(8,128)(2,1)S(1)}, u32[]{:S(2)}, u32[]{:S(2)}) collective-permute-start(bf16[32,3584]{1,0:T(8,128)(2,1)S(1)} %get-tuple-element.39), channel_id=1, source_target_pairs={{0,12},{2,14},{4,8},{6,10},{8,4},{10,6},{12,0},{14,2},{1,13},{3,15... | collective-permute-start | bytes 688136 | tf_op jit(solution)/shard_map/ppermute | solution.py:107
  43.3 3.8 %collective-permute-done.14.refs_1_ = bf16[32,3584]{1,0:T(8,128)(2,1)S(1)} collective-permute-done((bf16[32,3584]{1,0:T(8,128)(2,1)S(1)}, bf16[32,3584]{1,0:T(8,128)(2,1)S(1)}, u32[]{:S(2)}, u32[]{:S(2)}) %collective-permute-start.14) | collective-permute-done | bytes 229408 | tf_op jit(solution)/shard_map/ppermute | solution.py:107
  47.2 4.5 %collective-permute-done.11.refs_2_ = bf16[32,3584]{1,0:T(8,128)(2,1)S(1)} collective-permute-done((bf16[32,3584]{1,0:T(8,128)(2,1)S(1)}, bf16[32,3584]{1,0:T(8,128)(2,1)S(1)}, u32[]{:S(2)}, u32[]{:S(2)}) %collective-permute-start.11) | collective-permute-done | bytes 229408 | tf_op jit(solution)/shard_map/ppermute | solution.py:107
  51.7 0.1 shard_map.72.refs_0_
  51.8 2.6 %collective-permute-done.13.refs_1_ = bf16[32,3584]{1,0:T(8,128)(2,1)S(1)} collective-permute-done((bf16[32,3584]{1,0:T(8,128)(2,1)S(1)}, bf16[32,3584]{1,0:T(8,128)(2,1)S(1)}, u32[]{:S(2)}, u32[]{:S(2)}) %collective-permute-start.13) | collective-permute-done | bytes 229408 | tf_op jit(solution)/shard_map/ppermute | solution.py:107
  54.6 0.7 %shard_map.76.refs_0_ = bf16[2,32,1792]{2,1,0:T(8,128)(2,1)} custom-call(bf16[32,1792]{1,0:T(8,128)(2,1)S(1)} %get-tuple-element.43.value_ref), custom_call_target="tpu_custom_call" | custom-call | tf_op jit(solution)/shard_map/pallas_call | solution.py:257
  55.3 0.6 %collective-permute-done.16.value_ref = bf16[32,1792]{1,0:T(8,128)(2,1)S(1)} collective-permute-done((bf16[32,1792]{1,0:T(8,128)(2,1)S(1)}, bf16[32,1792]{1,0:T(8,128)(2,1)S(1)}, u32[]{:S(2)}, u32[]{:S(2)}) %collective-permute-start.16) | collective-permute-done | bytes 114720 | tf_op jit(solution)/shard_map/ppermute | solution.py:102
  55.9 0.7 %shard_map.77 = bf16[2,32,1792]{2,1,0:T(8,128)(2,1)} custom-call(bf16[32,1792]{1,0:T(8,128)(2,1)S(1)} %collective-permute-done.16.value_ref, bf16[2,32,1792]{2,1,0:T(8,128)(2,1)} %shard_map.76.refs_0_), custom_call_target="tpu_custom_call", output_to_operand_aliasing={{}: (1, {})} | custom-call | tf_op jit(solution)/shard_map/pallas_call | solution.py:257
  (20 shorter events, 0.6 us)
Async XLA Ops:
  0.0 8.8 %collective-permute-start.4 = (bf16[3584,256]{1,0:T(8,128)(2,1)}, bf16[3584,256]{1,0:T(8,128)(2,1)S(1)}, u32[]{:S(2)}, u32[]{:S(2)}) collective-permute-start(bf16[3584,256]{1,0:T(8,128)(2,1)} %refs_0_.1), channel_id=1, source_target_pairs={{0,1},{1,0},{2,3},{3,2},{4,5},{5,4},{6,7},{7,6},{8,9},{9,8},{10,11... | collective-permute-start | bytes 5505032 | tf_op jit(solution)/shard_map/ppermute | solution.py:102
  0.5 8.4 %collective-permute-start.3 = (bf16[256,3584]{1,0:T(8,128)(2,1)}, bf16[256,3584]{1,0:T(8,128)(2,1)}, u32[]{:S(2)}, u32[]{:S(2)}) collective-permute-start(bf16[256,3584]{1,0:T(8,128)(2,1)} %refs_1_.1), channel_id=1, source_target_pairs={{0,1},{1,0},{2,3},{3,2},{4,5},{5,4},{6,7},{7,6},{8,9},{9,8},{10,11... | collective-permute-start | bytes 5505032 | tf_op jit(solution)/shard_map/ppermute | solution.py:102
  1.6 14.0 %collective-permute-start.1 = (bf16[32,3712]{1,0:T(8,128)(2,1)S(1)}, bf16[32,3712]{1,0:T(8,128)(2,1)S(1)}, u32[]{:S(2)}, u32[]{:S(2)}) collective-permute-start(bf16[32,3712]{1,0:T(8,128)(2,1)S(1)} %shard_map.64.refs_0_), channel_id=1, source_target_pairs={{0,4},{2,6},{4,0},{6,2},{8,12},{10,14},{12,8},{14,10},{1,5},{3,7},... | collective-permute-start | bytes 712712 | tf_op jit(solution)/shard_map/ppermute | solution.py:107
  4.7 13.4 %collective-permute-start.2 = (bf16[32,3712]{1,0:T(8,128)(2,1)S(1)}, bf16[32,3712]{1,0:T(8,128)(2,1)S(1)}, u32[]{:S(2)}, u32[]{:S(2)}) collective-permute-start(bf16[32,3712]{1,0:T(8,128)(2,1)S(1)} %shard_map.64.refs_0_), channel_id=1, source_target_pairs={{0,8},{2,10},{4,12},{6,14},{8,0},{10,2},{12,4},{14,6},{1,9},{3,11}... | collective-permute-start | bytes 712712 | tf_op jit(solution)/shard_map/ppermute | solution.py:107
  7.3 12.8 %collective-permute-start = (bf16[32,3712]{1,0:T(8,128)(2,1)S(1)}, bf16[32,3712]{1,0:T(8,128)(2,1)S(1)}, u32[]{:S(2)}, u32[]{:S(2)}) collective-permute-start(bf16[32,3712]{1,0:T(8,128)(2,1)S(1)} %shard_map.64.refs_0_), channel_id=1, source_target_pairs={{0,2},{2,0},{4,6},{6,4},{8,10},{10,8},{12,14},{14,12},{1,3},{3,1},... | collective-permute-start | bytes 712712 | tf_op jit(solution)/shard_map/ppermute | solution.py:111
  18.2 6.1 %collective-permute-start.5 = (bf16[32,3712]{1,0:T(8,128)(2,1)S(1)}, bf16[32,3712]{1,0:T(8,128)(2,1)S(1)}, u32[]{:S(2)}, u32[]{:S(2)}) collective-permute-start(bf16[32,3712]{1,0:T(8,128)(2,1)S(1)} %shard_map.66.refs_0_), channel_id=1, source_target_pairs={{0,4},{2,6},{4,0},{6,2},{8,12},{10,14},{12,8},{14,10},{1,5},{3,7},... | collective-permute-start | bytes 712712 | tf_op jit(solution)/shard_map/ppermute | solution.py:107
  18.6 8.4 %collective-permute-start.7 = (bf16[32,3712]{1,0:T(8,128)(2,1)S(1)}, bf16[32,3712]{1,0:T(8,128)(2,1)S(1)}, u32[]{:S(2)}, u32[]{:S(2)}) collective-permute-start(bf16[32,3712]{1,0:T(8,128)(2,1)S(1)} %shard_map.66.refs_0_), channel_id=1, source_target_pairs={{0,2},{2,0},{4,6},{6,4},{8,10},{10,8},{12,14},{14,12},{1,3},{3,1},... | collective-permute-start | bytes 712712 | tf_op jit(solution)/shard_map/ppermute | solution.py:111
  24.3 6.2 %collective-permute-start.6 = (bf16[32,3712]{1,0:T(8,128)(2,1)S(1)}, bf16[32,3712]{1,0:T(8,128)(2,1)S(1)}, u32[]{:S(2)}, u32[]{:S(2)}) collective-permute-start(bf16[32,3712]{1,0:T(8,128)(2,1)S(1)} %shard_map.67), channel_id=1, source_target_pairs={{0,4},{2,6},{4,0},{6,2},{8,12},{10,14},{12,8},{14,10},{1,5},{3,7},... | collective-permute-start | bytes 712712 | tf_op jit(solution)/shard_map/ppermute | solution.py:107
  25.5 8.6 %collective-permute-start.10 = (bf16[32,3712]{1,0:T(8,128)(2,1)S(1)}, bf16[32,3712]{1,0:T(8,128)(2,1)S(1)}, u32[]{:S(2)}, u32[]{:S(2)}) collective-permute-start(bf16[32,3712]{1,0:T(8,128)(2,1)S(1)} %collective-permute-done.5.refs_1_.refs_0_), channel_id=1, source_target_pairs={{0,2},{2,0},{4,6},{6,4},{8,10},{10,8},{12,14},{14,12},{1,3},{3,1},... | collective-permute-start | bytes 712712 | tf_op jit(solution)/shard_map/ppermute | solution.py:111
  28.4 10.2 %collective-permute-start.9 = (bf16[32,3584]{1,0:T(8,128)(2,1)S(1)}, bf16[32,3584]{1,0:T(8,128)(2,1)S(1)}, u32[]{:S(2)}, u32[]{:S(2)}) collective-permute-start(bf16[32,3584]{1,0:T(8,128)(2,1)S(1)} %get-tuple-element.32), channel_id=1, source_target_pairs={{0,2},{2,0},{4,6},{6,4},{8,10},{10,8},{12,14},{14,12},{1,3},{3,1},... | collective-permute-start | bytes 688136 | tf_op jit(solution)/shard_map/ppermute | solution.py:111
  35.5 6.1 %collective-permute-start.12 = (bf16[32,3584]{1,0:T(8,128)(2,1)S(1)}, bf16[32,3584]{1,0:T(8,128)(2,1)S(1)}, u32[]{:S(2)}, u32[]{:S(2)}) collective-permute-start(bf16[32,3584]{1,0:T(8,128)(2,1)S(1)} %get-tuple-element.37), channel_id=1, source_target_pairs={{0,2},{2,0},{4,6},{6,4},{8,10},{10,8},{12,14},{14,12},{1,3},{3,1},... | collective-permute-start | bytes 688136 | tf_op jit(solution)/shard_map/ppermute | solution.py:111
  37.2 9.8 %collective-permute-start.14 = (bf16[32,3584]{1,0:T(8,128)(2,1)S(1)}, bf16[32,3584]{1,0:T(8,128)(2,1)S(1)}, u32[]{:S(2)}, u32[]{:S(2)}) collective-permute-start(bf16[32,3584]{1,0:T(8,128)(2,1)S(1)} %get-tuple-element.41), channel_id=1, source_target_pairs={{0,4},{2,6},{4,0},{6,2},{8,12},{10,14},{12,8},{14,10},{1,5},{3,7},... | collective-permute-start | bytes 688136 | tf_op jit(solution)/shard_map/ppermute | solution.py:107
  38.7 15.7 %copy-start = (bf16[2,32,3584]{2,1,0:T(8,128)(2,1)S(1)}, bf16[2,32,3584]{2,1,0:T(8,128)(2,1)}, u32[]{:S(2)}) copy-start(bf16[2,32,3584]{2,1,0:T(8,128)(2,1)} %hidden_ref.1) | copy-start | bytes 1376260
  38.7 13.0 %collective-permute-start.11 = (bf16[32,3584]{1,0:T(8,128)(2,1)S(1)}, bf16[32,3584]{1,0:T(8,128)(2,1)S(1)}, u32[]{:S(2)}, u32[]{:S(2)}) collective-permute-start(bf16[32,3584]{1,0:T(8,128)(2,1)S(1)} %get-tuple-element.35), channel_id=1, source_target_pairs={{0,8},{2,10},{4,12},{6,14},{8,0},{10,2},{12,4},{14,6},{1,9},{3,11}... | collective-permute-start | bytes 688136 | tf_op jit(solution)/shard_map/ppermute | solution.py:107
  40.0 11.7 %collective-permute-start.8 = (bf16[32,3584]{1,0:T(8,128)(2,1)S(1)}, bf16[32,3584]{1,0:T(8,128)(2,1)S(1)}, u32[]{:S(2)}, u32[]{:S(2)}) collective-permute-start(bf16[32,3584]{1,0:T(8,128)(2,1)S(1)} %get-tuple-element.30), channel_id=1, source_target_pairs={{0,4},{2,6},{4,0},{6,2},{8,12},{10,14},{12,8},{14,10},{1,5},{3,7},... | collective-permute-start | bytes 688136 | tf_op jit(solution)/shard_map/ppermute | solution.py:107
  41.6 12.7 %collective-permute-start.13 = (bf16[32,3584]{1,0:T(8,128)(2,1)S(1)}, bf16[32,3584]{1,0:T(8,128)(2,1)S(1)}, u32[]{:S(2)}, u32[]{:S(2)}) collective-permute-start(bf16[32,3584]{1,0:T(8,128)(2,1)S(1)} %get-tuple-element.39), channel_id=1, source_target_pairs={{0,12},{2,14},{4,8},{6,10},{8,4},{10,6},{12,0},{14,2},{1,13},{3,15... | collective-permute-start | bytes 688136 | tf_op jit(solution)/shard_map/ppermute | solution.py:107
  47.1 7.3 %collective-permute-start.15 = (bf16[32,3584]{1,0:T(8,128)(2,1)S(1)}, bf16[32,3584]{1,0:T(8,128)(2,1)S(1)}, u32[]{:S(2)}, u32[]{:S(2)}) collective-permute-start(bf16[32,3584]{1,0:T(8,128)(2,1)S(1)} %shard_map.75), channel_id=1, source_target_pairs={{0,2},{2,0},{4,6},{6,4},{8,10},{10,8},{12,14},{14,12},{1,3},{3,1},... | collective-permute-start | bytes 688136 | tf_op jit(solution)/shard_map/ppermute | solution.py:111
  54.5 1.4 %collective-permute-start.16 = (bf16[32,1792]{1,0:T(8,128)(2,1)S(1)}, bf16[32,1792]{1,0:T(8,128)(2,1)S(1)}, u32[]{:S(2)}, u32[]{:S(2)}) collective-permute-start(bf16[32,1792]{1,0:T(8,128)(2,1)S(1)} %get-tuple-element.44), channel_id=1, source_target_pairs={{0,1},{1,0},{2,3},{3,2},{4,5},{5,4},{6,7},{7,6},{8,9},{9,8},{10,11... | collective-permute-start | bytes 344072 | tf_op jit(solution)/shard_map/ppermute | solution.py:102

commit v6 on v5

--- a/solution.py
+++ b/solution.py
@@ -312,8 +312,7 @@
     total, _ = add([give[0], back_give], [token])
     there[0] = across(total, n_dev)
 
-    partial, _ = add([own[0], back_own, from_2], dtype=jnp.float32)
-    partial, _ = add([partial, from_3], dtype=jnp.float32)
+    partial, _ = add([own[0], back_own, from_2, from_3], dtype=jnp.float32)
     half = hidden.shape[2] // 2
     result = lax.dynamic_index_in_dim(hidden, core, 0, keepdims=False).astype(jnp.float32)
     result = (result + partial + there[0].astype(jnp.float32)).astype(jnp.bfloat16)

time: 56.8 us -> 56.9 us (level)
    pallas_call x10 -> x9, Pallas kernels: 7.2 us -> 7.19 us  [kernel_call(): pl.pallas_call(body, in_specs=kept + [pl.BlockSpec(memory_space=pl.ANY)]...]
where the time goes in v6:
time: 56.9 us; the launch traced here: 56.6 us
  waiting for transfers between devices  28 us (49%)
  starting transfers between devices  18.8 us (33%)
  Pallas kernels  9.63 us (17%)
    ppermute x8, waiting for transfers between devices, along(): return lax.ppermute(value, 'dev', pairs)  23.3 us
    ppermute x8, starting transfers between devices, along(): return lax.ppermute(value, 'dev', pairs)  11.4 us
    pallas_call x9, Pallas kernels, kernel_call(): pl.pallas_call(body, in_specs=kept + [pl.BlockSpec(memory_space=pl.ANY)]...  7.19 us
    ppermute x6, starting transfers between devices, across(): return lax.ppermute(value, 'dev', [(i, i ^ 1) for i in range(n_dev)])  6.84 us
    ppermute x6, waiting for transfers between devices, across(): return lax.ppermute(value, 'dev', [(i, i ^ 1) for i in range(n_dev)])  4.08 us
    pallas_call x2, Pallas kernels, place(): pl.pallas_call(kernel, in_specs=[pl.BlockSpec(memory_space=pltpu.VMEM)] +...  1.32 us
  transfers between devices with their start and end apart: 17, of which 11 were waited for; matrix products, arithmetic and copies ran while one was open for 0% of the time, Pallas kernels for 16%

profile of v6, /device:TPU:0, one launch (start us, length us, event | category | flops | bytes accessed | tf_op | source)
XLA Modules:
  0.0 56.6 jit_solution(1084018949310928836)
XLA Ops:
  0.0 0.5 collective-permute-start.4
  0.5 1.1 %shard_map.64.refs_0_ = bf16[32,3712]{1,0:T(8,128)(2,1)S(1)} custom-call(s32[1]{0:T(128)} %bitcast.1.core_ref, bf16[2,32,3584]{2,1,0:T(8,128)(2,1)} %hidden_ref.1, f32[3584]{0:T(1024)} %gain_ref.1, s32[2,2,32]{2,1,0:T(2,128)} %bitcast.6, f32[2,2,32]{2,1,0:T(2,128)} %bitcast.7), custom_call_target="tpu_custom_call" | custom-call | tf_op jit(solution)/shard_map/pallas_call | solution.py:162
  1.6 3.1 %collective-permute-start.1 = (bf16[32,3712]{1,0:T(8,128)(2,1)S(1)}, bf16[32,3712]{1,0:T(8,128)(2,1)S(1)}, u32[]{:S(2)}, u32[]{:S(2)}) collective-permute-start(bf16[32,3712]{1,0:T(8,128)(2,1)S(1)} %shard_map.64.refs_0_), channel_id=1, source_target_pairs={{0,4},{2,6},{4,0},{6,2},{8,12},{10,14},{12,8},{14,10},{1,5},{3,7},... | collective-permute-start | bytes 712712 | tf_op jit(solution)/shard_map/ppermute | solution.py:107
  4.7 2.6 %collective-permute-start.2 = (bf16[32,3712]{1,0:T(8,128)(2,1)S(1)}, bf16[32,3712]{1,0:T(8,128)(2,1)S(1)}, u32[]{:S(2)}, u32[]{:S(2)}) collective-permute-start(bf16[32,3712]{1,0:T(8,128)(2,1)S(1)} %shard_map.64.refs_0_), channel_id=1, source_target_pairs={{0,8},{2,10},{4,12},{6,14},{8,0},{10,2},{12,4},{14,6},{1,9},{3,11}... | collective-permute-start | bytes 712712 | tf_op jit(solution)/shard_map/ppermute | solution.py:107
  7.3 1.5 %collective-permute-start = (bf16[32,3712]{1,0:T(8,128)(2,1)S(1)}, bf16[32,3712]{1,0:T(8,128)(2,1)S(1)}, u32[]{:S(2)}, u32[]{:S(2)}) collective-permute-start(bf16[32,3712]{1,0:T(8,128)(2,1)S(1)} %shard_map.64.refs_0_), channel_id=1, source_target_pairs={{0,2},{2,0},{4,6},{6,4},{8,10},{10,8},{12,14},{14,12},{1,3},{3,1},... | collective-permute-start | bytes 712712 | tf_op jit(solution)/shard_map/ppermute | solution.py:111
  8.8 2.6 %shard_map.65 = (bf16[3584,256]{1,0:T(8,128)(2,1)S(1)}, bf16[256,3584]{1,0:T(8,128)(2,1)S(1)}, bf16[256,3584]{1,0:T(8,128)(2,1)S(1)}, f32[8,128]{1,0:T(8,128)S(1)}) custom-call(bf16[3584,256]{1,0:T(8,128)(2,1)} %refs_0_.1, bf16[256,3584]{1,0:T(8,128)(2,1)} %refs_1_.1, bf16[256,3584]{1,0:T(8,128)(2,1)} %collective-permute-done.3.refs_2_, ...), custom_call_target="tpu_custom_call" | custom-call | tf_op jit(solution)/shard_map/pallas_call | solution.py:127
  11.5 4.2 %collective-permute-done.1.refs_2_ = bf16[32,3712]{1,0:T(8,128)(2,1)S(1)} collective-permute-done((bf16[32,3712]{1,0:T(8,128)(2,1)S(1)}, bf16[32,3712]{1,0:T(8,128)(2,1)S(1)}, u32[]{:S(2)}, u32[]{:S(2)}) %collective-permute-start.1) | collective-permute-done | bytes 237600 | tf_op jit(solution)/shard_map/ppermute | solution.py:107
  15.7 2.5 %collective-permute-done.2.refs_0_ = bf16[32,3712]{1,0:T(8,128)(2,1)S(1)} collective-permute-done((bf16[32,3712]{1,0:T(8,128)(2,1)S(1)}, bf16[32,3712]{1,0:T(8,128)(2,1)S(1)}, u32[]{:S(2)}, u32[]{:S(2)}) %collective-permute-start.2) | collective-permute-done | bytes 237600 | tf_op jit(solution)/shard_map/ppermute | solution.py:107
  18.2 0.4 collective-permute-start.5
  18.6 1.5 %collective-permute-start.7 = (bf16[32,3712]{1,0:T(8,128)(2,1)S(1)}, bf16[32,3712]{1,0:T(8,128)(2,1)S(1)}, u32[]{:S(2)}, u32[]{:S(2)}) collective-permute-start(bf16[32,3712]{1,0:T(8,128)(2,1)S(1)} %shard_map.66.refs_0_), channel_id=1, source_target_pairs={{0,2},{2,0},{4,6},{6,4},{8,10},{10,8},{12,14},{14,12},{1,3},{3,1},... | collective-permute-start | bytes 712712 | tf_op jit(solution)/shard_map/ppermute | solution.py:111
  20.1 4.2 %collective-permute-done.5.refs_1_.refs_0_ = bf16[32,3712]{1,0:T(8,128)(2,1)S(1)} collective-permute-done((bf16[32,3712]{1,0:T(8,128)(2,1)S(1)}, bf16[32,3712]{1,0:T(8,128)(2,1)S(1)}, u32[]{:S(2)}, u32[]{:S(2)}) %collective-permute-start.5) | collective-permute-done | bytes 237600 | tf_op jit(solution)/shard_map/ppermute | solution.py:107
  24.3 1.2 %collective-permute-start.6 = (bf16[32,3712]{1,0:T(8,128)(2,1)S(1)}, bf16[32,3712]{1,0:T(8,128)(2,1)S(1)}, u32[]{:S(2)}, u32[]{:S(2)}) collective-permute-start(bf16[32,3712]{1,0:T(8,128)(2,1)S(1)} %shard_map.67), channel_id=1, source_target_pairs={{0,4},{2,6},{4,0},{6,2},{8,12},{10,14},{12,8},{14,10},{1,5},{3,7},... | collective-permute-start | bytes 712712 | tf_op jit(solution)/shard_map/ppermute | solution.py:107
  25.5 1.5 %collective-permute-start.10 = (bf16[32,3712]{1,0:T(8,128)(2,1)S(1)}, bf16[32,3712]{1,0:T(8,128)(2,1)S(1)}, u32[]{:S(2)}, u32[]{:S(2)}) collective-permute-start(bf16[32,3712]{1,0:T(8,128)(2,1)S(1)} %collective-permute-done.5.refs_1_.refs_0_), channel_id=1, source_target_pairs={{0,2},{2,0},{4,6},{6,4},{8,10},{10,8},{12,14},{14,12},{1,3},{3,1},... | collective-permute-start | bytes 712712 | tf_op jit(solution)/shard_map/ppermute | solution.py:111
  27.0 1.4 %shard_map.68 = (bf16[32,3584]{1,0:T(8,128)(2,1)S(1)}, bf16[32,3584]{1,0:T(8,128)(2,1)S(1)}, f32[8,128]{1,0:T(8,128)S(1)}) custom-call(bf16[32,3712]{1,0:T(8,128)(2,1)S(1)} %shard_map.66.refs_0_, bf16[32,3712]{1,0:T(8,128)(2,1)S(1)} %collective-permute-done.7.refs_1_, bf16[3584,256]{1,0:T(8,128)(2,1)S(1)} %get-tuple-element.25.refs_2_.refs_4_, ...), custom_call_target="tpu_custom_call" | custom-call | tf_op jit(solution)/shard_map/pallas_call | solution.py:127
  28.4 0.6 %collective-permute-start.9 = (bf16[32,3584]{1,0:T(8,128)(2,1)S(1)}, bf16[32,3584]{1,0:T(8,128)(2,1)S(1)}, u32[]{:S(2)}, u32[]{:S(2)}) collective-permute-start(bf16[32,3584]{1,0:T(8,128)(2,1)S(1)} %get-tuple-element.32), channel_id=1, source_target_pairs={{0,2},{2,0},{4,6},{6,4},{8,10},{10,8},{12,14},{14,12},{1,3},{3,1},... | collective-permute-start | bytes 688136 | tf_op jit(solution)/shard_map/ppermute | solution.py:111
  29.0 1.5 %collective-permute-done.6.refs_3_ = bf16[32,3712]{1,0:T(8,128)(2,1)S(1)} collective-permute-done((bf16[32,3712]{1,0:T(8,128)(2,1)S(1)}, bf16[32,3712]{1,0:T(8,128)(2,1)S(1)}, u32[]{:S(2)}, u32[]{:S(2)}) %collective-permute-start.6) | collective-permute-done | bytes 237600 | tf_op jit(solution)/shard_map/ppermute | solution.py:107
  30.5 1.4 %shard_map.69 = (bf16[32,3584]{1,0:T(8,128)(2,1)S(1)}, bf16[32,3584]{1,0:T(8,128)(2,1)S(1)}, bf16[32,3584]{1,0:T(8,128)(2,1)S(1)}, bf16[32,3584]{1,0:T(8,128)(2,1)S(1)}, f32[8,128]{1,0:T(8,128)S(1)}) custom-call(bf16[32,3712]{1,0:T(8,128)(2,1)S(1)} %shard_map.64.refs_0_, bf16[32,3712]{1,0:T(8,128)(2,1)S(1)} %collective-permute-done.refs_0_.refs_1_, ...), custom_call_target="tpu_custom_call" | custom-call | tf_op jit(solution)/shard_map/pallas_call | solution.py:127
  31.9 2.2 %collective-permute-done.10.refs_1_ = bf16[32,3712]{1,0:T(8,128)(2,1)S(1)} collective-permute-done((bf16[32,3712]{1,0:T(8,128)(2,1)S(1)}, bf16[32,3712]{1,0:T(8,128)(2,1)S(1)}, u32[]{:S(2)}, u32[]{:S(2)}) %collective-permute-start.10) | collective-permute-done | bytes 237600 | tf_op jit(solution)/shard_map/ppermute | solution.py:111
  34.1 1.4 %shard_map.70 = (bf16[32,3584]{1,0:T(8,128)(2,1)S(1)}, bf16[32,3584]{1,0:T(8,128)(2,1)S(1)}, f32[8,128]{1,0:T(8,128)S(1)}) custom-call(bf16[32,3712]{1,0:T(8,128)(2,1)S(1)} %collective-permute-done.5.refs_1_.refs_0_, bf16[32,3712]{1,0:T(8,128)(2,1)S(1)} %collective-permute-done.10.refs_1_, bf16[3584,256]{1,0:T(8,128)(2,1)S(1)} %get-tuple-element.25.refs_2_.refs_4_, ...), custom_call_target="tpu_custom_call" | custom-call | tf_op jit(solution)/shard_map/pallas_call | solution.py:127
  35.5 1.7 %collective-permute-start.12 = (bf16[32,3584]{1,0:T(8,128)(2,1)S(1)}, bf16[32,3584]{1,0:T(8,128)(2,1)S(1)}, u32[]{:S(2)}, u32[]{:S(2)}) collective-permute-start(bf16[32,3584]{1,0:T(8,128)(2,1)S(1)} %get-tuple-element.37), channel_id=1, source_target_pairs={{0,2},{2,0},{4,6},{6,4},{8,10},{10,8},{12,14},{14,12},{1,3},{3,1},... | collective-permute-start | bytes 688136 | tf_op jit(solution)/shard_map/ppermute | solution.py:111
  37.2 1.4 %collective-permute-done.9.refs_1_ = bf16[32,3584]{1,0:T(8,128)(2,1)S(1)} collective-permute-done((bf16[32,3584]{1,0:T(8,128)(2,1)S(1)}, bf16[32,3584]{1,0:T(8,128)(2,1)S(1)}, u32[]{:S(2)}, u32[]{:S(2)}) %collective-permute-start.9) | collective-permute-done | bytes 229408 | tf_op jit(solution)/shard_map/ppermute | solution.py:111
  38.7 1.3 %collective-permute-start.11 = (bf16[32,3584]{1,0:T(8,128)(2,1)S(1)}, bf16[32,3584]{1,0:T(8,128)(2,1)S(1)}, u32[]{:S(2)}, u32[]{:S(2)}) collective-permute-start(bf16[32,3584]{1,0:T(8,128)(2,1)S(1)} %get-tuple-element.35), channel_id=1, source_target_pairs={{0,8},{2,10},{4,12},{6,14},{8,0},{10,2},{12,4},{14,6},{1,9},{3,11}... | collective-permute-start | bytes 688136 | tf_op jit(solution)/shard_map/ppermute | solution.py:107
  40.0 1.1 %collective-permute-start.8 = (bf16[32,3584]{1,0:T(8,128)(2,1)S(1)}, bf16[32,3584]{1,0:T(8,128)(2,1)S(1)}, u32[]{:S(2)}, u32[]{:S(2)}) collective-permute-start(bf16[32,3584]{1,0:T(8,128)(2,1)S(1)} %get-tuple-element.30), channel_id=1, source_target_pairs={{0,4},{2,6},{4,0},{6,2},{8,12},{10,14},{12,8},{14,10},{1,5},{3,7},... | collective-permute-start | bytes 688136 | tf_op jit(solution)/shard_map/ppermute | solution.py:107
  41.1 0.5 collective-permute-done.12.refs_1_
  41.7 1.6 %collective-permute-start.13 = (bf16[32,3584]{1,0:T(8,128)(2,1)S(1)}, bf16[32,3584]{1,0:T(8,128)(2,1)S(1)}, u32[]{:S(2)}, u32[]{:S(2)}) collective-permute-start(bf16[32,3584]{1,0:T(8,128)(2,1)S(1)} %get-tuple-element.39), channel_id=1, source_target_pairs={{0,12},{2,14},{4,8},{6,10},{8,4},{10,6},{12,0},{14,2},{1,13},{3,15... | collective-permute-start | bytes 688136 | tf_op jit(solution)/shard_map/ppermute | solution.py:107
  43.3 3.8 %collective-permute-done.14.refs_1_ = bf16[32,3584]{1,0:T(8,128)(2,1)S(1)} collective-permute-done((bf16[32,3584]{1,0:T(8,128)(2,1)S(1)}, bf16[32,3584]{1,0:T(8,128)(2,1)S(1)}, u32[]{:S(2)}, u32[]{:S(2)}) %collective-permute-start.14) | collective-permute-done | bytes 229408 | tf_op jit(solution)/shard_map/ppermute | solution.py:107
  47.2 4.5 %collective-permute-done.11.refs_2_ = bf16[32,3584]{1,0:T(8,128)(2,1)S(1)} collective-permute-done((bf16[32,3584]{1,0:T(8,128)(2,1)S(1)}, bf16[32,3584]{1,0:T(8,128)(2,1)S(1)}, u32[]{:S(2)}, u32[]{:S(2)}) %collective-permute-start.11) | collective-permute-done | bytes 229408 | tf_op jit(solution)/shard_map/ppermute | solution.py:107
  51.7 2.6 %collective-permute-done.13.refs_3_ = bf16[32,3584]{1,0:T(8,128)(2,1)S(1)} collective-permute-done((bf16[32,3584]{1,0:T(8,128)(2,1)S(1)}, bf16[32,3584]{1,0:T(8,128)(2,1)S(1)}, u32[]{:S(2)}, u32[]{:S(2)}) %collective-permute-start.13) | collective-permute-done | bytes 229408 | tf_op jit(solution)/shard_map/ppermute | solution.py:107
  54.4 0.1 shard_map.73
  54.7 0.7 %shard_map.75.refs_0_ = bf16[2,32,1792]{2,1,0:T(8,128)(2,1)} custom-call(bf16[32,1792]{1,0:T(8,128)(2,1)S(1)} %get-tuple-element.43.value_ref), custom_call_target="tpu_custom_call" | custom-call | tf_op jit(solution)/shard_map/pallas_call | solution.py:257
  55.3 0.6 %collective-permute-done.16.value_ref = bf16[32,1792]{1,0:T(8,128)(2,1)S(1)} collective-permute-done((bf16[32,1792]{1,0:T(8,128)(2,1)S(1)}, bf16[32,1792]{1,0:T(8,128)(2,1)S(1)}, u32[]{:S(2)}, u32[]{:S(2)}) %collective-permute-start.16) | collective-permute-done | bytes 114720 | tf_op jit(solution)/shard_map/ppermute | solution.py:102
  56.0 0.7 %shard_map.76 = bf16[2,32,1792]{2,1,0:T(8,128)(2,1)} custom-call(bf16[32,1792]{1,0:T(8,128)(2,1)S(1)} %collective-permute-done.16.value_ref, bf16[2,32,1792]{2,1,0:T(8,128)(2,1)} %shard_map.75.refs_0_), custom_call_target="tpu_custom_call", output_to_operand_aliasing={{}: (1, {})} | custom-call | tf_op jit(solution)/shard_map/pallas_call | solution.py:257
  (19 shorter events, 0.5 us)
Async XLA Ops:
  0.0 8.8 %collective-permute-start.4 = (bf16[3584,256]{1,0:T(8,128)(2,1)}, bf16[3584,256]{1,0:T(8,128)(2,1)S(1)}, u32[]{:S(2)}, u32[]{:S(2)}) collective-permute-start(bf16[3584,256]{1,0:T(8,128)(2,1)} %refs_0_.1), channel_id=1, source_target_pairs={{0,1},{1,0},{2,3},{3,2},{4,5},{5,4},{6,7},{7,6},{8,9},{9,8},{10,11... | collective-permute-start | bytes 5505032 | tf_op jit(solution)/shard_map/ppermute | solution.py:102
  0.5 8.4 %collective-permute-start.3 = (bf16[256,3584]{1,0:T(8,128)(2,1)}, bf16[256,3584]{1,0:T(8,128)(2,1)}, u32[]{:S(2)}, u32[]{:S(2)}) collective-permute-start(bf16[256,3584]{1,0:T(8,128)(2,1)} %refs_1_.1), channel_id=1, source_target_pairs={{0,1},{1,0},{2,3},{3,2},{4,5},{5,4},{6,7},{7,6},{8,9},{9,8},{10,11... | collective-permute-start | bytes 5505032 | tf_op jit(solution)/shard_map/ppermute | solution.py:102
  1.6 14.0 %collective-permute-start.1 = (bf16[32,3712]{1,0:T(8,128)(2,1)S(1)}, bf16[32,3712]{1,0:T(8,128)(2,1)S(1)}, u32[]{:S(2)}, u32[]{:S(2)}) collective-permute-start(bf16[32,3712]{1,0:T(8,128)(2,1)S(1)} %shard_map.64.refs_0_), channel_id=1, source_target_pairs={{0,4},{2,6},{4,0},{6,2},{8,12},{10,14},{12,8},{14,10},{1,5},{3,7},... | collective-permute-start | bytes 712712 | tf_op jit(solution)/shard_map/ppermute | solution.py:107
  4.7 13.4 %collective-permute-start.2 = (bf16[32,3712]{1,0:T(8,128)(2,1)S(1)}, bf16[32,3712]{1,0:T(8,128)(2,1)S(1)}, u32[]{:S(2)}, u32[]{:S(2)}) collective-permute-start(bf16[32,3712]{1,0:T(8,128)(2,1)S(1)} %shard_map.64.refs_0_), channel_id=1, source_target_pairs={{0,8},{2,10},{4,12},{6,14},{8,0},{10,2},{12,4},{14,6},{1,9},{3,11}... | collective-permute-start | bytes 712712 | tf_op jit(solution)/shard_map/ppermute | solution.py:107
  7.3 12.8 %collective-permute-start = (bf16[32,3712]{1,0:T(8,128)(2,1)S(1)}, bf16[32,3712]{1,0:T(8,128)(2,1)S(1)}, u32[]{:S(2)}, u32[]{:S(2)}) collective-permute-start(bf16[32,3712]{1,0:T(8,128)(2,1)S(1)} %shard_map.64.refs_0_), channel_id=1, source_target_pairs={{0,2},{2,0},{4,6},{6,4},{8,10},{10,8},{12,14},{14,12},{1,3},{3,1},... | collective-permute-start | bytes 712712 | tf_op jit(solution)/shard_map/ppermute | solution.py:111
  18.2 6.1 %collective-permute-start.5 = (bf16[32,3712]{1,0:T(8,128)(2,1)S(1)}, bf16[32,3712]{1,0:T(8,128)(2,1)S(1)}, u32[]{:S(2)}, u32[]{:S(2)}) collective-permute-start(bf16[32,3712]{1,0:T(8,128)(2,1)S(1)} %shard_map.66.refs_0_), channel_id=1, source_target_pairs={{0,4},{2,6},{4,0},{6,2},{8,12},{10,14},{12,8},{14,10},{1,5},{3,7},... | collective-permute-start | bytes 712712 | tf_op jit(solution)/shard_map/ppermute | solution.py:107
  18.6 8.4 %collective-permute-start.7 = (bf16[32,3712]{1,0:T(8,128)(2,1)S(1)}, bf16[32,3712]{1,0:T(8,128)(2,1)S(1)}, u32[]{:S(2)}, u32[]{:S(2)}) collective-permute-start(bf16[32,3712]{1,0:T(8,128)(2,1)S(1)} %shard_map.66.refs_0_), channel_id=1, source_target_pairs={{0,2},{2,0},{4,6},{6,4},{8,10},{10,8},{12,14},{14,12},{1,3},{3,1},... | collective-permute-start | bytes 712712 | tf_op jit(solution)/shard_map/ppermute | solution.py:111
  24.3 6.2 %collective-permute-start.6 = (bf16[32,3712]{1,0:T(8,128)(2,1)S(1)}, bf16[32,3712]{1,0:T(8,128)(2,1)S(1)}, u32[]{:S(2)}, u32[]{:S(2)}) collective-permute-start(bf16[32,3712]{1,0:T(8,128)(2,1)S(1)} %shard_map.67), channel_id=1, source_target_pairs={{0,4},{2,6},{4,0},{6,2},{8,12},{10,14},{12,8},{14,10},{1,5},{3,7},... | collective-permute-start | bytes 712712 | tf_op jit(solution)/shard_map/ppermute | solution.py:107
  25.5 8.6 %collective-permute-start.10 = (bf16[32,3712]{1,0:T(8,128)(2,1)S(1)}, bf16[32,3712]{1,0:T(8,128)(2,1)S(1)}, u32[]{:S(2)}, u32[]{:S(2)}) collective-permute-start(bf16[32,3712]{1,0:T(8,128)(2,1)S(1)} %collective-permute-done.5.refs_1_.refs_0_), channel_id=1, source_target_pairs={{0,2},{2,0},{4,6},{6,4},{8,10},{10,8},{12,14},{14,12},{1,3},{3,1},... | collective-permute-start | bytes 712712 | tf_op jit(solution)/shard_map/ppermute | solution.py:111
  28.4 10.2 %collective-permute-start.9 = (bf16[32,3584]{1,0:T(8,128)(2,1)S(1)}, bf16[32,3584]{1,0:T(8,128)(2,1)S(1)}, u32[]{:S(2)}, u32[]{:S(2)}) collective-permute-start(bf16[32,3584]{1,0:T(8,128)(2,1)S(1)} %get-tuple-element.32), channel_id=1, source_target_pairs={{0,2},{2,0},{4,6},{6,4},{8,10},{10,8},{12,14},{14,12},{1,3},{3,1},... | collective-permute-start | bytes 688136 | tf_op jit(solution)/shard_map/ppermute | solution.py:111
  35.5 19.0 %copy-start = (bf16[2,32,3584]{2,1,0:T(8,128)(2,1)S(1)}, bf16[2,32,3584]{2,1,0:T(8,128)(2,1)}, u32[]{:S(2)}) copy-start(bf16[2,32,3584]{2,1,0:T(8,128)(2,1)} %hidden_ref.1) | copy-start | bytes 1376260
  35.5 6.1 %collective-permute-start.12 = (bf16[32,3584]{1,0:T(8,128)(2,1)S(1)}, bf16[32,3584]{1,0:T(8,128)(2,1)S(1)}, u32[]{:S(2)}, u32[]{:S(2)}) collective-permute-start(bf16[32,3584]{1,0:T(8,128)(2,1)S(1)} %get-tuple-element.37), channel_id=1, source_target_pairs={{0,2},{2,0},{4,6},{6,4},{8,10},{10,8},{12,14},{14,12},{1,3},{3,1},... | collective-permute-start | bytes 688136 | tf_op jit(solution)/shard_map/ppermute | solution.py:111
  37.2 9.9 %collective-permute-start.14 = (bf16[32,3584]{1,0:T(8,128)(2,1)S(1)}, bf16[32,3584]{1,0:T(8,128)(2,1)S(1)}, u32[]{:S(2)}, u32[]{:S(2)}) collective-permute-start(bf16[32,3584]{1,0:T(8,128)(2,1)S(1)} %get-tuple-element.41), channel_id=1, source_target_pairs={{0,4},{2,6},{4,0},{6,2},{8,12},{10,14},{12,8},{14,10},{1,5},{3,7},... | collective-permute-start | bytes 688136 | tf_op jit(solution)/shard_map/ppermute | solution.py:107
  38.7 13.0 %collective-permute-start.11 = (bf16[32,3584]{1,0:T(8,128)(2,1)S(1)}, bf16[32,3584]{1,0:T(8,128)(2,1)S(1)}, u32[]{:S(2)}, u32[]{:S(2)}) collective-permute-start(bf16[32,3584]{1,0:T(8,128)(2,1)S(1)} %get-tuple-element.35), channel_id=1, source_target_pairs={{0,8},{2,10},{4,12},{6,14},{8,0},{10,2},{12,4},{14,6},{1,9},{3,11}... | collective-permute-start | bytes 688136 | tf_op jit(solution)/shard_map/ppermute | solution.py:107
  40.0 11.7 %collective-permute-start.8 = (bf16[32,3584]{1,0:T(8,128)(2,1)S(1)}, bf16[32,3584]{1,0:T(8,128)(2,1)S(1)}, u32[]{:S(2)}, u32[]{:S(2)}) collective-permute-start(bf16[32,3584]{1,0:T(8,128)(2,1)S(1)} %get-tuple-element.30), channel_id=1, source_target_pairs={{0,4},{2,6},{4,0},{6,2},{8,12},{10,14},{12,8},{14,10},{1,5},{3,7},... | collective-permute-start | bytes 688136 | tf_op jit(solution)/shard_map/ppermute | solution.py:107
  41.7 12.7 %collective-permute-start.13 = (bf16[32,3584]{1,0:T(8,128)(2,1)S(1)}, bf16[32,3584]{1,0:T(8,128)(2,1)S(1)}, u32[]{:S(2)}, u32[]{:S(2)}) collective-permute-start(bf16[32,3584]{1,0:T(8,128)(2,1)S(1)} %get-tuple-element.39), channel_id=1, source_target_pairs={{0,12},{2,14},{4,8},{6,10},{8,4},{10,6},{12,0},{14,2},{1,13},{3,15... | collective-permute-start | bytes 688136 | tf_op jit(solution)/shard_map/ppermute | solution.py:107
  47.1 7.3 %collective-permute-start.15 = (bf16[32,3584]{1,0:T(8,128)(2,1)S(1)}, bf16[32,3584]{1,0:T(8,128)(2,1)S(1)}, u32[]{:S(2)}, u32[]{:S(2)}) collective-permute-start(bf16[32,3584]{1,0:T(8,128)(2,1)S(1)} %shard_map.74), channel_id=1, source_target_pairs={{0,2},{2,0},{4,6},{6,4},{8,10},{10,8},{12,14},{14,12},{1,3},{3,1},... | collective-permute-start | bytes 688136 | tf_op jit(solution)/shard_map/ppermute | solution.py:111
  54.6 1.4 %collective-permute-start.16 = (bf16[32,1792]{1,0:T(8,128)(2,1)S(1)}, bf16[32,1792]{1,0:T(8,128)(2,1)S(1)}, u32[]{:S(2)}, u32[]{:S(2)}) collective-permute-start(bf16[32,1792]{1,0:T(8,128)(2,1)S(1)} %get-tuple-element.44), channel_id=1, source_target_pairs={{0,1},{1,0},{2,3},{3,2},{4,5},{5,4},{6,7},{7,6},{8,9},{9,8},{10,11... | collective-permute-start | bytes 344072 | tf_op jit(solution)/shard_map/ppermute | solution.py:102
